TPU v7x, 32 devices: a whole 2x2x4 slice. The times are simulated.
32 devices in a mesh: pb: 8 (over z, y), slab: 4 (over x, core).
Axes of the slice: x: 2, y: 2, z: 4, core: 2. Of those that a mesh axis runs over, the one named last changes fastest.
Arguments:
- query_feats: bfloat16 [8, 128, 9, 256], P('pb', 'slab'), may hold values from -1.5 to 1.5
- frame_store: bfloat16 [32, 128, 9, 256], P(None, 'pb'), may hold values from -1.5 to 1.5
- candidates: int32 [8, 4], replicated, may hold values from 0 to 31
- query_length: int32 [8], P('pb'), may hold values from 16 to 128, as said below
- clip_length: int32 [32], replicated, may hold values from 16 to 128, as said below
- kernel_one: float32 [3, 3, 1, 32], replicated, may hold values from -2 to 2
- bias_one: float32 [32], replicated, may hold values from -0.2 to 0.2
- kernel_two: float32 [3, 3, 32, 64], replicated, may hold values from -0.375 to 0.375
- bias_two: float32 [64], replicated, may hold values from -0.2 to 0.2
- kernel_three: float32 [3, 3, 64, 128], replicated, may hold values from -0.25 to 0.25
- bias_three: float32 [128], replicated, may hold values from -0.2 to 0.2
- kernel_four: float32 [1, 1, 128, 1], replicated, may hold values from -0.5 to 0.5
- bias_four: float32 [1], replicated, may hold values from -1.75 to 1.75
Outputs:
- scores: float32 [8, 4], P('pb')
Inputs may be any that keep to these rules, and one draw needn't show every extreme that they name: `query_length`: some query has exactly 128 valid frames and some exactly 16. `clip_length`: some candidate clip has exactly 128 valid frames and some exactly 16.
All inputs are finite; a program needn't handle non-finite values.
Results may differ from a plain program's by a relative error of at most 0.0003.
Values may be sent and summed in bfloat16 or wider, within the bound.
No kernel may reach another device: no remote copies, remote signals or barrier semaphores. Data moves between devices by JAX's collectives and lax.ppermute only.
A program may use at most 128 MiB of HBM per device.

v0:
```python
import jax
import jax.numpy as jnp
from jax import lax
from jax.sharding import PartitionSpec as P


def extended(block, sides, width):
    for axis, dim in sides:
        count = lax.axis_size(axis)
        forward = [(i, i + 1) for i in range(count - 1)]
        backward = [(target, source) for source, target in forward]
        low = lax.ppermute(
            lax.slice_in_dim(block, block.shape[dim] - width, None, axis=dim), axis, forward
        )
        high = lax.ppermute(lax.slice_in_dim(block, 0, width, axis=dim), axis, backward)
        block = jnp.concatenate([low, block, high], axis=dim)
    return block


def conv_rows(field, kernel, bias):
    result = lax.conv_general_dilated(
        field,
        kernel,
        (1, 1),
        ((0, 0), (1, 1)),
        dimension_numbers=("NHWC", "HWIO", "NHWC"),
        precision=lax.Precision.HIGHEST,
    )
    return result + bias


def point_conv(field, kernel, bias):
    result = jnp.einsum("nhwk,ko->nhwo", field, kernel[0, 0], precision=lax.Precision.HIGHEST)
    return result + bias


def pool_pairs(field):
    shape_now = field.shape
    blocks = field.reshape(shape_now[0], shape_now[1] // 2, 2, shape_now[2] // 2, 2, shape_now[3])
    return jnp.max(blocks, axis=(2, 4))


def with_rims(field):
    return extended(field, (("slab", 1),), 1)


def per_device(
    query_feats,
    frame_store,
    candidates,
    query_length,
    clip_length,
    kernel_one,
    bias_one,
    kernel_two,
    bias_two,
    kernel_three,
    bias_three,
    kernel_four,
    bias_four,
):
    slab_rows = query_feats.shape[1]
    regions = query_feats.shape[2]
    feature_width = query_feats.shape[3]
    band_frames = frame_store.shape[1]
    frames = band_frames * lax.axis_size("pb")
    pair_count = candidates.shape[1]
    query_index = lax.axis_index("pb")
    slab_index = lax.axis_index("slab")
    query_rows = query_feats[0].reshape(-1, feature_width)
    own_ids = lax.dynamic_slice_in_dim(candidates, query_index, 1, 0)[0]
    outgoing = frame_store[candidates.T].reshape(pair_count, -1, regions, feature_width)

    def single_clip(clip):
        flat = clip.reshape(-1, feature_width)
        gram = lax.dot_general(
            query_rows, flat, (((1,), (1,)), ((), ())), preferred_element_type=jnp.float32
        )
        gram = gram.reshape(slab_rows, regions, clip.shape[0], regions)
        return jnp.mean(jnp.max(gram, axis=3), axis=1)

    similarity = lax.map(
        single_clip, lax.all_to_all(outgoing, "pb", split_axis=1, concat_axis=1, tiled=True)
    )
    clip_range = jnp.arange(clip_length.shape[0], dtype=jnp.int32)
    own_length = jnp.sum(
        jnp.where(own_ids[:, None] == clip_range[None, :], clip_length[None, :], 0), axis=1
    )
    query_len_now = query_length[0]
    global_rows = slab_index * slab_rows + jnp.arange(slab_rows, dtype=jnp.int32)
    columns = jnp.arange(frames, dtype=jnp.int32)
    row_valid = global_rows < query_len_now
    col_valid = columns[None, :] < own_length[:, None]
    masked = jnp.where(row_valid[None, :, None] & col_valid[:, None, :], similarity, 0.0)[..., None]
    layer_one = pool_pairs(jax.nn.relu(conv_rows(with_rims(masked), kernel_one, bias_one)))
    layer_two = pool_pairs(jax.nn.relu(conv_rows(with_rims(layer_one), kernel_two, bias_two)))
    layer_three = jax.nn.relu(conv_rows(with_rims(layer_two), kernel_three, bias_three))
    layer_four = point_conv(layer_three, kernel_four, bias_four)
    final_maps = jnp.clip(layer_four[..., 0], -1.0, 1.0)
    pooled_rows = slab_index * (slab_rows // 4) + jnp.arange(slab_rows // 4, dtype=jnp.int32)
    pooled_cols = jnp.arange(frames // 4, dtype=jnp.int32)
    col_keep = 4 * pooled_cols[None, :] < own_length[:, None]
    row_keep = 4 * pooled_rows < query_len_now
    row_best = jnp.max(jnp.where(col_keep[:, None, :], final_maps, -2.0), axis=2)
    partial_total = jnp.sum(jnp.where(row_keep[None, :], row_best, 0.0), axis=1)
    row_total = lax.psum(partial_total, "slab")
    row_number = ((query_len_now + 3) // 4).astype(jnp.float32)
    return (row_total / row_number)[None, :]


def solution(mesh):
    placed = (
        P("pb", "slab", None, None),
        P(None, "pb", None, None),
        P(),
        P("pb"),
        P(),
        P(),
        P(),
        P(),
        P(),
        P(),
        P(),
        P(),
        P(),
    )
    return jax.shard_map(
        per_device, mesh=mesh, in_specs=placed, out_specs=P("pb", None), check_vma=False
    )
```

profile of v0, /device:TPU:0, one launch (start us, length us, event | category | flops | bytes accessed | tf_op | source)
XLA Modules:
  0.0 297.1 jit_solution(3573649589602853562)
XLA Ops:
  0.0 0.8 compare_select_fusion
  0.9 0.8 copy-done
  1.7 2.1 gather_fusion
  3.8 1.9 copy.102
  5.7 3.2 %copy.103 = bf16[4,128,9,256]{3,0,2,1:T(4,128)(2,1)} copy(bf16[4,128,9,256]{3,1,0,2:T(8,128)(2,1)S(1)} %bitcast.86) | data formatting | bytes 4718592 | tf_op jit(solution)/shard_map/reshape | solution.py:72
  8.9 7.4 %all-to-all-start = ((bf16[4,128,9,256]{3,0,2,1:T(4,128)(2,1)}), bf16[4,128,9,256]{3,0,2,1:T(4,128)(2,1)S(1)}, u32[]{:S(2)}, u32[]{:S(2)}) async-start(bf16[4,128,9,256]{3,0,2,1:T(4,128)(2,1)} %copy.103), calls=%async_computation | async-start | bytes 4718592 | tf_op jit(solution)/shard_map/all_to_all | solution.py:83
  16.5 0.2 dynamic-slice_reduce_fusion
  17.4 0.2 select_reduce_fusion.1
  17.7 52.5 %all-to-all-done = bf16[4,128,9,256]{3,0,2,1:T(4,128)(2,1)S(1)} async-done(((bf16[4,128,9,256]{3,0,2,1:T(4,128)(2,1)}), bf16[4,128,9,256]{3,0,2,1:T(4,128)(2,1)S(1)}, u32[]{:S(2)}, u32[]{:S(2)}) %all-to-all-start) | async-done | bytes 2359328 | tf_op jit(solution)/shard_map/all_to_all | solution.py:83
  70.2 2.6 copy.105
  72.8 123.6 %while.11 = (s32[]{:T(128)}, f32[4,32,128]{2,1,0:T(8,128)S(1)}, bf16[4,128,9,256]{3,2,1,0:T(8,128)(2,1)}, bf16[288,256]{1,0:T(8,128)(2,1)S(1)}) while((s32[]{:T(128)}, f32[4,32,128]{2,1,0:T(8,128)S(1)}, bf16[4,128,9,256]{3,2,1,0:T(8,128)(2,1)}, bf16[288,256]{1,0:T(8,128)(2,1)S(1)}) %tuple.30), condition=%wide.region_4.5_spmd.clone, body=%wide.region_1.4_spmd.sunk.clone | while | flops 170201088 | bytes 8749133 | solution.py:82
  72.8 1.3 constant_dynamic-slice_fusion.3
  74.1 0.3 reshape.146
  74.4 0.4 convolution_bitcast_fusion.3
  74.8 19.9 %reshape.147 = f32[32,9,128,9]{3,2,1,0:T(8,128)} reshape(f32[288,1152]{1,0:T(8,128)S(1)} %convolution_bitcast_fusion.3) | data formatting | bytes 2654208 | tf_op jit(solution)/shard_map/while/body/eval_jaxpr/reshape | solution.py:79
  94.7 8.9 %reduce_max.42 = f32[32,9,128]{2,1,0:T(8,128)S(1)} reduce(f32[32,9,128,9]{3,2,1,0:T(8,128)} %reshape.147, f32[]{:T(128)} %constant.62.clone.1..sunk.1), dimensions={3}, to_apply=%region_2.2 | reduce | flops 294912 | bytes 1474564 | tf_op jit(solution)/shard_map/while/body/eval_jaxpr/reduce_max | solution.py:80
  103.7 1.3 constant_dynamic-slice_fusion.3
  105.0 0.3 reshape.146
  105.3 0.4 convolution_bitcast_fusion.3
  105.7 19.9 %reshape.147 = f32[32,9,128,9]{3,2,1,0:T(8,128)} reshape(f32[288,1152]{1,0:T(8,128)S(1)} %convolution_bitcast_fusion.3) | data formatting | bytes 2654208 | tf_op jit(solution)/shard_map/while/body/eval_jaxpr/reshape | solution.py:79
  125.6 8.9 %reduce_max.42 = f32[32,9,128]{2,1,0:T(8,128)S(1)} reduce(f32[32,9,128,9]{3,2,1,0:T(8,128)} %reshape.147, f32[]{:T(128)} %constant.62.clone.1..sunk.1), dimensions={3}, to_apply=%region_2.2 | reduce | flops 294912 | bytes 1474564 | tf_op jit(solution)/shard_map/while/body/eval_jaxpr/reduce_max | solution.py:80
  134.6 1.3 constant_dynamic-slice_fusion.3
  135.9 0.3 reshape.146
  136.2 0.4 convolution_bitcast_fusion.3
  136.6 19.9 %reshape.147 = f32[32,9,128,9]{3,2,1,0:T(8,128)} reshape(f32[288,1152]{1,0:T(8,128)S(1)} %convolution_bitcast_fusion.3) | data formatting | bytes 2654208 | tf_op jit(solution)/shard_map/while/body/eval_jaxpr/reshape | solution.py:79
  156.5 8.9 %reduce_max.42 = f32[32,9,128]{2,1,0:T(8,128)S(1)} reduce(f32[32,9,128,9]{3,2,1,0:T(8,128)} %reshape.147, f32[]{:T(128)} %constant.62.clone.1..sunk.1), dimensions={3}, to_apply=%region_2.2 | reduce | flops 294912 | bytes 1474564 | tf_op jit(solution)/shard_map/while/body/eval_jaxpr/reduce_max | solution.py:80
  165.6 1.3 constant_dynamic-slice_fusion.3
  166.9 0.3 reshape.146
  167.1 0.4 convolution_bitcast_fusion.3
  167.5 19.9 %reshape.147 = f32[32,9,128,9]{3,2,1,0:T(8,128)} reshape(f32[288,1152]{1,0:T(8,128)S(1)} %convolution_bitcast_fusion.3) | data formatting | bytes 2654208 | tf_op jit(solution)/shard_map/while/body/eval_jaxpr/reshape | solution.py:79
  187.4 8.9 %reduce_max.42 = f32[32,9,128]{2,1,0:T(8,128)S(1)} reduce(f32[32,9,128,9]{3,2,1,0:T(8,128)} %reshape.147, f32[]{:T(128)} %constant.62.clone.1..sunk.1), dimensions={3}, to_apply=%region_2.2 | reduce | flops 294912 | bytes 1474564 | tf_op jit(solution)/shard_map/while/body/eval_jaxpr/reduce_max | solution.py:80
  196.6 1.3 collective-permute-start.1
  197.9 3.3 %collective-permute-start = (f32[4,1,128,1]{2,1,0,3:T(1,128)S(1)}, f32[4,1,128,1]{2,1,0,3:T(1,128)S(1)}, u32[]{:S(2)}, u32[]{:S(2)}) collective-permute-start(f32[4,1,128,1]{2,1,0,3:T(1,128)S(1)} %get-tuple-element.64), channel_id=1, source_target_pairs={{0,1},{1,2},{2,3},{4,5},{5,6},{6,7},{8,9},{9,10},{10,11},{12,13},{... | collective-permute-start | bytes 6152 | tf_op jit(solution)/shard_map/ppermute | solution.py:12
  201.2 0.5 collective-permute-done
  201.7 0.2 copy.122
  202.1 0.2 copy.108
  202.4 18.4 %add_maximum_fusion = f32[32,32,17,32]{3,1,2,0:T(8,128)S(1)} fusion(f32[32]{0:T(128)S(1)} %copy-done.9, pred[32,17]{0,1:T(8,128)(4,1)S(1)} %copy-done.12, f32[34,32,19,1]{1,3,2,0:T(1,128)S(1)} %copy.108, f32[3,3,1,32]{3,2,1,0:T(1,128)S(1)} %copy-done.7), kind=kOutput, calls=%fused_computation.4 | convolution fusion | flops 61833216 | bytes 2312736 | tf_op jit(solution)/shard_map/conv_general_dilated | solution.py:21
  220.8 5.2 %copy.109 = f32[32,32,17,32]{3,0,2,1:T(8,128)S(1)} copy(f32[32,32,17,32]{3,1,2,0:T(8,128)S(1)} %add_maximum_fusion) | data formatting | bytes 4456448 | tf_op jit(solution)/shard_map/jit(relu)/max | solution.py:95
  226.0 4.2 %slice.35 = f32[32,4,128,32]{3,0,2,1:T(8,128)} slice(f32[32,4,136,32]{3,0,2,1:T(8,128)S(1)} %bitcast.82), slice={[0:32], [0:4], [0:128], [0:32]} | slice | bytes 4194304 | tf_op jit(solution)/shard_map/jit(relu)/max | solution.py:95
  230.2 9.7 %reduce_max.36 = f32[4,16,64,32]{3,1,2,0:T(8,128)S(1)} reduce(f32[4,16,2,64,2,32]{5,2,1,4,3,0:T(2,128)} %bitcast.83, f32[]{:T(128)} %constant.62.clone.1), dimensions={2,4}, to_apply=%region_5.6 | reduce | flops 393216 | bytes 2621444 | tf_op jit(solution)/shard_map/reduce_max | solution.py:40
  239.9 0.2 fusion.14
  240.0 1.3 collective-permute-start.3
  241.3 3.6 %collective-permute-start.2 = (f32[4,1,64,32]{3,1,2,0:T(1,128)S(1)}, f32[4,1,64,32]{3,1,2,0:T(1,128)S(1)}, u32[]{:S(2)}, u32[]{:S(2)}) collective-permute-start(f32[4,1,64,32]{3,1,2,0:T(1,128)S(1)} %get-tuple-element.60), channel_id=1, source_target_pairs={{0,1},{1,2},{2,3},{4,5},{5,6},{6,7},{8,9},{9,10},{10,11},{12,13},{... | collective-permute-start | bytes 98312 | tf_op jit(solution)/shard_map/ppermute | solution.py:12
  245.0 1.8 copy.111
  246.9 1.4 maximum_bitcast_fusion
  248.3 1.2 copy.123
  249.5 0.6 pad.2.clone
  250.2 0.8 select_maximum_fusion
  251.1 10.8 %add_maximum_fusion.1 = f32[16,32,9,64]{3,1,2,0:T(8,128)S(1)} fusion(f32[3,3,32,64]{3,2,1,0:T(8,128)S(1)} %copy-done.6, f32[18,4,8,11,32]{4,1,3,2,0:T(4,128)S(1)} %select_maximum_fusion, f32[64]{0:T(128)S(1)} %copy-done.10, pred[32,9]{0,1:T(8,128)(4,1)S(1)} %copy-done.13), kind=kOutput, calls=%fused_computation.10 | convolution fusion | flops 1020100608 | bytes 2064928 | tf_op jit(solution)/shard_map/conv_general_dilated | solution.py:21
  261.8 1.6 copy.115
  263.4 1.5 slice.39
  265.0 3.4 %reduce_max.37 = f32[4,8,32,64]{3,1,2,0:T(8,128)S(1)} reduce(f32[4,8,2,32,2,64]{5,2,1,4,3,0:T(2,128)} %bitcast.88, f32[]{:T(128)} %constant.62.clone.1), dimensions={2,4}, to_apply=%region_6.7 | reduce | flops 196608 | bytes 1310724 | tf_op jit(solution)/shard_map/reduce_max | solution.py:40
  268.5 1.3 collective-permute-start.5
  269.8 4.8 %collective-permute-start.4 = (f32[4,1,32,64]{3,1,2,0:T(1,128)S(1)}, f32[4,1,32,64]{3,1,2,0:T(1,128)S(1)}, u32[]{:S(2)}, u32[]{:S(2)}) collective-permute-start(f32[4,1,32,64]{3,1,2,0:T(1,128)S(1)} %get-tuple-element.62), channel_id=1, source_target_pairs={{0,1},{1,2},{2,3},{4,5},{5,6},{6,7},{8,9},{9,10},{10,11},{12,13},{... | collective-permute-start | bytes 98312 | tf_op jit(solution)/shard_map/ppermute | solution.py:12
  275.3 0.2 collective-permute-done.4
  275.5 0.2 maximum_bitcast_fusion.1
  275.7 0.4 copy.124
  276.4 0.3 select_maximum_fusion.1
  276.7 0.4 copy-done.5
  277.1 2.9 fusion.6
  280.0 0.4 copy.118
  280.4 7.0 %fusion.9 = f32[1,4,8,32]{2,0,3,1:T(1,128)S(1)} fusion(f32[8,4,40,128]{3,0,2,1:T(8,128)S(1)} %bitcast.91, f32[1,1,128,1]{2,3,1,0:T(1,128)S(1)} %copy-done.4), kind=kOutput, calls=%fused_computation.21 | convolution fusion | flops 1572864 | bytes 528896 | tf_op jit(solution)/shard_map/nhwk,ko->nhwo/dot_general | solution.py:33
  287.7 8.7 %psum.7 = f32[4]{0:T(128)S(1)} all-reduce(f32[4]{0:T(128)S(1)} %select_reduce_fusion), channel_id=1, replica_groups=mesh['pb'=8,'slab'=4] {'slab'}, use_global_device_ids=true, to_apply=%region_9.10 | all-reduce | flops 4 | bytes 32 | tf_op jit(solution)/shard_map/psum | solution.py:106
  296.3 0.5 divide_bitcast_fusion
  (66 shorter events, 1.8 us)
Async XLA Ops:
  0.0 1.7 copy-start
  8.9 7.4 %copy-start.2 = (bf16[1,32,9,256]{3,1,2,0:T(8,128)(2,1)S(1)}, bf16[1,32,9,256]{3,1,2,0:T(8,128)(2,1)}, u32[]{:S(2)}) copy-start(bf16[1,32,9,256]{3,1,2,0:T(8,128)(2,1)} %param.15) | copy-start | bytes 442372
  8.9 7.6 %copy-start.3 = (s32[8,4]{0,1:T(4,128)S(1)}, s32[8,4]{0,1:T(4,128)}, u32[]{:S(2)}) copy-start(s32[8,4]{0,1:T(4,128)} %param.17) | copy-start | bytes 388
  8.9 8.5 %copy-start.8 = (s32[32]{0:T(128)S(1)}, s32[32]{0:T(128)}, u32[]{:S(2)}) copy-start(s32[32]{0:T(128)} %param.19) | copy-start | bytes 388
  8.9 61.3 %all-to-all-start = ((bf16[4,128,9,256]{3,0,2,1:T(4,128)(2,1)}), bf16[4,128,9,256]{3,0,2,1:T(4,128)(2,1)S(1)}, u32[]{:S(2)}, u32[]{:S(2)}) async-start(bf16[4,128,9,256]{3,0,2,1:T(4,128)(2,1)} %copy.103), calls=%async_computation | async-start | bytes 4718592 | tf_op jit(solution)/shard_map/all_to_all | solution.py:83
  196.5 5.9 %copy-start.7 = (f32[3,3,1,32]{3,2,1,0:T(1,128)S(1)}, f32[3,3,1,32]{3,2,1,0:T(1,128)}, u32[]{:S(2)}) copy-start(f32[3,3,1,32]{3,2,1,0:T(1,128)} %param.20) | copy-start | bytes 3460
  196.5 5.9 %copy-start.9 = (f32[32]{0:T(128)S(1)}, f32[32]{0:T(128)}, u32[]{:S(2)}) copy-start(f32[32]{0:T(128)} %param.21) | copy-start | bytes 388
  196.5 5.9 %copy-start.12 = (pred[32,17]{0,1:T(8,128)(4,1)S(1)}, pred[32,17]{0,1:T(8,128)(4,1)}, u32[]{:S(2)}) copy-start(pred[32,17]{0,1:T(8,128)(4,1)} %constant.85) | copy-start | bytes 1636
  196.6 4.6 %collective-permute-start.1 = (f32[4,1,128,1]{2,1,0,3:T(1,128)S(1)}, f32[4,1,128,1]{2,1,0,3:T(1,128)S(1)}, u32[]{:S(2)}, u32[]{:S(2)}) collective-permute-start(f32[4,1,128,1]{2,1,0,3:T(1,128)S(1)} %get-tuple-element.65), channel_id=1, source_target_pairs={{1,0},{2,1},{3,2},{5,4},{6,5},{7,6},{9,8},{10,9},{11,10},{13,12},{... | collective-permute-start | bytes 6152 | tf_op jit(solution)/shard_map/ppermute | solution.py:15
  197.9 3.8 %collective-permute-start = (f32[4,1,128,1]{2,1,0,3:T(1,128)S(1)}, f32[4,1,128,1]{2,1,0,3:T(1,128)S(1)}, u32[]{:S(2)}, u32[]{:S(2)}) collective-permute-start(f32[4,1,128,1]{2,1,0,3:T(1,128)S(1)} %get-tuple-element.64), channel_id=1, source_target_pairs={{0,1},{1,2},{2,3},{4,5},{5,6},{6,7},{8,9},{9,10},{10,11},{12,13},{... | collective-permute-start | bytes 6152 | tf_op jit(solution)/shard_map/ppermute | solution.py:12
  240.0 6.7 %collective-permute-start.3 = (f32[4,1,64,32]{3,1,2,0:T(1,128)S(1)}, f32[4,1,64,32]{3,1,2,0:T(1,128)S(1)}, u32[]{:S(2)}, u32[]{:S(2)}) collective-permute-start(f32[4,1,64,32]{3,1,2,0:T(1,128)S(1)} %get-tuple-element.61), channel_id=1, source_target_pairs={{1,0},{2,1},{3,2},{5,4},{6,5},{7,6},{9,8},{10,9},{11,10},{13,12},{... | collective-permute-start | bytes 98312 | tf_op jit(solution)/shard_map/ppermute | solution.py:15
  241.3 5.5 %collective-permute-start.2 = (f32[4,1,64,32]{3,1,2,0:T(1,128)S(1)}, f32[4,1,64,32]{3,1,2,0:T(1,128)S(1)}, u32[]{:S(2)}, u32[]{:S(2)}) collective-permute-start(f32[4,1,64,32]{3,1,2,0:T(1,128)S(1)} %get-tuple-element.60), channel_id=1, source_target_pairs={{0,1},{1,2},{2,3},{4,5},{5,6},{6,7},{8,9},{9,10},{10,11},{12,13},{... | collective-permute-start | bytes 98312 | tf_op jit(solution)/shard_map/ppermute | solution.py:12
  250.1 0.9 copy-start.6
  250.2 0.9 copy-start.10
  250.2 0.9 copy-start.13
  268.5 6.8 %collective-permute-start.5 = (f32[4,1,32,64]{3,1,2,0:T(1,128)S(1)}, f32[4,1,32,64]{3,1,2,0:T(1,128)S(1)}, u32[]{:S(2)}, u32[]{:S(2)}) collective-permute-start(f32[4,1,32,64]{3,1,2,0:T(1,128)S(1)} %get-tuple-element.63), channel_id=1, source_target_pairs={{1,0},{2,1},{3,2},{5,4},{6,5},{7,6},{9,8},{10,9},{11,10},{13,12},{... | collective-permute-start | bytes 98312 | tf_op jit(solution)/shard_map/ppermute | solution.py:15
  269.8 5.7 %collective-permute-start.4 = (f32[4,1,32,64]{3,1,2,0:T(1,128)S(1)}, f32[4,1,32,64]{3,1,2,0:T(1,128)S(1)}, u32[]{:S(2)}, u32[]{:S(2)}) collective-permute-start(f32[4,1,32,64]{3,1,2,0:T(1,128)S(1)} %get-tuple-element.62), channel_id=1, source_target_pairs={{0,1},{1,2},{2,3},{4,5},{5,6},{6,7},{8,9},{9,10},{10,11},{12,13},{... | collective-permute-start | bytes 98312 | tf_op jit(solution)/shard_map/ppermute | solution.py:12
  276.1 1.0 copy-start.5
  276.2 1.0 copy-start.11
  276.2 0.9 copy-start.14
  276.4 20.5 %copy-start.1 = (bf16[32,16,9,256]{3,1,2,0:T(8,128)(2,1)S(1)}, bf16[32,16,9,256]{3,1,2,0:T(8,128)(2,1)}, u32[]{:S(2)}) copy-start(bf16[32,16,9,256]{3,1,2,0:T(8,128)(2,1)} %param.16) | copy-start | bytes 7077892
  277.1 3.3 %copy-start.4 = (f32[1,1,128,1]{2,3,1,0:T(1,128)S(1)}, f32[1,1,128,1]{2,3,1,0:T(1,128)}, u32[]{:S(2)}) copy-start(f32[1,1,128,1]{2,3,1,0:T(1,128)} %param.26) | copy-start | bytes 1540
where the time goes:
time: 303 us; the launch traced here: 297 us
  local copies, waits for them, and re-layouts  116 us (38%)
  other arithmetic  53.8 us (18%)
  waiting for transfers between devices  53.2 us (18%)
  matrix products  40.6 us (13%)
  starting transfers between devices  23 us (8%)
  blocking collectives  8.66 us (3%)
    reshape x4, local copies, waits for them, and re-layouts, single_clip(): gram = gram.reshape(slab_rows, regions, clip.shape[0], regions)  79.7 us
    all_to_all x1, waiting for transfers between devices, per_device(): lax.all_to_all(outgoing, 'pb', split_axis=1, concat_axis=1, tiled=True)  52.5 us
    reduce_max x4, other arithmetic, single_clip(): return jnp.mean(jnp.max(gram, axis=3), axis=1)  35.7 us
    conv_general_dilated x3, matrix products, conv_rows(): lax.conv_general_dilated(field, kernel, (1, 1), ((0, 0), (1, 1)), dimensi...  32.1 us
    reduce_max x2, other arithmetic, pool_pairs(): return jnp.max(blocks, axis=(2, 4))  13.1 us
    ppermute x3, starting transfers between devices, extended(): lax.ppermute(lax.slice_in_dim(block, block.shape[dim] - width, None, axis...  11.7 us
    max x2, local copies, waits for them, and re-layouts, per_device(): jax.nn.relu(conv_rows(with_rims(masked), kernel_one, bias_one))  9.36 us
    psum x1, blocking collectives, per_device(): row_total = lax.psum(partial_total, 'slab')  8.66 us
  transfers between devices with their start and end apart: 7, of which 3 were waited for; matrix products, arithmetic and copies ran while one was open for 1% of the time, Pallas kernels for 0%

commit v1 on v0

v1 whole, which is shorter than its diff:
```python
import functools

import jax
import jax.numpy as jnp
from jax import lax
from jax.experimental import pallas as pl
from jax.experimental.pallas import tpu as pltpu
from jax.sharding import PartitionSpec as P

F32 = jnp.float32
BF16 = jnp.bfloat16
LANES = 128


def exchange_rounds(count, core):
    half = count // 2
    far = list(range(count - 1, half - 1, -1))
    near = list(range(half - 1, 0, -1))
    return far + near if core == 0 else near + far


def split(x):
    high = x.astype(BF16)
    return high, (x - high.astype(F32)).astype(BF16)


def pick_kernel(rounds, cand_ref, store_ref, *rest):
    outs, sem = rest[:-1], rest[-1]
    query = lax.axis_index("pb")
    pair = lax.axis_index("slab")
    odd = lax.rem(pair, 2)
    copies = []
    for at, out in enumerate(outs):
        if at < len(rounds[0]):
            target = query ^ jnp.where(odd == 0, rounds[0][at], rounds[1][at])
        else:
            target = query
        copy = pltpu.make_async_copy(store_ref.at[cand_ref[target, pair]], out, sem.at[at])
        copy.start()
        copies.append(copy)
    for copy in copies:
        copy.wait()


def weight_kernel(one_ref, two_ref, three_ref, w1_ref, w2a_ref, w2b_ref, w3a_ref, w3b_ref):
    def place(ref, base, value):
        rows = value.shape[0]
        span = ref.shape[0] // 3
        high, low = split(value)
        ref[pl.ds(base, rows), :] = high
        ref[pl.ds(span + base, rows), :] = high
        ref[pl.ds(2 * span + base, rows), :] = low

    def iotas(rows):
        return (
            lax.broadcasted_iota(jnp.int32, (rows, 256), 0),
            lax.broadcasted_iota(jnp.int32, (rows, 256), 1),
        )

    row, lane = iotas(LANES)
    group = lane // 32
    column = 2 * (group % 4) + group // 4
    total = jnp.zeros((LANES, 256), F32)
    for d in range(3):
        for t in range(3):
            mask = (row // 16 == d) & (row % 16 - column == t)
            total = jnp.where(mask, one_ref[3 * d + t : 3 * d + t + 1, :], total)
    place(w1_ref, 0, total)

    group = lane // 64
    column = 2 * (group % 2) + group // 2
    for ref, first in ((w2a_ref, 0), (w2b_ref, 4)):
        for d in range(3):
            total = jnp.zeros((LANES, 256), F32)
            for t in range(3):
                tile = two_ref[3 * d + t]
                total = jnp.where(row // 32 + first - column == t, jnp.concatenate([tile] * 4, axis=0), total)
            place(ref, LANES * d, total)

    column = lane // 128
    for ref, first in ((w3a_ref, 0), (w3b_ref, 2)):
        for d in range(3):
            total = jnp.zeros((LANES, 256), F32)
            for t in range(3):
                tile = three_ref[3 * d + t]
                total = jnp.where(row // 64 + first - column == t, jnp.concatenate([tile] * 2, axis=0), total)
            place(ref, LANES * d, total)


def moved_rows(x, step):
    rows = x.shape[0]
    row = lax.broadcasted_iota(jnp.int32, x.shape, 0)
    if step == 1:
        return jnp.where(row == 0, 0.0, pltpu.roll(x, 1, 0))
    return jnp.where(row == rows - 1, 0.0, pltpu.roll(x, rows - 1, 0))


def dot(a, b):
    return jnp.dot(a, b, preferred_element_type=F32)


def score_kernel(
    rounds,
    n_blocks,
    n_slabs,
    regions,
    frames,
    cand_ref,
    qlen_ref,
    clen_ref,
    *rest,
):
    blocks = rest[:n_blocks]
    slabs = rest[n_blocks : n_blocks + n_slabs]
    (
        w1_ref,
        w2a_ref,
        w2b_ref,
        w3a_ref,
        w3b_ref,
        b1_ref,
        b2_ref,
        b3_ref,
        k4_ref,
        b4_ref,
        out_ref,
        clip,
        feats,
        best,
        sim,
        x1,
        x2,
        x3,
    ) = rest[n_blocks + n_slabs :]
    query = lax.axis_index("pb")
    pair = lax.axis_index("slab")
    odd = lax.rem(pair, 2)
    feature_width = feats.shape[-1]
    query_len = qlen_ref[0]
    clip_len = clen_ref[cand_ref[query, pair]]

    if n_blocks == 1:
        clip[...] = blocks[0][...]
    else:
        for at, block in enumerate(blocks):
            band = block.shape[1]
            source = query
            if at < n_blocks - 1:
                source = query ^ jnp.where(odd == 0, rounds[0][at], rounds[1][at])
            clip[:, pl.ds(pl.multiple_of(source * band, band), band), :] = block[...]
    for k, slab in enumerate(slabs):
        rows = slab.shape[1]
        feats[:, pl.ds(pl.multiple_of((pair ^ k) * rows, rows), rows), :] = slab[...]

    flat = feats[...].reshape(regions * frames, feature_width)
    for s in range(0, regions, 2):
        width = min(2, regions - s)
        part = clip[s : s + width].reshape(width * frames, feature_width)
        gram = lax.dot_general(flat, part, (((1,), (1,)), ((), ())), preferred_element_type=F32)
        if width == 2:
            gram = jnp.maximum(gram[:, :frames], gram[:, frames:])
        best[...] = gram if s == 0 else jnp.maximum(best[...], gram)
    total = best[0:frames, :]
    for r in range(1, regions):
        total = total + best[r * frames : (r + 1) * frames, :]
    row = lax.broadcasted_iota(jnp.int32, (frames, frames), 0)
    col = lax.broadcasted_iota(jnp.int32, (frames, frames), 1)
    sim[...] = jnp.where((row < query_len) & (col < clip_len), total * (1.0 / regions), 0.0)

    quarter = frames // 4
    phases = [sim[pl.ds(p, quarter, stride=4), :] for p in range(4)]
    ordered = jnp.concatenate([moved_rows(phases[3], 1), *phases, moved_rows(phases[0], -1)], axis=0)
    windows = frames // 8
    rolled = [pltpu.roll(ordered, 8 * m + 1, 1) for m in range(16)]
    lane = lax.broadcasted_iota(jnp.int32, (frames, LANES), 1)
    for n in range(windows):
        taps = [rolled[(2 * d - n) % 16][d * quarter : d * quarter + frames] for d in range(3)]
        field = jnp.where(lane < 16, taps[0], jnp.where(lane < 32, taps[1], taps[2]))
        if n == 0:
            field = jnp.where(lane % 16 == 0, 0.0, field)
        if n == windows - 1:
            field = jnp.where(lane % 16 == 9, 0.0, field)
        high, low = split(field)
        x1[n * frames : (n + 1) * frames, 0:LANES] = high
        x1[n * frames : (n + 1) * frames, LANES : 2 * LANES] = low
    made = dot(x1[...], w1_ref[0:256, :]) + dot(x1[:, 0:LANES], w1_ref[256:384, :])
    made = jnp.maximum(made[:, :LANES], made[:, LANES:])
    first = []
    for n in range(windows):
        here = made[n * frames : (n + 1) * frames]
        halves = []
        for e in range(2):
            pooled = jnp.maximum(
                here[2 * e * quarter : (2 * e + 1) * quarter], here[(2 * e + 1) * quarter : (2 * e + 2) * quarter]
            )
            halves.append(jnp.maximum(pooled + b1_ref[...], 0.0))
        first.append(halves)

    lane = lax.broadcasted_iota(jnp.int32, (quarter, LANES), 1)

    def shifted(parts, width):
        turned = [pltpu.roll(x, width, 1) for x in parts]
        result = []
        for n in range(len(parts) + 1):
            before = turned[n - 1] if n > 0 else jnp.zeros_like(turned[0])
            after = turned[n] if n < len(parts) else jnp.zeros_like(turned[0])
            result.append(jnp.where(lane < width, before, after))
        return result

    even = shifted([x[0] for x in first], 32)
    odds = shifted([x[1] for x in first], 32)
    half = 2 * quarter
    for n in range(windows + 1):
        base = n * half
        e = split(even[n])
        o = split(odds[n])
        down = split(moved_rows(odds[n], 1))
        up = split(moved_rows(even[n], -1))
        for d, (top, bottom) in enumerate(((down, e), (e, o), (o, up))):
            for part in range(2):
                at = part * 3 * LANES + d * LANES
                x2[base : base + quarter, at : at + LANES] = top[part]
                x2[base + quarter : base + half, at : at + LANES] = bottom[part]
    rows = windows * half
    made = (
        dot(x2[0:rows, :], w2a_ref[0:768, :])
        + dot(x2[0:rows, 0:384], w2a_ref[768:1152, :])
        + dot(x2[half : half + rows, :], w2b_ref[0:768, :])
        + dot(x2[half : half + rows, 0:384], w2b_ref[768:1152, :])
    )
    made = jnp.maximum(made[:, :LANES], made[:, LANES:])
    second = []
    for n in range(windows):
        here = jnp.maximum(made[n * half : n * half + quarter], made[n * half + quarter : (n + 1) * half])
        second.append(jnp.maximum(here + b2_ref[...], 0.0))

    moved = shifted(second, 64)
    for n in range(windows + 1):
        base = n * quarter
        for d, value in enumerate((moved_rows(moved[n], 1), moved[n], moved_rows(moved[n], -1))):
            high, low = split(value)
            x3[base : base + quarter, d * LANES : (d + 1) * LANES] = high
            x3[base : base + quarter, (3 + d) * LANES : (4 + d) * LANES] = low
    rows = windows * quarter
    made = (
        dot(x3[0:rows, :], w3a_ref[0:768, :])
        + dot(x3[0:rows, 0:384], w3a_ref[768:1152, :])
        + dot(x3[quarter : quarter + rows, :], w3b_ref[0:768, :])
        + dot(x3[quarter : quarter + rows, 0:384], w3b_ref[768:1152, :])
    )
    made = jnp.maximum(made + b3_ref[...], 0.0) * k4_ref[...]
    bias_four = b4_ref[0]
    row_best = jnp.full((quarter, 1), -2.0, F32)
    for c in range(2):
        summed = jnp.sum(made[:, c * LANES : (c + 1) * LANES], axis=1, keepdims=True)
        final = jnp.clip(summed + bias_four, -1.0, 1.0)
        for n in range(windows):
            here = final[n * quarter : (n + 1) * quarter]
            keep = 4 * (2 * n + c) < clip_len
            row_best = jnp.maximum(row_best, jnp.where(keep, here, -2.0))
    row = lax.broadcasted_iota(jnp.int32, (quarter, 1), 0)
    kept = jnp.where(4 * row < query_len, row_best, 0.0)
    number = jnp.broadcast_to(((query_len + 3) // 4).astype(F32), (1, 1))
    score = jnp.sum(kept, axis=0, keepdims=True) / number
    lane = lax.broadcasted_iota(jnp.int32, out_ref.shape, 1)
    out_ref[...] = jnp.where(lane == pair, score, 0.0)


def per_device(
    query_feats,
    frame_store,
    candidates,
    query_length,
    clip_length,
    kernel_one,
    bias_one,
    kernel_two,
    bias_two,
    kernel_three,
    bias_three,
    kernel_four,
    bias_four,
):
    slab_rows, regions, feature_width = query_feats.shape[1:]
    band = frame_store.shape[1]
    n_query = lax.axis_size("pb")
    n_slab = lax.axis_size("slab")
    frames = band * n_query
    pair_count = candidates.shape[1]
    assert pair_count == n_slab and slab_rows * n_slab == frames == LANES
    vmem = pl.BlockSpec(memory_space=pltpu.VMEM)
    smem = pl.BlockSpec(memory_space=pltpu.SMEM)
    anywhere = pl.BlockSpec(memory_space=pl.ANY)
    store = jnp.transpose(frame_store, (0, 2, 1, 3))
    own = jnp.transpose(query_feats[0], (1, 0, 2))

    rounds = None
    if n_query <= 8:
        rounds = [exchange_rounds(n_query, core) for core in range(2)]
        sent = pl.pallas_call(
            functools.partial(pick_kernel, rounds),
            out_shape=[jax.ShapeDtypeStruct(store.shape[1:], BF16)] * n_query,
            in_specs=[smem, anywhere],
            out_specs=[anywhere] * n_query,
            scratch_shapes=[pltpu.SemaphoreType.DMA((n_query,))],
            name="pick_bands",
        )(candidates, store)
        blocks = []
        for at in range(n_query - 1):
            moves = [
                (q * n_slab + s, (q ^ rounds[s % 2][at]) * n_slab + s) for q in range(n_query) for s in range(n_slab)
            ]
            blocks.append(lax.ppermute(sent[at], ("pb", "slab"), moves))
        blocks.append(sent[n_query - 1])
    else:
        ids = lax.dynamic_index_in_dim(candidates, lax.axis_index("slab"), 1, keepdims=False)
        got = lax.all_to_all(store[ids], "pb", 0, 0, tiled=True)
        blocks = [jnp.transpose(got, (1, 0, 2, 3)).reshape(regions, frames, feature_width)]
    slabs = [own]
    for k in range(1, n_slab):
        slabs.append(lax.ppermute(own, "slab", [(s, s ^ k) for s in range(n_slab)]))

    one = jnp.tile(kernel_one.reshape(9, -1), (1, 8))
    two = jnp.tile(kernel_two.reshape(9, 32, 64), (1, 1, 4))
    three = jnp.tile(kernel_three.reshape(9, 64, 128), (1, 1, 2))
    weights = pl.pallas_call(
        weight_kernel,
        out_shape=[jax.ShapeDtypeStruct((384, 256), BF16)] + [jax.ShapeDtypeStruct((1152, 256), BF16)] * 4,
        in_specs=[vmem] * 3,
        out_specs=[vmem] * 5,
        cost_estimate=pl.CostEstimate(flops=2_000_000, bytes_accessed=6_000_000, transcendentals=0),
        name="lay_out_kernels",
    )(one, two, three)

    vector = pl.pallas_call(
        functools.partial(score_kernel, rounds, len(blocks), n_slab, regions, frames),
        out_shape=jax.ShapeDtypeStruct((1, LANES), F32),
        in_specs=[smem] * 3 + [vmem] * (len(blocks) + n_slab + 9) + [smem],
        out_specs=vmem,
        scratch_shapes=[
            pltpu.VMEM((regions, frames, feature_width), BF16),
            pltpu.VMEM((regions, frames, feature_width), BF16),
            pltpu.VMEM((regions * frames, frames), F32),
            pltpu.VMEM((frames, frames), F32),
            pltpu.VMEM((16 * frames, 256), BF16),
            pltpu.VMEM((17 * 64, 768), BF16),
            pltpu.VMEM((17 * 32, 768), BF16),
        ],
        compiler_params=pltpu.CompilerParams(vmem_limit_bytes=40 * 1024 * 1024),
        cost_estimate=pl.CostEstimate(flops=2_000_000_000, bytes_accessed=8_000_000, transcendentals=0),
        name="score_pair",
    )(
        candidates,
        query_length,
        clip_length,
        *blocks,
        *slabs,
        *weights,
        jnp.tile(bias_one, 4)[None],
        jnp.tile(bias_two, 2)[None],
        jnp.tile(bias_three, 2)[None],
        jnp.tile(kernel_four.reshape(-1), 2)[None],
        bias_four,
    )
    for k in (1, 2):
        vector = vector + lax.ppermute(vector, "slab", [(s, s ^ k) for s in range(n_slab)])
    return vector[:, :pair_count]


def solution(mesh):
    placed = (
        P("pb", "slab", None, None),
        P(None, "pb", None, None),
        P(),
        P("pb"),
        P(),
        P(),
        P(),
        P(),
        P(),
        P(),
        P(),
        P(),
        P(),
    )
    return jax.shard_map(
        per_device, mesh=mesh, in_specs=placed, out_specs=P("pb", None), check_vma=False
    )
```

time: 303 us -> 68 us (0.22); the launches traced: 297 us -> 67.6 us
  local copies, waits for them, and re-layouts: 116 us -> 10.2 us
  other arithmetic: 53.8 us -> 0.55 us
  waiting for transfers between devices: 53.2 us -> 7.92 us
  matrix products: 40.6 us -> 0 us
  Pallas kernels: 0 us -> 29.9 us
  blocking collectives: 8.66 us -> 0 us
  starting transfers between devices: 23 us -> 17.5 us
    reshape x9 -> x0, local copies, waits for them, and re-layouts: 84 us -> none  [the longest x4 79.7 us: single_clip(): gram = gram.reshape(slab_rows, regions, clip.shape[0], regions)]
    all_to_all x1 -> x0, waiting for transfers between devices: 52.5 us -> none  [per_device(): lax.all_to_all(outgoing, 'pb', split_axis=1, concat_axis=1, tiled=True)]
    reduce_max x7 -> x0, other arithmetic: 48.9 us -> none  [the longest x4 35.7 us: single_clip(): return jnp.mean(jnp.max(gram, axis=3), axis=1)]
    conv_general_dilated x3 -> x0, matrix products: 32.1 us -> none  [conv_rows(): lax.conv_general_dilated(field, kernel, (1, 1), ((0, 0), (1, 1)), dimensi...]
    pallas_call x0 -> x3, Pallas kernels: none -> 29.9 us  [the longest x1 19.8 us: per_device(): pl.pallas_call(functools.partial(pick_kernel, rounds), out_shape=[jax.Sha...]
    max x5 -> x0, local copies, waits for them, and re-layouts: 12.9 us -> none  [the longest x2 9.36 us: per_device(): jax.nn.relu(conv_rows(with_rims(masked), kernel_one, bias_one))]
    psum x1 -> x0, blocking collectives: 8.66 us -> none  [per_device(): row_total = lax.psum(partial_total, 'slab')]
    dot_general x5 -> x0, matrix products: 8.52 us -> none  [the longest x1 6.97 us: point_conv(): jnp.einsum('nhwk,ko->nhwo', field, kernel[0, 0], precision=lax.Precision....]
  transfers between devices with their start and end apart: 7 -> 12, of which waited for: 3 -> 5; matrix products, arithmetic and copies ran while one was open for 1% -> 5% of each run, Pallas kernels for 0% -> 4%
where the time goes in v1:
time: 68 us; the launch traced here: 67.6 us
  Pallas kernels  29.9 us (44%)
  starting transfers between devices  17.5 us (26%)
  local copies, waits for them, and re-layouts  10.2 us (15%)
  waiting for transfers between devices  7.92 us (12%)
  between operations  1.49 us (2%)
    pallas_call x1, Pallas kernels, per_device(): pl.pallas_call(functools.partial(pick_kernel, rounds), out_shape=[jax.Sha...  19.8 us
    ppermute x7, starting transfers between devices, per_device(): blocks.append(lax.ppermute(sent[at], ('pb', 'slab'), moves))  12.1 us
    pallas_call x1, Pallas kernels, per_device(): pl.pallas_call(functools.partial(score_kernel, rounds, len(blocks), n_sla...  7.38 us
    unnamed x33, local copies, waits for them, and re-layouts  6.63 us
    ppermute x7, waiting for transfers between devices, per_device(): blocks.append(lax.ppermute(sent[at], ('pb', 'slab'), moves))  4.09 us
    ppermute x2, starting transfers between devices, per_device(): lax.ppermute(vector, 'slab', [(s, s ^ k) for s in range(n_slab)])  3.92 us
    ppermute x2, waiting for transfers between devices, per_device(): lax.ppermute(vector, 'slab', [(s, s ^ k) for s in range(n_slab)])  3.83 us
    pallas_call x1, Pallas kernels, per_device(): pl.pallas_call(weight_kernel, out_shape=[jax.ShapeDtypeStruct((384, 256),...  2.78 us
  transfers between devices with their start and end apart: 12, of which 5 were waited for; matrix products, arithmetic and copies ran while one was open for 5% of the time, Pallas kernels for 4%

profile of v1, /device:TPU:0, one launch (start us, length us, event | category | flops | bytes accessed | tf_op | source)
XLA Modules:
  0.0 67.6 jit_solution(10486971813909449398)
XLA Ops:
  0.0 0.0 copy-start.6
  0.0 0.0 copy-start.9
  0.0 0.0 copy-start.10
  0.0 1.4 %copy.15.cand_ref = s32[8,4]{1,0:T(8,128)} copy(s32[8,4]{0,1:T(4,128)} %param.15) | data formatting | bytes 256 | tf_op args[2]
  1.4 19.8 %pick_bands.1 = (bf16[9,16,256]{2,1,0:T(8,128)(2,1)}, bf16[9,16,256]{2,1,0:T(8,128)(2,1)}, bf16[9,16,256]{2,1,0:T(8,128)(2,1)}, bf16[9,16,256]{2,1,0:T(8,128)(2,...) custom-call(s32[8,4]{1,0:T(8,128)} %copy.15.cand_ref, ...), custom_call_target="tpu_custom_call" | custom-call | tf_op jit(solution)/shard_map/pick_bands/pallas_call | solution.py:300
  21.2 0.0 copy-start.11
  21.2 0.0 copy-start.12
  21.2 0.0 copy-start.13
  21.2 6.1 %collective-permute-start = (bf16[9,16,256]{2,1,0:T(8,128)(2,1)}, bf16[9,16,256]{2,1,0:T(8,128)(2,1)S(1)}, u32[]{:S(2)}, u32[]{:S(2)}) collective-permute-start(bf16[9,16,256]{2,1,0:T(8,128)(2,1)} %get-tuple-element.18), channel_id=1, source_target_pairs={{0,28},{1,13},{2,30},{3,15},{4,24},{5,9},{6,26},{7,11},{8,20},{9,5... | collective-permute-start | bytes 221192 | tf_op jit(solution)/shard_map/ppermute | solution.py:313
  27.3 0.2 collective-permute-start.1
  27.5 0.7 %collective-permute-start.2 = (bf16[9,16,256]{2,1,0:T(8,128)(2,1)}, bf16[9,16,256]{2,1,0:T(8,128)(2,1)S(1)}, u32[]{:S(2)}, u32[]{:S(2)}) collective-permute-start(bf16[9,16,256]{2,1,0:T(8,128)(2,1)} %get-tuple-element.20), channel_id=1, source_target_pairs={{0,20},{1,5},{2,22},{3,7},{4,16},{5,1},{6,18},{7,3},{8,28},{9,13},... | collective-permute-start | bytes 221192 | tf_op jit(solution)/shard_map/ppermute | solution.py:313
  28.3 2.0 %collective-permute-start.3 = (bf16[9,16,256]{2,1,0:T(8,128)(2,1)}, bf16[9,16,256]{2,1,0:T(8,128)(2,1)S(1)}, u32[]{:S(2)}, u32[]{:S(2)}) collective-permute-start(bf16[9,16,256]{2,1,0:T(8,128)(2,1)} %get-tuple-element.21), channel_id=1, source_target_pairs={{0,16},{1,29},{2,18},{3,31},{4,20},{5,25},{6,22},{7,27},{8,24},{9,... | collective-permute-start | bytes 221192 | tf_op jit(solution)/shard_map/ppermute | solution.py:313
  30.3 2.3 %collective-permute-start.4 = (bf16[9,16,256]{2,1,0:T(8,128)(2,1)}, bf16[9,16,256]{2,1,0:T(8,128)(2,1)S(1)}, u32[]{:S(2)}, u32[]{:S(2)}) collective-permute-start(bf16[9,16,256]{2,1,0:T(8,128)(2,1)} %get-tuple-element.22), channel_id=1, source_target_pairs={{0,12},{1,25},{2,14},{3,27},{4,8},{5,29},{6,10},{7,31},{8,4},{9,17... | collective-permute-start | bytes 221192 | tf_op jit(solution)/shard_map/ppermute | solution.py:313
  32.6 0.0 collective-permute-done.rest_0_
  32.6 0.0 copy-done.6
  32.6 0.0 collective-permute-start.7
  32.6 1.2 %collective-permute-done.1.rest_1_ = bf16[9,16,256]{2,1,0:T(8,128)(2,1)S(1)} collective-permute-done((bf16[9,16,256]{2,1,0:T(8,128)(2,1)}, bf16[9,16,256]{2,1,0:T(8,128)(2,1)S(1)}, u32[]{:S(2)}, u32[]{:S(2)}) %collective-permute-start.1) | collective-permute-done | bytes 73760 | tf_op jit(solution)/shard_map/ppermute | solution.py:313
  33.8 1.5 %collective-permute-start.8 = (bf16[9,32,256]{2,1,0:T(8,128)(2,1)S(1)}, bf16[9,32,256]{2,1,0:T(8,128)(2,1)S(1)}, u32[]{:S(2)}, u32[]{:S(2)}) collective-permute-start(bf16[9,32,256]{2,1,0:T(8,128)(2,1)S(1)} %bitcast.11), channel_id=1, source_target_pairs={{0,2},{1,3},{2,0},{3,1},{4,6},{5,7},{6,4},{7,5},{8,10},{9,11},{10,... | collective-permute-start | bytes 442376 | tf_op jit(solution)/shard_map/ppermute | solution.py:321
  35.3 1.2 %collective-permute-done.2.rest_2_ = bf16[9,16,256]{2,1,0:T(8,128)(2,1)S(1)} collective-permute-done((bf16[9,16,256]{2,1,0:T(8,128)(2,1)}, bf16[9,16,256]{2,1,0:T(8,128)(2,1)S(1)}, u32[]{:S(2)}, u32[]{:S(2)}) %collective-permute-start.2) | collective-permute-done | bytes 73760 | tf_op jit(solution)/shard_map/ppermute | solution.py:313
  36.4 0.0 collective-permute-start.9
  36.4 1.8 %collective-permute-done.3.rest_3_ = bf16[9,16,256]{2,1,0:T(8,128)(2,1)S(1)} collective-permute-done((bf16[9,16,256]{2,1,0:T(8,128)(2,1)}, bf16[9,16,256]{2,1,0:T(8,128)(2,1)S(1)}, u32[]{:S(2)}, u32[]{:S(2)}) %collective-permute-start.3) | collective-permute-done | bytes 73760 | tf_op jit(solution)/shard_map/ppermute | solution.py:313
  38.2 0.0 collective-permute-start.5
  38.2 0.0 collective-permute-done.4.rest_4_
  38.2 0.8 %collective-permute-start.6 = (bf16[9,16,256]{2,1,0:T(8,128)(2,1)}, bf16[9,16,256]{2,1,0:T(8,128)(2,1)S(1)}, u32[]{:S(2)}, u32[]{:S(2)}) collective-permute-start(bf16[9,16,256]{2,1,0:T(8,128)(2,1)} %get-tuple-element.24), channel_id=1, source_target_pairs={{0,4},{1,17},{2,6},{3,19},{4,0},{5,21},{6,2},{7,23},{8,12},{9,25},... | collective-permute-start | bytes 221192 | tf_op jit(solution)/shard_map/ppermute | solution.py:313
  38.9 0.0 copy-done.9
  39.0 0.0 copy-start.14
  39.0 0.0 copy-start.15
  39.0 0.0 copy-start
  39.0 0.0 copy-start.7
  39.0 0.0 copy-start.8
  39.0 0.2 tile.62
  39.2 1.3 %tile.63.three_ref = f32[9,64,256]{2,1,0:T(8,128)} reshape(f32[9,64,2,128]{3,2,1,0:T(2,128)S(1)} %tile.62) | data formatting | bytes 1179648 | tf_op jit(solution)/shard_map/tile | solution.py:325
  40.5 0.0 copy-done.10
  40.5 0.1 tile.59
  40.6 1.1 %tile.60.two_ref = f32[9,32,256]{2,1,0:T(8,128)} reshape(f32[9,32,4,64]{3,2,1,0:T(4,128)S(1)} %tile.59) | data formatting | bytes 589824 | tf_op jit(solution)/shard_map/tile | solution.py:324
  41.7 0.0 copy-done.11
  41.7 0.7 %tile.57.one_ref = f32[9,256]{1,0:T(8,128)} reshape(f32[9,8,32]{2,1,0:T(8,128)S(1)} %tile.56) | data formatting | bytes 18432 | tf_op jit(solution)/shard_map/tile | solution.py:323
  42.4 0.0 copy-done.12
  42.4 0.1 broadcast_in_dim_tile.12.rest_17_
  42.5 0.0 copy-done.13
  42.5 0.1 broadcast_in_dim_tile.13.rest_18_
  43.9 2.8 %lay_out_kernels.1 = (bf16[384,256]{1,0:T(8,128)(2,1)}, bf16[1152,256]{1,0:T(8,128)(2,1)}, bf16[1152,256]{1,0:T(8,128)(2,1)}, bf16[1152,256]{1,0:T(8,128)(2,1)}, bf16[1152,256]{1,0:T(8,128)(2,1)}) custom-call(f32[9,256]{1,0:T(8,128)} %tile.57.one_ref, f32[9,32,256]{2,1,0:T(8,128)} %tile.60.two_ref, f32[9,64,256]{2,1,0:T(8,128)} %tile.63.three_ref), custom_call_target="tpu_custom_call" | custom-call | flops 2000000 | bytes 6000000 | tf_op jit(solution)/shard_map/lay_out_kernels/pallas_call | solution.py:326
  46.7 0.0 collective-permute-done.5.rest_5_
  46.7 0.0 collective-permute-done.6.rest_6_
  46.7 0.0 collective-permute-done.7.rest_9_
  46.7 0.0 collective-permute-done.8.rest_10_
  46.7 0.0 collective-permute-done.9.rest_11_
  46.7 0.0 copy-done.14
  46.7 0.0 copy-done.15
  46.8 0.0 copy-done
  46.8 0.0 copy-done.7
  46.8 0.0 copy-done.8
  46.8 0.0 copy-start.1
  46.8 1.1 %copy-done.1 = bf16[1152,256]{1,0:T(8,128)(2,1)S(1)} copy-done((bf16[1152,256]{1,0:T(8,128)(2,1)S(1)}, bf16[1152,256]{1,0:T(8,128)(2,1)}, u32[]{:S(2)}) %copy-start.1) | copy-done | bytes 589848
  47.9 1.1 %copy-done.2 = bf16[1152,256]{1,0:T(8,128)(2,1)S(1)} copy-done((bf16[1152,256]{1,0:T(8,128)(2,1)S(1)}, bf16[1152,256]{1,0:T(8,128)(2,1)}, u32[]{:S(2)}) %copy-start.2) | copy-done | bytes 589848
  48.9 1.1 %copy-done.3 = bf16[1152,256]{1,0:T(8,128)(2,1)S(1)} copy-done((bf16[1152,256]{1,0:T(8,128)(2,1)S(1)}, bf16[1152,256]{1,0:T(8,128)(2,1)}, u32[]{:S(2)}) %copy-start.3) | copy-done | bytes 589848
  50.0 1.1 %copy-done.4 = bf16[1152,256]{1,0:T(8,128)(2,1)S(1)} copy-done((bf16[1152,256]{1,0:T(8,128)(2,1)S(1)}, bf16[1152,256]{1,0:T(8,128)(2,1)}, u32[]{:S(2)}) %copy-start.4) | copy-done | bytes 589848
  51.1 0.9 %copy-done.5 = bf16[384,256]{1,0:T(8,128)(2,1)S(1)} copy-done((bf16[384,256]{1,0:T(8,128)(2,1)S(1)}, bf16[384,256]{1,0:T(8,128)(2,1)}, u32[]{:S(2)}) %copy-start.5) | copy-done | bytes 196632
  52.0 7.4 %score_pair.1 = f32[1,128]{1,0:T(1,128)S(1)} custom-call(s32[8,4]{1,0:T(8,128)S(1)} %copy-done, s32[1]{0:T(128)S(6)} %copy.17.qlen_ref, s32[32]{0:T(128)S(1)} %copy-done.8, bf16[9,16,256]{2,1,0:T(8,128)(2,1)S(1)} %collective-permute-done.rest_0_, bf16[9,16,256]{2,1,0:T(8,128)(2,1)S(1)} %collective-permute-done.1.rest_1_, ...), custom_call_target="tpu_custom_call" | custom-call | flops 2000000000 | bytes 8000000 | tf_op jit(solution)/shard_map/score_pair/pallas_call | solution.py:335
  59.4 3.4 %collective-permute-start.10 = (f32[1,128]{1,0:T(1,128)S(1)}, f32[1,128]{1,0:T(1,128)S(1)}, u32[]{:S(2)}, u32[]{:S(2)}) collective-permute-start(f32[1,128]{1,0:T(1,128)S(1)} %score_pair.1), channel_id=1, source_target_pairs={{0,1},{1,0},{2,3},{3,2},{4,5},{5,4},{6,7},{7,6},{8,9},{9,8},{10,11... | collective-permute-start | bytes 1544 | tf_op jit(solution)/shard_map/ppermute | solution.py:366
  62.8 0.8 %collective-permute-done.10 = f32[1,128]{1,0:T(1,128)S(1)} collective-permute-done((f32[1,128]{1,0:T(1,128)S(1)}, f32[1,128]{1,0:T(1,128)S(1)}, u32[]{:S(2)}, u32[]{:S(2)}) %collective-permute-start.10) | collective-permute-done | bytes 544 | tf_op jit(solution)/shard_map/ppermute | solution.py:366
  63.6 0.5 collective-permute-start.11
  64.1 3.0 %collective-permute-done.11 = f32[1,128]{1,0:T(1,128)S(1)} collective-permute-done((f32[1,128]{1,0:T(1,128)S(1)}, f32[1,128]{1,0:T(1,128)S(1)}, u32[]{:S(2)}, u32[]{:S(2)}) %collective-permute-start.11) | collective-permute-done | bytes 544 | tf_op jit(solution)/shard_map/ppermute | solution.py:366
  67.1 0.5 add.7
  (12 shorter events, 0.1 us)
Async XLA Ops:
  0.0 32.6 %copy-start.6 = (bf16[1,32,9,256]{3,1,2,0:T(8,128)(2,1)S(1)}, bf16[1,32,9,256]{3,1,2,0:T(8,128)(2,1)}, u32[]{:S(2)}) copy-start(bf16[1,32,9,256]{3,1,2,0:T(8,128)(2,1)} %param.13) | copy-start | bytes 442372
  0.0 38.9 %copy-start.9 = (f32[3,3,64,128]{3,2,1,0:T(8,128)S(1)}, f32[3,3,64,128]{3,2,1,0:T(8,128)}, u32[]{:S(2)}) copy-start(f32[3,3,64,128]{3,2,1,0:T(8,128)} %param.22) | copy-start | bytes 884740
  0.0 40.5 %copy-start.10 = (f32[3,3,32,64]{3,2,1,0:T(8,128)S(1)}, f32[3,3,32,64]{3,2,1,0:T(8,128)}, u32[]{:S(2)}) copy-start(f32[3,3,32,64]{3,2,1,0:T(8,128)} %param.20) | copy-start | bytes 221188
  21.2 20.5 %copy-start.11 = (f32[3,3,1,32]{3,2,1,0:T(1,128)S(1)}, f32[3,3,1,32]{3,2,1,0:T(1,128)}, u32[]{:S(2)}) copy-start(f32[3,3,1,32]{3,2,1,0:T(1,128)} %param.18) | copy-start | bytes 3460
  21.2 21.2 %copy-start.12 = (f32[32]{0:T(128)S(1)}, f32[32]{0:T(128)}, u32[]{:S(2)}) copy-start(f32[32]{0:T(128)} %param.19) | copy-start | bytes 388
  21.2 21.3 %copy-start.13 = (f32[64]{0:T(128)S(1)}, f32[64]{0:T(128)}, u32[]{:S(2)}) copy-start(f32[64]{0:T(128)} %param.21) | copy-start | bytes 772
  21.2 11.4 %collective-permute-start = (bf16[9,16,256]{2,1,0:T(8,128)(2,1)}, bf16[9,16,256]{2,1,0:T(8,128)(2,1)S(1)}, u32[]{:S(2)}, u32[]{:S(2)}) collective-permute-start(bf16[9,16,256]{2,1,0:T(8,128)(2,1)} %get-tuple-element.18), channel_id=1, source_target_pairs={{0,28},{1,13},{2,30},{3,15},{4,24},{5,9},{6,26},{7,11},{8,20},{9,5... | collective-permute-start | bytes 221192 | tf_op jit(solution)/shard_map/ppermute | solution.py:313
  27.3 6.5 %collective-permute-start.1 = (bf16[9,16,256]{2,1,0:T(8,128)(2,1)}, bf16[9,16,256]{2,1,0:T(8,128)(2,1)S(1)}, u32[]{:S(2)}, u32[]{:S(2)}) collective-permute-start(bf16[9,16,256]{2,1,0:T(8,128)(2,1)} %get-tuple-element.19), channel_id=1, source_target_pairs={{0,24},{1,9},{2,26},{3,11},{4,28},{5,13},{6,30},{7,15},{8,16},{9,1... | collective-permute-start | bytes 221192 | tf_op jit(solution)/shard_map/ppermute | solution.py:313
  27.5 8.9 %collective-permute-start.2 = (bf16[9,16,256]{2,1,0:T(8,128)(2,1)}, bf16[9,16,256]{2,1,0:T(8,128)(2,1)S(1)}, u32[]{:S(2)}, u32[]{:S(2)}) collective-permute-start(bf16[9,16,256]{2,1,0:T(8,128)(2,1)} %get-tuple-element.20), channel_id=1, source_target_pairs={{0,20},{1,5},{2,22},{3,7},{4,16},{5,1},{6,18},{7,3},{8,28},{9,13},... | collective-permute-start | bytes 221192 | tf_op jit(solution)/shard_map/ppermute | solution.py:313
  28.3 9.9 %collective-permute-start.3 = (bf16[9,16,256]{2,1,0:T(8,128)(2,1)}, bf16[9,16,256]{2,1,0:T(8,128)(2,1)S(1)}, u32[]{:S(2)}, u32[]{:S(2)}) collective-permute-start(bf16[9,16,256]{2,1,0:T(8,128)(2,1)} %get-tuple-element.21), channel_id=1, source_target_pairs={{0,16},{1,29},{2,18},{3,31},{4,20},{5,25},{6,22},{7,27},{8,24},{9,... | collective-permute-start | bytes 221192 | tf_op jit(solution)/shard_map/ppermute | solution.py:313
  30.3 7.9 %collective-permute-start.4 = (bf16[9,16,256]{2,1,0:T(8,128)(2,1)}, bf16[9,16,256]{2,1,0:T(8,128)(2,1)S(1)}, u32[]{:S(2)}, u32[]{:S(2)}) collective-permute-start(bf16[9,16,256]{2,1,0:T(8,128)(2,1)} %get-tuple-element.22), channel_id=1, source_target_pairs={{0,12},{1,25},{2,14},{3,27},{4,8},{5,29},{6,10},{7,31},{8,4},{9,17... | collective-permute-start | bytes 221192 | tf_op jit(solution)/shard_map/ppermute | solution.py:313
  32.6 14.1 %collective-permute-start.7 = (bf16[9,32,256]{2,1,0:T(8,128)(2,1)S(1)}, bf16[9,32,256]{2,1,0:T(8,128)(2,1)S(1)}, u32[]{:S(2)}, u32[]{:S(2)}) collective-permute-start(bf16[9,32,256]{2,1,0:T(8,128)(2,1)S(1)} %bitcast.10), channel_id=1, source_target_pairs={{0,1},{1,0},{2,3},{3,2},{4,5},{5,4},{6,7},{7,6},{8,9},{9,8},{10,11... | collective-permute-start | bytes 442376 | tf_op jit(solution)/shard_map/ppermute | solution.py:321
  33.8 12.9 %collective-permute-start.8 = (bf16[9,32,256]{2,1,0:T(8,128)(2,1)S(1)}, bf16[9,32,256]{2,1,0:T(8,128)(2,1)S(1)}, u32[]{:S(2)}, u32[]{:S(2)}) collective-permute-start(bf16[9,32,256]{2,1,0:T(8,128)(2,1)S(1)} %bitcast.11), channel_id=1, source_target_pairs={{0,2},{1,3},{2,0},{3,1},{4,6},{5,7},{6,4},{7,5},{8,10},{9,11},{10,... | collective-permute-start | bytes 442376 | tf_op jit(solution)/shard_map/ppermute | solution.py:321
  36.4 10.3 %collective-permute-start.9 = (bf16[9,32,256]{2,1,0:T(8,128)(2,1)S(1)}, bf16[9,32,256]{2,1,0:T(8,128)(2,1)S(1)}, u32[]{:S(2)}, u32[]{:S(2)}) collective-permute-start(bf16[9,32,256]{2,1,0:T(8,128)(2,1)S(1)} %bitcast.12), channel_id=1, source_target_pairs={{0,3},{1,2},{2,1},{3,0},{4,7},{5,6},{6,5},{7,4},{8,11},{9,10},{10,... | collective-permute-start | bytes 442376 | tf_op jit(solution)/shard_map/ppermute | solution.py:321
  38.2 8.5 %collective-permute-start.5 = (bf16[9,16,256]{2,1,0:T(8,128)(2,1)}, bf16[9,16,256]{2,1,0:T(8,128)(2,1)S(1)}, u32[]{:S(2)}, u32[]{:S(2)}) collective-permute-start(bf16[9,16,256]{2,1,0:T(8,128)(2,1)} %get-tuple-element.23), channel_id=1, source_target_pairs={{0,8},{1,21},{2,10},{3,23},{4,12},{5,17},{6,14},{7,19},{8,0},{9,29... | collective-permute-start | bytes 221192 | tf_op jit(solution)/shard_map/ppermute | solution.py:313
  38.2 8.5 %collective-permute-start.6 = (bf16[9,16,256]{2,1,0:T(8,128)(2,1)}, bf16[9,16,256]{2,1,0:T(8,128)(2,1)S(1)}, u32[]{:S(2)}, u32[]{:S(2)}) collective-permute-start(bf16[9,16,256]{2,1,0:T(8,128)(2,1)} %get-tuple-element.24), channel_id=1, source_target_pairs={{0,4},{1,17},{2,6},{3,19},{4,0},{5,21},{6,2},{7,23},{8,12},{9,25},... | collective-permute-start | bytes 221192 | tf_op jit(solution)/shard_map/ppermute | solution.py:313
  39.0 7.8 %copy-start.14 = (f32[128]{0:T(128)S(1)}, f32[128]{0:T(128)}, u32[]{:S(2)}) copy-start(f32[128]{0:T(128)} %param.23) | copy-start | bytes 1540
  39.0 7.8 %copy-start.15 = (f32[1,1,128,1]{2,3,1,0:T(1,128)S(1)}, f32[1,1,128,1]{2,3,1,0:T(1,128)}, u32[]{:S(2)}) copy-start(f32[1,1,128,1]{2,3,1,0:T(1,128)} %param.24) | copy-start | bytes 1540
  39.0 7.8 %copy-start = (s32[8,4]{1,0:T(8,128)S(1)}, s32[8,4]{1,0:T(8,128)}, u32[]{:S(2)}) copy-start(s32[8,4]{1,0:T(8,128)} %copy.15.cand_ref) | copy-start | bytes 388
  39.0 7.8 %copy-start.7 = (bf16[9,16,256]{2,1,0:T(8,128)(2,1)S(1)}, bf16[9,16,256]{2,1,0:T(8,128)(2,1)}, u32[]{:S(2)}) copy-start(bf16[9,16,256]{2,1,0:T(8,128)(2,1)} %get-tuple-element.25.rest_7_) | copy-start | bytes 221188
  39.0 7.8 %copy-start.8 = (s32[32]{0:T(128)S(1)}, s32[32]{0:T(128)}, u32[]{:S(2)}) copy-start(s32[32]{0:T(128)} %clen_ref.1) | copy-start | bytes 388
  46.8 1.1 %copy-start.1 = (bf16[1152,256]{1,0:T(8,128)(2,1)S(1)}, bf16[1152,256]{1,0:T(8,128)(2,1)}, u32[]{:S(2)}) copy-start(bf16[1152,256]{1,0:T(8,128)(2,1)} %get-tuple-element.27.rest_13_) | copy-start | bytes 1769476
  47.9 1.1 %copy-start.2 = (bf16[1152,256]{1,0:T(8,128)(2,1)S(1)}, bf16[1152,256]{1,0:T(8,128)(2,1)}, u32[]{:S(2)}) copy-start(bf16[1152,256]{1,0:T(8,128)(2,1)} %get-tuple-element.28.rest_14_) | copy-start | bytes 1769476
  48.9 1.1 %copy-start.3 = (bf16[1152,256]{1,0:T(8,128)(2,1)S(1)}, bf16[1152,256]{1,0:T(8,128)(2,1)}, u32[]{:S(2)}) copy-start(bf16[1152,256]{1,0:T(8,128)(2,1)} %get-tuple-element.29.rest_15_) | copy-start | bytes 1769476
  50.0 1.1 %copy-start.4 = (bf16[1152,256]{1,0:T(8,128)(2,1)S(1)}, bf16[1152,256]{1,0:T(8,128)(2,1)}, u32[]{:S(2)}) copy-start(bf16[1152,256]{1,0:T(8,128)(2,1)} %get-tuple-element.30.rest_16_) | copy-start | bytes 1769476
  51.1 0.9 %copy-start.5 = (bf16[384,256]{1,0:T(8,128)(2,1)S(1)}, bf16[384,256]{1,0:T(8,128)(2,1)}, u32[]{:S(2)}) copy-start(bf16[384,256]{1,0:T(8,128)(2,1)} %get-tuple-element.26.rest_12_) | copy-start | bytes 589828
  59.4 4.2 %collective-permute-start.10 = (f32[1,128]{1,0:T(1,128)S(1)}, f32[1,128]{1,0:T(1,128)S(1)}, u32[]{:S(2)}, u32[]{:S(2)}) collective-permute-start(f32[1,128]{1,0:T(1,128)S(1)} %score_pair.1), channel_id=1, source_target_pairs={{0,1},{1,0},{2,3},{3,2},{4,5},{5,4},{6,7},{7,6},{8,9},{9,8},{10,11... | collective-permute-start | bytes 1544 | tf_op jit(solution)/shard_map/ppermute | solution.py:366
  63.6 3.5 %collective-permute-start.11 = (f32[1,128]{1,0:T(1,128)S(1)}, f32[1,128]{1,0:T(1,128)S(1)}, u32[]{:S(2)}, u32[]{:S(2)}) collective-permute-start(f32[1,128]{1,0:T(1,128)S(1)} %add.6), channel_id=1, source_target_pairs={{0,2},{1,3},{2,0},{3,1},{4,6},{5,7},{6,4},{7,5},{8,10},{9,11},{10,... | collective-permute-start | bytes 1544 | tf_op jit(solution)/shard_map/ppermute | solution.py:366

commit v2 on v1

--- a/solution.py
+++ b/solution.py
@@ -12,11 +12,9 @@
 LANES = 128
 
 
-def exchange_rounds(count, core):
-    half = count // 2
-    far = list(range(count - 1, half - 1, -1))
-    near = list(range(half - 1, 0, -1))
-    return far + near if core == 0 else near + far
+def exchange_rounds(count):
+    odd, even = list(range(count - 1, 1, -2)), list(range(count - 2, 1, -2))
+    return odd, even[-1:] + even[:-1]
 
 
 def split(x):
@@ -29,15 +27,19 @@
     query = lax.axis_index("pb")
     pair = lax.axis_index("slab")
     odd = lax.rem(pair, 2)
+    steps = len(rounds[0])
     copies = []
     for at, out in enumerate(outs):
-        if at < len(rounds[0]):
+        if at < steps:
             target = query ^ jnp.where(odd == 0, rounds[0][at], rounds[1][at])
+            for part in range(2):
+                clip = cand_ref[pair ^ part, target]
+                copies.append(pltpu.make_async_copy(store_ref.at[clip], out.at[part], sem.at[2 * at + part]))
         else:
-            target = query
-        copy = pltpu.make_async_copy(store_ref.at[cand_ref[target, pair]], out, sem.at[at])
+            clip = cand_ref[pair, query ^ (steps + 1 - at)]
+            copies.append(pltpu.make_async_copy(store_ref.at[clip], out, sem.at[steps + at]))
+    for copy in copies:
         copy.start()
-        copies.append(copy)
     for copy in copies:
         copy.wait()
 
@@ -57,6 +59,12 @@
             lax.broadcasted_iota(jnp.int32, (rows, 256), 1),
         )
 
+    def wide(x, times):
+        while times > 1:
+            x = jnp.concatenate([x, x], axis=1)
+            times //= 2
+        return x
+
     row, lane = iotas(LANES)
     group = lane // 32
     column = 2 * (group % 4) + group // 4
@@ -64,7 +72,7 @@
     for d in range(3):
         for t in range(3):
             mask = (row // 16 == d) & (row % 16 - column == t)
-            total = jnp.where(mask, one_ref[3 * d + t : 3 * d + t + 1, :], total)
+            total = jnp.where(mask, wide(one_ref[3 * d + t], 8), total)
     place(w1_ref, 0, total)
 
     group = lane // 64
@@ -73,8 +81,8 @@
         for d in range(3):
             total = jnp.zeros((LANES, 256), F32)
             for t in range(3):
-                tile = two_ref[3 * d + t]
-                total = jnp.where(row // 32 + first - column == t, jnp.concatenate([tile] * 4, axis=0), total)
+                tile = jnp.concatenate([wide(two_ref[3 * d + t], 4)] * 4, axis=0)
+                total = jnp.where(row // 32 + first - column == t, tile, total)
             place(ref, LANES * d, total)
 
     column = lane // 128
@@ -82,8 +90,8 @@
         for d in range(3):
             total = jnp.zeros((LANES, 256), F32)
             for t in range(3):
-                tile = three_ref[3 * d + t]
-                total = jnp.where(row // 64 + first - column == t, jnp.concatenate([tile] * 2, axis=0), total)
+                tile = jnp.concatenate([wide(three_ref[3 * d + t], 2)] * 2, axis=0)
+                total = jnp.where(row // 64 + first - column == t, tile, total)
             place(ref, LANES * d, total)
 
 
@@ -102,7 +110,7 @@
 def score_kernel(
     rounds,
     n_blocks,
-    n_slabs,
+    order,
     regions,
     frames,
     cand_ref,
@@ -111,6 +119,7 @@
     *rest,
 ):
     blocks = rest[:n_blocks]
+    n_slabs = len(order)
     slabs = rest[n_blocks : n_blocks + n_slabs]
     (
         w1_ref,
@@ -137,18 +146,21 @@
     odd = lax.rem(pair, 2)
     feature_width = feats.shape[-1]
     query_len = qlen_ref[0]
-    clip_len = clen_ref[cand_ref[query, pair]]
+    clip_len = clen_ref[cand_ref[pair, query]]
 
     if n_blocks == 1:
         clip[...] = blocks[0][...]
     else:
-        for at, block in enumerate(blocks):
-            band = block.shape[1]
-            source = query
-            if at < n_blocks - 1:
-                source = query ^ jnp.where(odd == 0, rounds[0][at], rounds[1][at])
-            clip[:, pl.ds(pl.multiple_of(source * band, band), band), :] = block[...]
-    for k, slab in enumerate(slabs):
+        steps = len(rounds[0])
+        band = blocks[-1].shape[1]
+        pieces = [(0, blocks[-1][...]), (1, blocks[-2][...])]
+        for at in range(steps):
+            first, second = rounds[0][at], rounds[1][at]
+            pieces.append((jnp.where(odd == 0, first, second), blocks[at][0]))
+            pieces.append((jnp.where(odd == 0, second, first), blocks[steps + at][1]))
+        for k, value in pieces:
+            clip[:, pl.ds(pl.multiple_of((query ^ k) * band, band), band), :] = value
+    for k, slab in zip(order, slabs):
         rows = slab.shape[1]
         feats[:, pl.ds(pl.multiple_of((pair ^ k) * rows, rows), rows), :] = slab[...]
 
@@ -185,6 +197,8 @@
         x1[n * frames : (n + 1) * frames, LANES : 2 * LANES] = low
     made = dot(x1[...], w1_ref[0:256, :]) + dot(x1[:, 0:LANES], w1_ref[256:384, :])
     made = jnp.maximum(made[:, :LANES], made[:, LANES:])
+    bias_one = jnp.concatenate([b1_ref[...]] * 4, axis=1)
+    bias_two = jnp.concatenate([b2_ref[...]] * 2, axis=1)
     first = []
     for n in range(windows):
         here = made[n * frames : (n + 1) * frames]
@@ -193,7 +207,7 @@
             pooled = jnp.maximum(
                 here[2 * e * quarter : (2 * e + 1) * quarter], here[(2 * e + 1) * quarter : (2 * e + 2) * quarter]
             )
-            halves.append(jnp.maximum(pooled + b1_ref[...], 0.0))
+            halves.append(jnp.maximum(pooled + bias_one, 0.0))
         first.append(halves)
 
     lane = lax.broadcasted_iota(jnp.int32, (quarter, LANES), 1)
@@ -232,7 +246,7 @@
     second = []
     for n in range(windows):
         here = jnp.maximum(made[n * half : n * half + quarter], made[n * half + quarter : (n + 1) * half])
-        second.append(jnp.maximum(here + b2_ref[...], 0.0))
+        second.append(jnp.maximum(here + bias_two, 0.0))
 
     moved = shifted(second, 64)
     for n in range(windows + 1):
@@ -248,11 +262,11 @@
         + dot(x3[quarter : quarter + rows, :], w3b_ref[0:768, :])
         + dot(x3[quarter : quarter + rows, 0:384], w3b_ref[768:1152, :])
     )
-    made = jnp.maximum(made + b3_ref[...], 0.0) * k4_ref[...]
     bias_four = b4_ref[0]
     row_best = jnp.full((quarter, 1), -2.0, F32)
     for c in range(2):
-        summed = jnp.sum(made[:, c * LANES : (c + 1) * LANES], axis=1, keepdims=True)
+        third = jnp.maximum(made[:, c * LANES : (c + 1) * LANES] + b3_ref[...], 0.0)
+        summed = jnp.sum(third * k4_ref[...], axis=1, keepdims=True)
         final = jnp.clip(summed + bias_four, -1.0, 1.0)
         for n in range(windows):
             here = final[n * quarter : (n + 1) * quarter]
@@ -294,46 +308,53 @@
     store = jnp.transpose(frame_store, (0, 2, 1, 3))
     own = jnp.transpose(query_feats[0], (1, 0, 2))
 
+    def swap(x, k):
+        return lax.ppermute(x, "slab", [(s, s ^ k) for s in range(n_slab)])
+
     rounds = None
-    if n_query <= 8:
-        rounds = [exchange_rounds(n_query, core) for core in range(2)]
+    if n_query == 8 and n_slab % 2 == 0:
+        rounds = exchange_rounds(n_query)
+        steps = len(rounds[0])
         sent = pl.pallas_call(
             functools.partial(pick_kernel, rounds),
-            out_shape=[jax.ShapeDtypeStruct(store.shape[1:], BF16)] * n_query,
+            out_shape=[jax.ShapeDtypeStruct((2, *store.shape[1:]), BF16)] * steps
+            + [jax.ShapeDtypeStruct(store.shape[1:], BF16)] * 2,
             in_specs=[smem, anywhere],
-            out_specs=[anywhere] * n_query,
-            scratch_shapes=[pltpu.SemaphoreType.DMA((n_query,))],
+            out_specs=[vmem] * (steps + 2),
+            scratch_shapes=[pltpu.SemaphoreType.DMA((2 * steps + 2,))],
+            compiler_params=pltpu.CompilerParams(vmem_limit_bytes=2 * 1024 * 1024),
             name="pick_bands",
-        )(candidates, store)
-        blocks = []
-        for at in range(n_query - 1):
-            moves = [
-                (q * n_slab + s, (q ^ rounds[s % 2][at]) * n_slab + s) for q in range(n_query) for s in range(n_slab)
-            ]
-            blocks.append(lax.ppermute(sent[at], ("pb", "slab"), moves))
-        blocks.append(sent[n_query - 1])
+        )(candidates.T, store)
+        near = []
+        for at in range(steps):
+            moves = [(q * n_slab + s, (q ^ rounds[s % 2][at]) * n_slab + s) for q in range(n_query) for s in range(n_slab)]
+            near.append(lax.ppermute(sent[at], ("pb", "slab"), moves))
+        one_away = lax.ppermute(sent[steps], "pb", [(q, q ^ 1) for q in range(n_query)])
+        blocks = [*near, *[swap(x, 1) for x in near], one_away, sent[steps + 1]]
     else:
         ids = lax.dynamic_index_in_dim(candidates, lax.axis_index("slab"), 1, keepdims=False)
         got = lax.all_to_all(store[ids], "pb", 0, 0, tiled=True)
         blocks = [jnp.transpose(got, (1, 0, 2, 3)).reshape(regions, frames, feature_width)]
     slabs = [own]
-    for k in range(1, n_slab):
-        slabs.append(lax.ppermute(own, "slab", [(s, s ^ k) for s in range(n_slab)]))
-
-    one = jnp.tile(kernel_one.reshape(9, -1), (1, 8))
-    two = jnp.tile(kernel_two.reshape(9, 32, 64), (1, 1, 4))
-    three = jnp.tile(kernel_three.reshape(9, 64, 128), (1, 1, 2))
+    steps = [1 << i for i in range(n_slab.bit_length() - 1)]
+    for k in reversed(steps):
+        slabs = slabs + [swap(x, k) for x in slabs]
+    order = [0]
+    for k in reversed(steps):
+        order = order + [o ^ k for o in order]
+
     weights = pl.pallas_call(
         weight_kernel,
         out_shape=[jax.ShapeDtypeStruct((384, 256), BF16)] + [jax.ShapeDtypeStruct((1152, 256), BF16)] * 4,
         in_specs=[vmem] * 3,
         out_specs=[vmem] * 5,
+        compiler_params=pltpu.CompilerParams(vmem_limit_bytes=4 * 1024 * 1024),
         cost_estimate=pl.CostEstimate(flops=2_000_000, bytes_accessed=6_000_000, transcendentals=0),
         name="lay_out_kernels",
-    )(one, two, three)
+    )(kernel_one.reshape(9, 1, -1), kernel_two.reshape(9, 32, 64), kernel_three.reshape(9, 64, 128))
 
     vector = pl.pallas_call(
-        functools.partial(score_kernel, rounds, len(blocks), n_slab, regions, frames),
+        functools.partial(score_kernel, rounds, len(blocks), order, regions, frames),
         out_shape=jax.ShapeDtypeStruct((1, LANES), F32),
         in_specs=[smem] * 3 + [vmem] * (len(blocks) + n_slab + 9) + [smem],
         out_specs=vmem,
@@ -346,24 +367,24 @@
             pltpu.VMEM((17 * 64, 768), BF16),
             pltpu.VMEM((17 * 32, 768), BF16),
         ],
-        compiler_params=pltpu.CompilerParams(vmem_limit_bytes=40 * 1024 * 1024),
+        compiler_params=pltpu.CompilerParams(vmem_limit_bytes=32 * 1024 * 1024),
         cost_estimate=pl.CostEstimate(flops=2_000_000_000, bytes_accessed=8_000_000, transcendentals=0),
         name="score_pair",
     )(
-        candidates,
+        candidates.T,
         query_length,
         clip_length,
         *blocks,
         *slabs,
         *weights,
-        jnp.tile(bias_one, 4)[None],
-        jnp.tile(bias_two, 2)[None],
-        jnp.tile(bias_three, 2)[None],
-        jnp.tile(kernel_four.reshape(-1), 2)[None],
+        bias_one[None],
+        bias_two[None],
+        bias_three[None],
+        kernel_four.reshape(1, -1),
         bias_four,
     )
-    for k in (1, 2):
-        vector = vector + lax.ppermute(vector, "slab", [(s, s ^ k) for s in range(n_slab)])
+    for k in steps:
+        vector = vector + swap(vector, k)
     return vector[:, :pair_count]
 
 

time: 68 us -> 40.2 us (0.59)
  Pallas kernels: 29.9 us -> 9.41 us
  local copies, waits for them, and re-layouts: 10.2 us -> 2.38 us
  waiting for transfers between devices: 7.92 us -> 14.7 us
  starting transfers between devices: 17.5 us -> 11.5 us
    pallas_call x1, Pallas kernels: 19.8 us -> 1.48 us  [per_device(): pl.pallas_call(functools.partial(pick_kernel, rounds), out_shape=[jax.Sha...]
    ppermute x12, waiting for transfers between devices: 7.92 us -> 14.7 us  [the longest x1 5.29 us: per_device(): lax.ppermute(sent[steps], 'pb', [(q, q ^ 1) for q in range(n_query)])]
    ppermute x12, starting transfers between devices: 17.5 us -> 11.5 us  [the longest x3 6.31 us: per_device(): near.append(lax.ppermute(sent[at], ('pb', 'slab'), moves))]
    unnamed x33 -> x24, local copies, waits for them, and re-layouts: 6.63 us -> 2.38 us
    another operation x13 -> x0, local copies, waits for them, and re-layouts: 3.57 us -> none  [the longest x2 1.51 us: per_device(): three = jnp.tile(kernel_three.reshape(9, 64, 128), (1, 1, 2))]
    pallas_call x1, Pallas kernels: 2.78 us -> 0.56 us  [per_device(): pl.pallas_call(weight_kernel, out_shape=[jax.ShapeDtypeStruct((384, 256),...]
  transfers between devices with their start and end apart: 12 -> 12, of which waited for: 5 -> 4; matrix products, arithmetic and copies ran while one was open for 5% -> 0% of each run, Pallas kernels for 4% -> 5%
where the time goes in v2:
time: 40.2 us; the launch traced here: 40 us
  waiting for transfers between devices  14.7 us (37%)
  starting transfers between devices  11.5 us (29%)
  Pallas kernels  9.41 us (23%)
  local copies, waits for them, and re-layouts  2.38 us (6%)
  between operations  1.48 us (4%)
  other arithmetic  0.52 us (1%)
    pallas_call x1, Pallas kernels, per_device(): pl.pallas_call(functools.partial(score_kernel, rounds, len(blocks), order...  7.37 us
    ppermute x3, starting transfers between devices, per_device(): near.append(lax.ppermute(sent[at], ('pb', 'slab'), moves))  6.31 us
    ppermute x1, waiting for transfers between devices, per_device(): lax.ppermute(sent[steps], 'pb', [(q, q ^ 1) for q in range(n_query)])  5.29 us
    ppermute x3, waiting for transfers between devices, per_device(): near.append(lax.ppermute(sent[at], ('pb', 'slab'), moves))  5.26 us
    ppermute x8, starting transfers between devices, swap(): return lax.ppermute(x, 'slab', [(s, s ^ k) for s in range(n_slab)])  4.7 us
    ppermute x8, waiting for transfers between devices, swap(): return lax.ppermute(x, 'slab', [(s, s ^ k) for s in range(n_slab)])  4.13 us
    unnamed x24, local copies, waits for them, and re-layouts  2.38 us
    pallas_call x1, Pallas kernels, per_device(): pl.pallas_call(functools.partial(pick_kernel, rounds), out_shape=[jax.Sha...  1.48 us
  transfers between devices with their start and end apart: 12, of which 4 were waited for; matrix products, arithmetic and copies ran while one was open for 0% of the time, Pallas kernels for 5%

profile of v2, /device:TPU:0, one launch (start us, length us, event | category | flops | bytes accessed | tf_op | source)
XLA Modules:
  0.0 40.0 jit_solution(15998083061879100775)
XLA Ops:
  0.0 0.0 copy-start.3
  0.0 0.0 copy-start.8
  0.0 0.0 copy-start.7
  0.0 3.0 %collective-permute-start.7 = (bf16[9,32,256]{2,1,0:T(8,128)(2,1)}, bf16[9,32,256]{2,1,0:T(8,128)(2,1)S(1)}, u32[]{:S(2)}, u32[]{:S(2)}) collective-permute-start(bf16[9,32,256]{2,1,0:T(8,128)(2,1)} %bitcast.19), channel_id=1, source_target_pairs={{0,2},{1,3},{2,0},{3,1},{4,6},{5,7},{6,4},{7,5},{8,10},{9,11},{10,... | collective-permute-start | bytes 442376 | tf_op jit(solution)/shard_map/ppermute | solution.py:312
  3.0 0.0 copy-start
  3.0 1.7 %copy-done = bf16[32,16,9,256]{3,1,2,0:T(8,128)(2,1)S(1)} copy-done((bf16[32,16,9,256]{3,1,2,0:T(8,128)(2,1)S(1)}, bf16[32,16,9,256]{3,1,2,0:T(8,128)(2,1)}, u32[]{:S(2)}) %copy-start) | copy-done | bytes 2359320
  4.7 0.0 copy-start.4
  4.7 0.7 %copy-done.4 = s32[8,4]{0,1:T(4,128)S(1)} copy-done((s32[8,4]{0,1:T(4,128)S(1)}, s32[8,4]{0,1:T(4,128)}, u32[]{:S(2)}) %copy-start.4) | copy-done | bytes 152
  5.4 0.0 copy-start.6
  5.4 0.0 copy-start.1
  5.4 0.0 copy-start.2
  5.4 0.0 copy-start.5
  5.4 0.0 copy-start.9
  5.4 0.0 copy-start.10
  5.4 0.0 copy-start.11
  5.4 1.5 %pick_bands.1 = (bf16[2,9,16,256]{3,2,1,0:T(8,128)(2,1)S(1)}, bf16[2,9,16,256]{3,2,1,0:T(8,128)(2,1)S(1)}, bf16[2,9,16,256]{3,2,1,0:T(8,128)(2,1)S(1)}, bf16[9,1...) custom-call(s32[4,8]{1,0:T(4,128)S(1)} %bitcast.17, bf16[32,9,16,256]{3,2,1,0:T(8,128)(2,1)S(1)} %bitcast.13), custom_call_target="tpu_custom_call" | custom-call | tf_op jit(solution)/shard_map/pick_bands/pallas_call | solution.py:318
  6.9 4.6 %collective-permute-start = (bf16[2,9,16,256]{3,2,1,0:T(8,128)(2,1)S(1)}, bf16[2,9,16,256]{3,2,1,0:T(8,128)(2,1)S(1)}, u32[]{:S(2)}, u32[]{:S(2)}) collective-permute-start(bf16[2,9,16,256]{3,2,1,0:T(8,128)(2,1)S(1)} %get-tuple-element.15), channel_id=1, source_target_pairs={{0,28},{1,9},{2,30},{3,11},{4,24},{5,13},{6,26},{7,15},{8,20},{9,1... | collective-permute-start | bytes 442376 | tf_op jit(solution)/shard_map/ppermute | solution.py:331
  11.5 0.0 collective-permute-start.1
  11.5 1.7 %collective-permute-start.2 = (bf16[2,9,16,256]{3,2,1,0:T(8,128)(2,1)S(1)}, bf16[2,9,16,256]{3,2,1,0:T(8,128)(2,1)S(1)}, u32[]{:S(2)}, u32[]{:S(2)}) collective-permute-start(bf16[2,9,16,256]{3,2,1,0:T(8,128)(2,1)S(1)} %get-tuple-element.17), channel_id=1, source_target_pairs={{0,12},{1,17},{2,14},{3,19},{4,8},{5,21},{6,10},{7,23},{8,4},{9,25... | collective-permute-start | bytes 442376 | tf_op jit(solution)/shard_map/ppermute | solution.py:331
  13.2 0.5 %collective-permute-start.6 = (bf16[9,16,256]{2,1,0:T(8,128)(2,1)S(1)}, bf16[9,16,256]{2,1,0:T(8,128)(2,1)S(1)}, u32[]{:S(2)}, u32[]{:S(2)}) collective-permute-start(bf16[9,16,256]{2,1,0:T(8,128)(2,1)S(1)} %get-tuple-element.18), channel_id=1, source_target_pairs={{0,4},{4,0},{8,12},{12,8},{16,20},{20,16},{24,28},{28,24},{1,5},{5... | collective-permute-start | bytes 221192 | tf_op jit(solution)/shard_map/ppermute | solution.py:332
  13.7 5.3 %collective-permute-done.6.rest_6_ = bf16[9,16,256]{2,1,0:T(8,128)(2,1)S(1)} collective-permute-done((bf16[9,16,256]{2,1,0:T(8,128)(2,1)S(1)}, bf16[9,16,256]{2,1,0:T(8,128)(2,1)S(1)}, u32[]{:S(2)}, u32[]{:S(2)}) %collective-permute-start.6) | collective-permute-done | bytes 73760 | tf_op jit(solution)/shard_map/ppermute | solution.py:332
  19.0 0.0 copy-done.6
  19.0 0.0 collective-permute-start.8
  19.0 0.0 collective-permute-done.7.rest_9_
  19.0 0.5 %collective-permute-start.9 = (bf16[9,32,256]{2,1,0:T(8,128)(2,1)S(1)}, bf16[9,32,256]{2,1,0:T(8,128)(2,1)S(1)}, u32[]{:S(2)}, u32[]{:S(2)}) collective-permute-start(bf16[9,32,256]{2,1,0:T(8,128)(2,1)S(1)} %collective-permute-done.7.rest_9_), channel_id=1, source_target_pairs={{0,1},{1,0},{2,3},{3,2},{4,5},{5,4},{6,7},{7,6},{8,9},{9,8},{10,11... | collective-permute-start | bytes 442376 | tf_op jit(solution)/shard_map/ppermute | solution.py:312
  19.5 0.0 collective-permute-done.rest_0_
  19.5 0.1 collective-permute-start.3
  19.6 5.2 %collective-permute-done.1.rest_1_ = bf16[2,9,16,256]{3,2,1,0:T(8,128)(2,1)S(1)} collective-permute-done((bf16[2,9,16,256]{3,2,1,0:T(8,128)(2,1)S(1)}, bf16[2,9,16,256]{3,2,1,0:T(8,128)(2,1)S(1)}, u32[]{:S(2)}, u32[]{:S(2)}) %collective-permute-start.1) | collective-permute-done | bytes 147488 | tf_op jit(solution)/shard_map/ppermute | solution.py:331
  24.8 0.0 collective-permute-start.4
  24.8 0.0 collective-permute-done.2.rest_2_
  24.9 0.5 %collective-permute-start.5 = (bf16[2,9,16,256]{3,2,1,0:T(8,128)(2,1)S(1)}, bf16[2,9,16,256]{3,2,1,0:T(8,128)(2,1)S(1)}, u32[]{:S(2)}, u32[]{:S(2)}) collective-permute-start(bf16[2,9,16,256]{3,2,1,0:T(8,128)(2,1)S(1)} %collective-permute-done.2.rest_2_), channel_id=1, source_target_pairs={{0,1},{1,0},{2,3},{3,2},{4,5},{5,4},{6,7},{7,6},{8,9},{9,8},{10,11... | collective-permute-start | bytes 442376 | tf_op jit(solution)/shard_map/ppermute | solution.py:312
  26.7 0.0 copy-done.3
  26.7 0.0 copy-done.1
  26.7 0.0 copy-done.2
  26.7 0.6 %lay_out_kernels.1 = (bf16[384,256]{1,0:T(8,128)(2,1)S(1)}, bf16[1152,256]{1,0:T(8,128)(2,1)S(1)}, bf16[1152,256]{1,0:T(8,128)(2,1)S(1)}, bf16[1152,256]{1,0:T(8,128)(2,1)S(1)}, bf16[1152,256]{1,0:T(8,128)(2,1)S(1)}) custom-call(f32[9,1,32]{2,1,0:T(1,128)S(1)} %bitcast.16, f32[9,32,64]{2,1,0:T(8,128)S(1)} %bitcast.15, f32[9,64,128]{2,1,0:T(8,128)S(1)} %bitcast.14), custom_call_target="tpu_custom_call" | custom-call | flops 2000000 | bytes 6000000 | tf_op jit(solution)/shard_map/lay_out_kernels/pallas_call | solution.py:346
  27.3 0.0 collective-permute-done.8.rest_10_
  27.3 0.0 collective-permute-done.9.rest_11_
  27.3 0.0 collective-permute-done.3.rest_3_
  27.3 0.0 collective-permute-done.4.rest_4_
  27.3 0.0 collective-permute-done.5.rest_5_
  27.3 0.0 copy-done.8
  27.3 0.0 copy-done.7
  27.3 0.0 copy-done.5
  27.3 0.0 copy-done.9
  27.4 0.0 copy-done.10
  27.4 0.0 copy-done.11
  27.4 7.4 %score_pair.1 = f32[1,128]{1,0:T(1,128)S(1)} custom-call(s32[4,8]{1,0:T(4,128)S(1)} %bitcast.18, s32[1]{0:T(128)S(6)} %copy.14.qlen_ref, s32[32]{0:T(128)S(1)} %copy-done.7, bf16[2,9,16,256]{3,2,1,0:T(8,128)(2,1)S(1)} %collective-permute-done.rest_0_, bf16[2,9,16,256]{3,2,1,0:T(8,128)(2,1)S(1)} %collective-permute-done.1.rest_1_, ...), custom_call_target="tpu_custom_call" | custom-call | flops 2000000000 | bytes 8000000 | tf_op jit(solution)/shard_map/score_pair/pallas_call | solution.py:356
  34.7 0.1 collective-permute-start.10
  34.8 1.1 %collective-permute-done.10 = f32[1,128]{1,0:T(1,128)S(1)} collective-permute-done((f32[1,128]{1,0:T(1,128)S(1)}, f32[1,128]{1,0:T(1,128)S(1)}, u32[]{:S(2)}, u32[]{:S(2)}) %collective-permute-start.10) | collective-permute-done | bytes 544 | tf_op jit(solution)/shard_map/ppermute | solution.py:312
  35.9 0.5 %collective-permute-start.11 = (f32[1,128]{1,0:T(1,128)S(1)}, f32[1,128]{1,0:T(1,128)S(1)}, u32[]{:S(2)}, u32[]{:S(2)}) collective-permute-start(f32[1,128]{1,0:T(1,128)S(1)} %add.6), channel_id=1, source_target_pairs={{0,2},{1,3},{2,0},{3,1},{4,6},{5,7},{6,4},{7,5},{8,10},{9,11},{10,... | collective-permute-start | bytes 1544 | tf_op jit(solution)/shard_map/ppermute | solution.py:312
  36.5 3.0 %collective-permute-done.11 = f32[1,128]{1,0:T(1,128)S(1)} collective-permute-done((f32[1,128]{1,0:T(1,128)S(1)}, f32[1,128]{1,0:T(1,128)S(1)}, u32[]{:S(2)}, u32[]{:S(2)}) %collective-permute-start.11) | collective-permute-done | bytes 544 | tf_op jit(solution)/shard_map/ppermute | solution.py:312
  39.5 0.5 %add.7 = f32[1,128]{1,0:T(1,128)} add(f32[1,128]{1,0:T(1,128)S(1)} %add.6, f32[1,128]{1,0:T(1,128)S(1)} %collective-permute-done.11) | non-fusion elementwise | flops 128 | bytes 1536 | tf_op jit(solution)/shard_map/add | solution.py:387
  (1 shorter events, 0.0 us)
Async XLA Ops:
  0.0 26.7 %copy-start.3 = (f32[3,3,1,32]{3,2,1,0:T(1,128)S(1)}, f32[3,3,1,32]{3,2,1,0:T(1,128)}, u32[]{:S(2)}) copy-start(f32[3,3,1,32]{3,2,1,0:T(1,128)} %param.18) | copy-start | bytes 3460
  0.0 27.3 %copy-start.8 = (f32[32]{0:T(128)S(1)}, f32[32]{0:T(128)}, u32[]{:S(2)}) copy-start(f32[32]{0:T(128)} %param.19) | copy-start | bytes 388
  0.0 27.3 %copy-start.7 = (s32[32]{0:T(128)S(1)}, s32[32]{0:T(128)}, u32[]{:S(2)}) copy-start(s32[32]{0:T(128)} %clen_ref.1) | copy-start | bytes 388
  0.0 19.0 %collective-permute-start.7 = (bf16[9,32,256]{2,1,0:T(8,128)(2,1)}, bf16[9,32,256]{2,1,0:T(8,128)(2,1)S(1)}, u32[]{:S(2)}, u32[]{:S(2)}) collective-permute-start(bf16[9,32,256]{2,1,0:T(8,128)(2,1)} %bitcast.19), channel_id=1, source_target_pairs={{0,2},{1,3},{2,0},{3,1},{4,6},{5,7},{6,4},{7,5},{8,10},{9,11},{10,... | collective-permute-start | bytes 442376 | tf_op jit(solution)/shard_map/ppermute | solution.py:312
  3.0 1.7 %copy-start = (bf16[32,16,9,256]{3,1,2,0:T(8,128)(2,1)S(1)}, bf16[32,16,9,256]{3,1,2,0:T(8,128)(2,1)}, u32[]{:S(2)}) copy-start(bf16[32,16,9,256]{3,1,2,0:T(8,128)(2,1)} %param.14) | copy-start | bytes 7077892
  4.7 0.7 %copy-start.4 = (s32[8,4]{0,1:T(4,128)S(1)}, s32[8,4]{0,1:T(4,128)}, u32[]{:S(2)}) copy-start(s32[8,4]{0,1:T(4,128)} %param.15) | copy-start | bytes 388
  5.4 13.6 %copy-start.6 = (bf16[1,32,9,256]{3,1,2,0:T(8,128)(2,1)S(1)}, bf16[1,32,9,256]{3,1,2,0:T(8,128)(2,1)}, u32[]{:S(2)}) copy-start(bf16[1,32,9,256]{3,1,2,0:T(8,128)(2,1)} %param.13) | copy-start | bytes 442372
  5.4 21.3 %copy-start.1 = (f32[3,3,64,128]{3,2,1,0:T(8,128)S(1)}, f32[3,3,64,128]{3,2,1,0:T(8,128)}, u32[]{:S(2)}) copy-start(f32[3,3,64,128]{3,2,1,0:T(8,128)} %param.22) | copy-start | bytes 884740
  5.4 21.3 %copy-start.2 = (f32[3,3,32,64]{3,2,1,0:T(8,128)S(1)}, f32[3,3,32,64]{3,2,1,0:T(8,128)}, u32[]{:S(2)}) copy-start(f32[3,3,32,64]{3,2,1,0:T(8,128)} %param.20) | copy-start | bytes 221188
  5.4 22.0 %copy-start.5 = (s32[8,4]{0,1:T(4,128)S(1)}, s32[8,4]{0,1:T(4,128)}, u32[]{:S(2)}) copy-start(s32[8,4]{0,1:T(4,128)} %param.15) | copy-start | bytes 388
  5.4 22.0 %copy-start.9 = (f32[64]{0:T(128)S(1)}, f32[64]{0:T(128)}, u32[]{:S(2)}) copy-start(f32[64]{0:T(128)} %param.21) | copy-start | bytes 772
  5.4 22.0 %copy-start.10 = (f32[128]{0:T(128)S(1)}, f32[128]{0:T(128)}, u32[]{:S(2)}) copy-start(f32[128]{0:T(128)} %param.23) | copy-start | bytes 1540
  5.4 22.0 %copy-start.11 = (f32[1,1,128,1]{2,3,1,0:T(1,128)S(1)}, f32[1,1,128,1]{2,3,1,0:T(1,128)}, u32[]{:S(2)}) copy-start(f32[1,1,128,1]{2,3,1,0:T(1,128)} %param.24) | copy-start | bytes 1540
  6.9 12.6 %collective-permute-start = (bf16[2,9,16,256]{3,2,1,0:T(8,128)(2,1)S(1)}, bf16[2,9,16,256]{3,2,1,0:T(8,128)(2,1)S(1)}, u32[]{:S(2)}, u32[]{:S(2)}) collective-permute-start(bf16[2,9,16,256]{3,2,1,0:T(8,128)(2,1)S(1)} %get-tuple-element.15), channel_id=1, source_target_pairs={{0,28},{1,9},{2,30},{3,11},{4,24},{5,13},{6,26},{7,15},{8,20},{9,1... | collective-permute-start | bytes 442376 | tf_op jit(solution)/shard_map/ppermute | solution.py:331
  11.5 13.3 %collective-permute-start.1 = (bf16[2,9,16,256]{3,2,1,0:T(8,128)(2,1)S(1)}, bf16[2,9,16,256]{3,2,1,0:T(8,128)(2,1)S(1)}, u32[]{:S(2)}, u32[]{:S(2)}) collective-permute-start(bf16[2,9,16,256]{3,2,1,0:T(8,128)(2,1)S(1)} %get-tuple-element.16), channel_id=1, source_target_pairs={{0,20},{1,25},{2,22},{3,27},{4,16},{5,29},{6,18},{7,31},{8,28},{9,... | collective-permute-start | bytes 442376 | tf_op jit(solution)/shard_map/ppermute | solution.py:331
  11.5 13.3 %collective-permute-start.2 = (bf16[2,9,16,256]{3,2,1,0:T(8,128)(2,1)S(1)}, bf16[2,9,16,256]{3,2,1,0:T(8,128)(2,1)S(1)}, u32[]{:S(2)}, u32[]{:S(2)}) collective-permute-start(bf16[2,9,16,256]{3,2,1,0:T(8,128)(2,1)S(1)} %get-tuple-element.17), channel_id=1, source_target_pairs={{0,12},{1,17},{2,14},{3,19},{4,8},{5,21},{6,10},{7,23},{8,4},{9,25... | collective-permute-start | bytes 442376 | tf_op jit(solution)/shard_map/ppermute | solution.py:331
  13.2 5.8 %collective-permute-start.6 = (bf16[9,16,256]{2,1,0:T(8,128)(2,1)S(1)}, bf16[9,16,256]{2,1,0:T(8,128)(2,1)S(1)}, u32[]{:S(2)}, u32[]{:S(2)}) collective-permute-start(bf16[9,16,256]{2,1,0:T(8,128)(2,1)S(1)} %get-tuple-element.18), channel_id=1, source_target_pairs={{0,4},{4,0},{8,12},{12,8},{16,20},{20,16},{24,28},{28,24},{1,5},{5... | collective-permute-start | bytes 221192 | tf_op jit(solution)/shard_map/ppermute | solution.py:332
  19.0 8.3 %collective-permute-start.8 = (bf16[9,32,256]{2,1,0:T(8,128)(2,1)S(1)}, bf16[9,32,256]{2,1,0:T(8,128)(2,1)S(1)}, u32[]{:S(2)}, u32[]{:S(2)}) collective-permute-start(bf16[9,32,256]{2,1,0:T(8,128)(2,1)S(1)} %bitcast.20), channel_id=1, source_target_pairs={{0,1},{1,0},{2,3},{3,2},{4,5},{5,4},{6,7},{7,6},{8,9},{9,8},{10,11... | collective-permute-start | bytes 442376 | tf_op jit(solution)/shard_map/ppermute | solution.py:312
  19.0 8.3 %collective-permute-start.9 = (bf16[9,32,256]{2,1,0:T(8,128)(2,1)S(1)}, bf16[9,32,256]{2,1,0:T(8,128)(2,1)S(1)}, u32[]{:S(2)}, u32[]{:S(2)}) collective-permute-start(bf16[9,32,256]{2,1,0:T(8,128)(2,1)S(1)} %collective-permute-done.7.rest_9_), channel_id=1, source_target_pairs={{0,1},{1,0},{2,3},{3,2},{4,5},{5,4},{6,7},{7,6},{8,9},{9,8},{10,11... | collective-permute-start | bytes 442376 | tf_op jit(solution)/shard_map/ppermute | solution.py:312
  19.5 7.8 %collective-permute-start.3 = (bf16[2,9,16,256]{3,2,1,0:T(8,128)(2,1)S(1)}, bf16[2,9,16,256]{3,2,1,0:T(8,128)(2,1)S(1)}, u32[]{:S(2)}, u32[]{:S(2)}) collective-permute-start(bf16[2,9,16,256]{3,2,1,0:T(8,128)(2,1)S(1)} %collective-permute-done.rest_0_), channel_id=1, source_target_pairs={{0,1},{1,0},{2,3},{3,2},{4,5},{5,4},{6,7},{7,6},{8,9},{9,8},{10,11... | collective-permute-start | bytes 442376 | tf_op jit(solution)/shard_map/ppermute | solution.py:312
  24.8 2.4 %collective-permute-start.4 = (bf16[2,9,16,256]{3,2,1,0:T(8,128)(2,1)S(1)}, bf16[2,9,16,256]{3,2,1,0:T(8,128)(2,1)S(1)}, u32[]{:S(2)}, u32[]{:S(2)}) collective-permute-start(bf16[2,9,16,256]{3,2,1,0:T(8,128)(2,1)S(1)} %collective-permute-done.1.rest_1_), channel_id=1, source_target_pairs={{0,1},{1,0},{2,3},{3,2},{4,5},{5,4},{6,7},{7,6},{8,9},{9,8},{10,11... | collective-permute-start | bytes 442376 | tf_op jit(solution)/shard_map/ppermute | solution.py:312
  24.9 2.5 %collective-permute-start.5 = (bf16[2,9,16,256]{3,2,1,0:T(8,128)(2,1)S(1)}, bf16[2,9,16,256]{3,2,1,0:T(8,128)(2,1)S(1)}, u32[]{:S(2)}, u32[]{:S(2)}) collective-permute-start(bf16[2,9,16,256]{3,2,1,0:T(8,128)(2,1)S(1)} %collective-permute-done.2.rest_2_), channel_id=1, source_target_pairs={{0,1},{1,0},{2,3},{3,2},{4,5},{5,4},{6,7},{7,6},{8,9},{9,8},{10,11... | collective-permute-start | bytes 442376 | tf_op jit(solution)/shard_map/ppermute | solution.py:312
  34.7 1.2 %collective-permute-start.10 = (f32[1,128]{1,0:T(1,128)S(1)}, f32[1,128]{1,0:T(1,128)S(1)}, u32[]{:S(2)}, u32[]{:S(2)}) collective-permute-start(f32[1,128]{1,0:T(1,128)S(1)} %score_pair.1), channel_id=1, source_target_pairs={{0,1},{1,0},{2,3},{3,2},{4,5},{5,4},{6,7},{7,6},{8,9},{9,8},{10,11... | collective-permute-start | bytes 1544 | tf_op jit(solution)/shard_map/ppermute | solution.py:312
  35.9 3.5 %collective-permute-start.11 = (f32[1,128]{1,0:T(1,128)S(1)}, f32[1,128]{1,0:T(1,128)S(1)}, u32[]{:S(2)}, u32[]{:S(2)}) collective-permute-start(f32[1,128]{1,0:T(1,128)S(1)} %add.6), channel_id=1, source_target_pairs={{0,2},{1,3},{2,0},{3,1},{4,6},{5,7},{6,4},{7,5},{8,10},{9,11},{10,... | collective-permute-start | bytes 1544 | tf_op jit(solution)/shard_map/ppermute | solution.py:312

commit v3 on v2

--- a/solution.py
+++ b/solution.py
@@ -13,8 +13,7 @@
 
 
 def exchange_rounds(count):
-    odd, even = list(range(count - 1, 1, -2)), list(range(count - 2, 1, -2))
-    return odd, even[-1:] + even[:-1]
+    return list(range(count - 1, 1, -2)), list(range(count - 2, 1, -2))
 
 
 def split(x):
@@ -22,13 +21,24 @@
     return high, (x - high.astype(F32)).astype(BF16)
 
 
-def pick_kernel(rounds, cand_ref, store_ref, *rest):
-    outs, sem = rest[:-1], rest[-1]
+def split_three(x):
+    high = x.astype(BF16)
+    rest = x - high.astype(F32)
+    middle = rest.astype(BF16)
+    return high, middle, (rest - middle.astype(F32)).astype(BF16)
+
+
+def pick_kernel(rounds, cand_hbm, store_ref, own_ref, *rest):
+    outs, feats, cand_ref, sem = rest[:-3], rest[-3], rest[-2], rest[-1]
     query = lax.axis_index("pb")
     pair = lax.axis_index("slab")
     odd = lax.rem(pair, 2)
     steps = len(rounds[0])
-    copies = []
+    listed = pltpu.make_async_copy(cand_hbm, cand_ref, sem.at[2 * steps + 3])
+    listed.start()
+    copies = [pltpu.make_async_copy(own_ref, feats, sem.at[2 * steps + 2])]
+    copies[0].start()
+    listed.wait()
     for at, out in enumerate(outs):
         if at < steps:
             target = query ^ jnp.where(odd == 0, rounds[0][at], rounds[1][at])
@@ -38,26 +48,15 @@
         else:
             clip = cand_ref[pair, query ^ (steps + 1 - at)]
             copies.append(pltpu.make_async_copy(store_ref.at[clip], out, sem.at[steps + at]))
-    for copy in copies:
+    for copy in copies[1:]:
         copy.start()
     for copy in copies:
         copy.wait()
 
 
-def weight_kernel(one_ref, two_ref, three_ref, w1_ref, w2a_ref, w2b_ref, w3a_ref, w3b_ref):
-    def place(ref, base, value):
-        rows = value.shape[0]
-        span = ref.shape[0] // 3
-        high, low = split(value)
-        ref[pl.ds(base, rows), :] = high
-        ref[pl.ds(span + base, rows), :] = high
-        ref[pl.ds(2 * span + base, rows), :] = low
-
-    def iotas(rows):
-        return (
-            lax.broadcasted_iota(jnp.int32, (rows, 256), 0),
-            lax.broadcasted_iota(jnp.int32, (rows, 256), 1),
-        )
+def weight_kernel(one_ref, two_ref, three_ref, w1_ref, w2_ref, w3a_ref, w3b_ref):
+    row = lax.broadcasted_iota(jnp.int32, (LANES, 256), 0)
+    lane = lax.broadcasted_iota(jnp.int32, (LANES, 256), 1)
 
     def wide(x, times):
         while times > 1:
@@ -65,34 +64,50 @@
             times //= 2
         return x
 
-    row, lane = iotas(LANES)
+    def tall(x, times):
+        return jnp.concatenate([x] * times, axis=0)
+
     group = lane // 32
     column = 2 * (group % 4) + group // 4
+    slot = row // 16
     total = jnp.zeros((LANES, 256), F32)
     for d in range(3):
         for t in range(3):
-            mask = (row // 16 == d) & (row % 16 - column == t)
+            mask = (slot < 6) & (slot % 3 == d) & (row % 16 - column == t)
             total = jnp.where(mask, wide(one_ref[3 * d + t], 8), total)
-    place(w1_ref, 0, total)
+    high, middle, low = split_three(total)
+    both = jnp.where(slot < 3, high.astype(F32), middle.astype(F32)).astype(BF16)
+    w1_ref[0:LANES, :] = both
+    w1_ref[LANES : 2 * LANES, :] = both
+    w1_ref[2 * LANES : 3 * LANES, :] = jnp.where(slot < 3, low.astype(F32), 0.0).astype(BF16)
+
+    def place(ref, base, starts, value):
+        for start, part in zip(starts, split_three(value)):
+            for s in start:
+                ref[s + base : s + base + value.shape[0], :] = part
 
     group = lane // 64
     column = 2 * (group % 2) + group // 2
-    for ref, first in ((w2a_ref, 0), (w2b_ref, 4)):
-        for d in range(3):
-            total = jnp.zeros((LANES, 256), F32)
+    starts = ((0, 640), (1280,), (1920,))
+    for d in range(3):
+        for first, rows, base in ((0, 128, 128 * d), (4, 64, 384 + 64 * d)):
+            total = jnp.zeros((rows, 256), F32)
             for t in range(3):
-                tile = jnp.concatenate([wide(two_ref[3 * d + t], 4)] * 4, axis=0)
-                total = jnp.where(row // 32 + first - column == t, tile, total)
-            place(ref, LANES * d, total)
+                tile = tall(wide(two_ref[3 * d + t], 4), rows // 32)
+                total = jnp.where((row // 32 + first - column)[:rows] == t, tile, total)
+            place(w2_ref, base, starts, total)
+    for start in range(0, w2_ref.shape[0], 640):
+        w2_ref[start + 576 : start + 640, :] = jnp.zeros((64, 256), BF16)
 
     column = lane // 128
+    starts = ((0, 384), (768, 1152), (1536,))
     for ref, first in ((w3a_ref, 0), (w3b_ref, 2)):
         for d in range(3):
             total = jnp.zeros((LANES, 256), F32)
             for t in range(3):
-                tile = jnp.concatenate([wide(three_ref[3 * d + t], 2)] * 2, axis=0)
+                tile = tall(wide(three_ref[3 * d + t], 2), 2)
                 total = jnp.where(row // 64 + first - column == t, tile, total)
-            place(ref, LANES * d, total)
+            place(ref, LANES * d, starts, total)
 
 
 def moved_rows(x, step):
@@ -123,8 +138,7 @@
     slabs = rest[n_blocks : n_blocks + n_slabs]
     (
         w1_ref,
-        w2a_ref,
-        w2b_ref,
+        w2_ref,
         w3a_ref,
         w3b_ref,
         b1_ref,
@@ -140,6 +154,7 @@
         x1,
         x2,
         x3,
+        pooled_two,
     ) = rest[n_blocks + n_slabs :]
     query = lax.axis_index("pb")
     pair = lax.axis_index("slab")
@@ -186,8 +201,11 @@
     rolled = [pltpu.roll(ordered, 8 * m + 1, 1) for m in range(16)]
     lane = lax.broadcasted_iota(jnp.int32, (frames, LANES), 1)
     for n in range(windows):
-        taps = [rolled[(2 * d - n) % 16][d * quarter : d * quarter + frames] for d in range(3)]
-        field = jnp.where(lane < 16, taps[0], jnp.where(lane < 32, taps[1], taps[2]))
+        field = None
+        for slot in range(5, -1, -1):
+            d = slot % 3
+            tap = rolled[(2 * slot - n) % 16][d * quarter : d * quarter + frames]
+            field = tap if field is None else jnp.where(lane < 16 * slot + 16, tap, field)
         if n == 0:
             field = jnp.where(lane % 16 == 0, 0.0, field)
         if n == windows - 1:
@@ -225,28 +243,36 @@
     odds = shifted([x[1] for x in first], 32)
     half = 2 * quarter
     for n in range(windows + 1):
-        base = n * half
-        e = split(even[n])
-        o = split(odds[n])
-        down = split(moved_rows(odds[n], 1))
-        up = split(moved_rows(even[n], -1))
-        for d, (top, bottom) in enumerate(((down, e), (e, o), (o, up))):
-            for part in range(2):
-                at = part * 3 * LANES + d * LANES
-                x2[base : base + quarter, at : at + LANES] = top[part]
-                x2[base + quarter : base + half, at : at + LANES] = bottom[part]
-    rows = windows * half
-    made = (
-        dot(x2[0:rows, :], w2a_ref[0:768, :])
-        + dot(x2[0:rows, 0:384], w2a_ref[768:1152, :])
-        + dot(x2[half : half + rows, :], w2b_ref[0:768, :])
-        + dot(x2[half : half + rows, 0:384], w2b_ref[768:1152, :])
-    )
-    made = jnp.maximum(made[:, :LANES], made[:, LANES:])
-    second = []
-    for n in range(windows):
-        here = jnp.maximum(made[n * half : n * half + quarter], made[n * half + quarter : (n + 1) * half])
-        second.append(jnp.maximum(here + bias_two, 0.0))
+        e, o = even[n], odds[n]
+        below, above = moved_rows(o, 1), moved_rows(e, -1)
+        if n < windows:
+            for d, values in enumerate(((below, e), (e, o), (o, above))):
+                high, low = split(jnp.concatenate(values, axis=0))
+                x2[n * half : (n + 1) * half, d * LANES : (d + 1) * LANES] = high
+                x2[n * half : (n + 1) * half, 640 + d * LANES : 640 + (d + 1) * LANES] = low
+        if n > 0:
+            base = (n - 1) * half
+            packed = (
+                jnp.where(lane < 64, below, pltpu.roll(e, 64, 1)),
+                jnp.where(lane < 64, e, pltpu.roll(o, 64, 1)),
+            )
+            for i, values in enumerate((packed, (o, above))):
+                high, low = split(jnp.concatenate(values, axis=0))
+                at = (3 + i) * LANES
+                x2[base : base + half, at : at + LANES] = high
+                x2[base : base + half, 640 + at : 640 + at + LANES] = low
+    for n in range(0, windows, 2):
+        rows = pl.ds(n * half, 2 * half)
+        made = (
+            dot(x2[rows, :], w2_ref[0:1280, :])
+            + dot(x2[rows, 0:640], w2_ref[1280:1920, :])
+            + dot(x2[rows, 0:640], w2_ref[1920:2560, :])
+        )
+        made = jnp.maximum(made[:, :LANES], made[:, LANES:])
+        for i in range(2):
+            here = jnp.maximum(made[i * half : i * half + quarter], made[i * half + quarter : (i + 1) * half])
+            pooled_two[n + i] = jnp.maximum(here + bias_two, 0.0)
+    second = [pooled_two[n] for n in range(windows)]
 
     moved = shifted(second, 64)
     for n in range(windows + 1):
@@ -255,23 +281,25 @@
             high, low = split(value)
             x3[base : base + quarter, d * LANES : (d + 1) * LANES] = high
             x3[base : base + quarter, (3 + d) * LANES : (4 + d) * LANES] = low
-    rows = windows * quarter
-    made = (
-        dot(x3[0:rows, :], w3a_ref[0:768, :])
-        + dot(x3[0:rows, 0:384], w3a_ref[768:1152, :])
-        + dot(x3[quarter : quarter + rows, :], w3b_ref[0:768, :])
-        + dot(x3[quarter : quarter + rows, 0:384], w3b_ref[768:1152, :])
-    )
     bias_four = b4_ref[0]
     row_best = jnp.full((quarter, 1), -2.0, F32)
-    for c in range(2):
-        third = jnp.maximum(made[:, c * LANES : (c + 1) * LANES] + b3_ref[...], 0.0)
-        summed = jnp.sum(third * k4_ref[...], axis=1, keepdims=True)
-        final = jnp.clip(summed + bias_four, -1.0, 1.0)
-        for n in range(windows):
-            here = final[n * quarter : (n + 1) * quarter]
-            keep = 4 * (2 * n + c) < clip_len
-            row_best = jnp.maximum(row_best, jnp.where(keep, here, -2.0))
+    group = 4
+    for n in range(0, windows, group):
+        made = jnp.zeros((group * quarter, 256), F32)
+        for at, ref in ((n, w3a_ref), (n + 1, w3b_ref)):
+            rows = pl.ds(at * quarter, group * quarter)
+            made = made + (
+                dot(x3[rows, :], ref[0:768, :])
+                + dot(x3[rows, :], ref[768:1536, :])
+                + dot(x3[rows, 0:384], ref[1536:1920, :])
+            )
+        for c in range(2):
+            third = jnp.maximum(made[:, c * LANES : (c + 1) * LANES] + b3_ref[...], 0.0)
+            summed = jnp.sum(third * k4_ref[...], axis=1, keepdims=True)
+            final = jnp.clip(summed + bias_four, -1.0, 1.0)
+            for i in range(group):
+                keep = 4 * (2 * (n + i) + c) < clip_len
+                row_best = jnp.maximum(row_best, jnp.where(keep, final[i * quarter : (i + 1) * quarter], -2.0))
     row = lax.broadcasted_iota(jnp.int32, (quarter, 1), 0)
     kept = jnp.where(4 * row < query_len, row_best, 0.0)
     number = jnp.broadcast_to(((query_len + 3) // 4).astype(F32), (1, 1))
@@ -304,7 +332,7 @@
     assert pair_count == n_slab and slab_rows * n_slab == frames == LANES
     vmem = pl.BlockSpec(memory_space=pltpu.VMEM)
     smem = pl.BlockSpec(memory_space=pltpu.SMEM)
-    anywhere = pl.BlockSpec(memory_space=pl.ANY)
+    in_hbm = pl.BlockSpec(memory_space=pltpu.HBM)
     store = jnp.transpose(frame_store, (0, 2, 1, 3))
     own = jnp.transpose(query_feats[0], (1, 0, 2))
 
@@ -318,13 +346,18 @@
         sent = pl.pallas_call(
             functools.partial(pick_kernel, rounds),
             out_shape=[jax.ShapeDtypeStruct((2, *store.shape[1:]), BF16)] * steps
-            + [jax.ShapeDtypeStruct(store.shape[1:], BF16)] * 2,
-            in_specs=[smem, anywhere],
-            out_specs=[vmem] * (steps + 2),
-            scratch_shapes=[pltpu.SemaphoreType.DMA((2 * steps + 2,))],
+            + [jax.ShapeDtypeStruct(store.shape[1:], BF16)] * 2
+            + [jax.ShapeDtypeStruct(own.shape, BF16)],
+            in_specs=[in_hbm] * 3,
+            out_specs=[vmem] * (steps + 3),
+            scratch_shapes=[
+                pltpu.SMEM(candidates.T.shape, jnp.int32),
+                pltpu.SemaphoreType.DMA((2 * steps + 4,)),
+            ],
             compiler_params=pltpu.CompilerParams(vmem_limit_bytes=2 * 1024 * 1024),
             name="pick_bands",
-        )(candidates.T, store)
+        )(*[pltpu.with_memory_space_constraint(x, pltpu.HBM) for x in (candidates.T, store, own)])
+        own = sent[steps + 2]
         near = []
         for at in range(steps):
             moves = [(q * n_slab + s, (q ^ rounds[s % 2][at]) * n_slab + s) for q in range(n_query) for s in range(n_slab)]
@@ -345,9 +378,9 @@
 
     weights = pl.pallas_call(
         weight_kernel,
-        out_shape=[jax.ShapeDtypeStruct((384, 256), BF16)] + [jax.ShapeDtypeStruct((1152, 256), BF16)] * 4,
+        out_shape=[jax.ShapeDtypeStruct((rows, 256), BF16) for rows in (384, 2560, 1920, 1920)],
         in_specs=[vmem] * 3,
-        out_specs=[vmem] * 5,
+        out_specs=[vmem] * 4,
         compiler_params=pltpu.CompilerParams(vmem_limit_bytes=4 * 1024 * 1024),
         cost_estimate=pl.CostEstimate(flops=2_000_000, bytes_accessed=6_000_000, transcendentals=0),
         name="lay_out_kernels",
@@ -356,7 +389,7 @@
     vector = pl.pallas_call(
         functools.partial(score_kernel, rounds, len(blocks), order, regions, frames),
         out_shape=jax.ShapeDtypeStruct((1, LANES), F32),
-        in_specs=[smem] * 3 + [vmem] * (len(blocks) + n_slab + 9) + [smem],
+        in_specs=[smem] * 3 + [vmem] * (len(blocks) + n_slab + 8) + [smem],
         out_specs=vmem,
         scratch_shapes=[
             pltpu.VMEM((regions, frames, feature_width), BF16),
@@ -364,8 +397,9 @@
             pltpu.VMEM((regions * frames, frames), F32),
             pltpu.VMEM((frames, frames), F32),
             pltpu.VMEM((16 * frames, 256), BF16),
-            pltpu.VMEM((17 * 64, 768), BF16),
+            pltpu.VMEM((16 * 64, 1280), BF16),
             pltpu.VMEM((17 * 32, 768), BF16),
+            pltpu.VMEM((16, 32, LANES), F32),
         ],
         compiler_params=pltpu.CompilerParams(vmem_limit_bytes=32 * 1024 * 1024),
         cost_estimate=pl.CostEstimate(flops=2_000_000_000, bytes_accessed=8_000_000, transcendentals=0),
@@ -383,8 +417,7 @@
         kernel_four.reshape(1, -1),
         bias_four,
     )
-    for k in steps:
-        vector = vector + swap(vector, k)
+    vector = sum([swap(vector, k) for k in reversed(range(1, n_slab))], vector)
     return vector[:, :pair_count]
 
 

time: 40.2 us -> 35.5 us (0.88)
  waiting for transfers between devices: 14.7 us -> 11.3 us
  local copies, waits for them, and re-layouts: 2.38 us -> 0.04 us
  starting transfers between devices: 11.5 us -> 12.9 us
    unnamed x24 -> x18, local copies, waits for them, and re-layouts: 2.38 us -> 0.04 us
    ppermute x3, starting transfers between devices: 6.31 us -> 7.77 us  [per_device(): near.append(lax.ppermute(sent[at], ('pb', 'slab'), moves))]
    ppermute x3, waiting for transfers between devices: 5.26 us -> 4.07 us  [per_device(): near.append(lax.ppermute(sent[at], ('pb', 'slab'), moves))]
    ppermute x8 -> x9, waiting for transfers between devices: 4.13 us -> 2.98 us  [swap(): return lax.ppermute(x, 'slab', [(s, s ^ k) for s in range(n_slab)])]
    ppermute x1, waiting for transfers between devices: 5.29 us -> 4.21 us  [per_device(): lax.ppermute(sent[steps], 'pb', [(q, q ^ 1) for q in range(n_query)])]
    pallas_call x1, Pallas kernels: 7.37 us -> 6.4 us  [per_device(): pl.pallas_call(functools.partial(score_kernel, rounds, len(blocks), order...]
    pallas_call x1, Pallas kernels: 1.48 us -> 2.06 us  [per_device(): pl.pallas_call(functools.partial(pick_kernel, rounds), out_shape=[jax.Sha...]
    ppermute x8 -> x9, starting transfers between devices: 4.7 us -> 4.58 us  [swap(): return lax.ppermute(x, 'slab', [(s, s ^ k) for s in range(n_slab)])]
  transfers between devices with their start and end apart: 12 -> 13, of which waited for: 4 -> 4; matrix products, arithmetic and copies ran while one was open for 0% -> 0% of each run, Pallas kernels for 5% -> 2%
where the time goes in v3:
time: 35.5 us; the launch traced here: 35.3 us
  starting transfers between devices  12.9 us (36%)
  waiting for transfers between devices  11.3 us (32%)
  Pallas kernels  9.19 us (26%)
  between operations  1.48 us (4%)
  other arithmetic  0.52 us (1%)
    ppermute x3, starting transfers between devices, per_device(): near.append(lax.ppermute(sent[at], ('pb', 'slab'), moves))  7.77 us
    pallas_call x1, Pallas kernels, per_device(): pl.pallas_call(functools.partial(score_kernel, rounds, len(blocks), order...  6.4 us
    ppermute x9, starting transfers between devices, swap(): return lax.ppermute(x, 'slab', [(s, s ^ k) for s in range(n_slab)])  4.58 us
    ppermute x1, waiting for transfers between devices, per_device(): lax.ppermute(sent[steps], 'pb', [(q, q ^ 1) for q in range(n_query)])  4.21 us
    ppermute x3, waiting for transfers between devices, per_device(): near.append(lax.ppermute(sent[at], ('pb', 'slab'), moves))  4.07 us
    ppermute x9, waiting for transfers between devices, swap(): return lax.ppermute(x, 'slab', [(s, s ^ k) for s in range(n_slab)])  2.98 us
    pallas_call x1, Pallas kernels, per_device(): pl.pallas_call(functools.partial(pick_kernel, rounds), out_shape=[jax.Sha...  2.06 us
    pallas_call x1, Pallas kernels, per_device(): pl.pallas_call(weight_kernel, out_shape=[jax.ShapeDtypeStruct((rows, 256)...  0.73 us
  transfers between devices with their start and end apart: 13, of which 4 were waited for; matrix products, arithmetic and copies ran while one was open for 0% of the time, Pallas kernels for 2%

profile of v3, /device:TPU:0, one launch (start us, length us, event | category | flops | bytes accessed | tf_op | source)
XLA Modules:
  0.0 35.3 jit_solution(7437331994668857091)
XLA Ops:
  0.0 0.0 copy-start.3
  0.0 0.0 copy-start
  0.0 0.0 copy-start.1
  0.0 0.0 copy-start.2
  0.0 0.0 copy-start.8
  0.0 0.0 copy-start.7
  0.0 0.0 copy-start.6
  0.0 0.0 copy-start.5
  0.0 0.0 copy-start.4
  0.1 2.1 %pick_bands.1 = (bf16[2,9,16,256]{3,2,1,0:T(8,128)(2,1)S(1)}, bf16[2,9,16,256]{3,2,1,0:T(8,128)(2,1)S(1)}, bf16[2,9,16,256]{3,2,1,0:T(8,128)(2,1)S(1)}, bf16[9,1...) custom-call(s32[4,8]{1,0:T(4,128)} %bitcast.16, ...), custom_call_target="tpu_custom_call" | custom-call | tf_op jit(solution)/shard_map/pick_bands/pallas_call | solution.py:346
  2.1 6.1 %collective-permute-start = (bf16[2,9,16,256]{3,2,1,0:T(8,128)(2,1)S(1)}, bf16[2,9,16,256]{3,2,1,0:T(8,128)(2,1)S(1)}, u32[]{:S(2)}, u32[]{:S(2)}) collective-permute-start(bf16[2,9,16,256]{3,2,1,0:T(8,128)(2,1)S(1)} %get-tuple-element.15), channel_id=1, source_target_pairs={{0,28},{1,25},{2,30},{3,27},{4,24},{5,29},{6,26},{7,31},{8,20},{9,... | collective-permute-start | bytes 442376 | tf_op jit(solution)/shard_map/ppermute | solution.py:364
  8.2 0.0 collective-permute-start.1
  8.2 1.7 %collective-permute-start.2 = (bf16[2,9,16,256]{3,2,1,0:T(8,128)(2,1)S(1)}, bf16[2,9,16,256]{3,2,1,0:T(8,128)(2,1)S(1)}, u32[]{:S(2)}, u32[]{:S(2)}) collective-permute-start(bf16[2,9,16,256]{3,2,1,0:T(8,128)(2,1)S(1)} %get-tuple-element.17), channel_id=1, source_target_pairs={{0,12},{1,9},{2,14},{3,11},{4,8},{5,13},{6,10},{7,15},{8,4},{9,1},... | collective-permute-start | bytes 442376 | tf_op jit(solution)/shard_map/ppermute | solution.py:364
  9.9 1.5 %collective-permute-start.7 = (bf16[9,32,256]{2,1,0:T(8,128)(2,1)S(1)}, bf16[9,32,256]{2,1,0:T(8,128)(2,1)S(1)}, u32[]{:S(2)}, u32[]{:S(2)}) collective-permute-start(bf16[9,32,256]{2,1,0:T(8,128)(2,1)S(1)} %get-tuple-element.20.rest_8_), channel_id=1, source_target_pairs={{0,2},{1,3},{2,0},{3,1},{4,6},{5,7},{6,4},{7,5},{8,10},{9,11},{10,... | collective-permute-start | bytes 442376 | tf_op jit(solution)/shard_map/ppermute | solution.py:340
  11.4 0.5 %collective-permute-start.6 = (bf16[9,16,256]{2,1,0:T(8,128)(2,1)S(1)}, bf16[9,16,256]{2,1,0:T(8,128)(2,1)S(1)}, u32[]{:S(2)}, u32[]{:S(2)}) collective-permute-start(bf16[9,16,256]{2,1,0:T(8,128)(2,1)S(1)} %get-tuple-element.18), channel_id=1, source_target_pairs={{0,4},{4,0},{8,12},{12,8},{16,20},{20,16},{24,28},{28,24},{1,5},{5... | collective-permute-start | bytes 221192 | tf_op jit(solution)/shard_map/ppermute | solution.py:365
  11.9 4.2 %collective-permute-done.6.rest_6_ = bf16[9,16,256]{2,1,0:T(8,128)(2,1)S(1)} collective-permute-done((bf16[9,16,256]{2,1,0:T(8,128)(2,1)S(1)}, bf16[9,16,256]{2,1,0:T(8,128)(2,1)S(1)}, u32[]{:S(2)}, u32[]{:S(2)}) %collective-permute-start.6) | collective-permute-done | bytes 73760 | tf_op jit(solution)/shard_map/ppermute | solution.py:365
  16.1 0.0 collective-permute-start.8
  16.1 0.0 collective-permute-done.rest_0_
  16.1 0.5 %collective-permute-start.3 = (bf16[2,9,16,256]{3,2,1,0:T(8,128)(2,1)S(1)}, bf16[2,9,16,256]{3,2,1,0:T(8,128)(2,1)S(1)}, u32[]{:S(2)}, u32[]{:S(2)}) collective-permute-start(bf16[2,9,16,256]{3,2,1,0:T(8,128)(2,1)S(1)} %collective-permute-done.rest_0_), channel_id=1, source_target_pairs={{0,1},{1,0},{2,3},{3,2},{4,5},{5,4},{6,7},{7,6},{8,9},{9,8},{10,11... | collective-permute-start | bytes 442376 | tf_op jit(solution)/shard_map/ppermute | solution.py:340
  16.6 4.1 %collective-permute-done.1.rest_1_ = bf16[2,9,16,256]{3,2,1,0:T(8,128)(2,1)S(1)} collective-permute-done((bf16[2,9,16,256]{3,2,1,0:T(8,128)(2,1)S(1)}, bf16[2,9,16,256]{3,2,1,0:T(8,128)(2,1)S(1)}, u32[]{:S(2)}, u32[]{:S(2)}) %collective-permute-start.1) | collective-permute-done | bytes 147488 | tf_op jit(solution)/shard_map/ppermute | solution.py:364
  20.7 0.0 collective-permute-start.4
  20.7 0.0 collective-permute-done.2.rest_2_
  20.7 0.5 %collective-permute-start.5 = (bf16[2,9,16,256]{3,2,1,0:T(8,128)(2,1)S(1)}, bf16[2,9,16,256]{3,2,1,0:T(8,128)(2,1)S(1)}, u32[]{:S(2)}, u32[]{:S(2)}) collective-permute-start(bf16[2,9,16,256]{3,2,1,0:T(8,128)(2,1)S(1)} %collective-permute-done.2.rest_2_), channel_id=1, source_target_pairs={{0,1},{1,0},{2,3},{3,2},{4,5},{5,4},{6,7},{7,6},{8,9},{9,8},{10,11... | collective-permute-start | bytes 442376 | tf_op jit(solution)/shard_map/ppermute | solution.py:340
  21.2 0.0 collective-permute-done.7.rest_9_
  21.2 0.1 collective-permute-start.9
  22.6 0.0 copy-done
  22.6 0.0 copy-done.1
  22.6 0.0 copy-done.2
  22.6 0.7 %lay_out_kernels.1 = (bf16[384,256]{1,0:T(8,128)(2,1)S(1)}, bf16[2560,256]{1,0:T(8,128)(2,1)S(1)}, bf16[1920,256]{1,0:T(8,128)(2,1)S(1)}, bf16[1920,256]{1,0:T(8,128)(2,1)S(1)}) custom-call(f32[9,1,32]{2,1,0:T(1,128)S(1)} %bitcast.15, f32[9,32,64]{2,1,0:T(8,128)S(1)} %bitcast.14, f32[9,64,128]{2,1,0:T(8,128)S(1)} %bitcast.13), custom_call_target="tpu_custom_call" | custom-call | flops 2000000 | bytes 6000000 | tf_op jit(solution)/shard_map/lay_out_kernels/pallas_call | solution.py:379
  23.3 0.0 collective-permute-done.8.rest_10_
  23.4 0.0 collective-permute-done.3.rest_3_
  23.4 0.0 collective-permute-done.4.rest_4_
  23.4 0.0 collective-permute-done.5.rest_5_
  23.4 0.0 collective-permute-done.9.rest_11_
  23.4 0.0 copy-done.3
  23.4 0.0 copy-done.8
  23.4 0.0 copy-done.7
  23.4 0.0 copy-done.6
  23.4 0.0 copy-done.5
  23.4 0.0 copy-done.4
  23.5 6.4 %score_pair.1 = f32[1,128]{1,0:T(1,128)S(1)} custom-call(s32[4,8]{1,0:T(4,128)S(1)} %bitcast.17, s32[1]{0:T(128)S(6)} %copy.14.qlen_ref, s32[32]{0:T(128)S(1)} %copy-done.4, bf16[2,9,16,256]{3,2,1,0:T(8,128)(2,1)S(1)} %collective-permute-done.rest_0_, bf16[2,9,16,256]{3,2,1,0:T(8,128)(2,1)S(1)} %collective-permute-done.1.rest_1_, ...), custom_call_target="tpu_custom_call" | custom-call | flops 2000000000 | bytes 8000000 | tf_op jit(solution)/shard_map/score_pair/pallas_call | solution.py:389
  29.9 0.5 %collective-permute-start.12 = (f32[1,128]{1,0:T(1,128)S(1)}, f32[1,128]{1,0:T(1,128)S(1)}, u32[]{:S(2)}, u32[]{:S(2)}) collective-permute-start(f32[1,128]{1,0:T(1,128)S(1)} %score_pair.1), channel_id=1, source_target_pairs={{0,1},{1,0},{2,3},{3,2},{4,5},{5,4},{6,7},{7,6},{8,9},{9,8},{10,11... | collective-permute-start | bytes 1544 | tf_op jit(solution)/shard_map/ppermute | solution.py:340
  30.4 1.5 %collective-permute-start.11 = (f32[1,128]{1,0:T(1,128)S(1)}, f32[1,128]{1,0:T(1,128)S(1)}, u32[]{:S(2)}, u32[]{:S(2)}) collective-permute-start(f32[1,128]{1,0:T(1,128)S(1)} %score_pair.1), channel_id=1, source_target_pairs={{0,2},{1,3},{2,0},{3,1},{4,6},{5,7},{6,4},{7,5},{8,10},{9,11},{10,... | collective-permute-start | bytes 1544 | tf_op jit(solution)/shard_map/ppermute | solution.py:340
  31.9 0.0 collective-permute-start.10
  31.9 0.0 collective-permute-done.12
  31.9 2.0 %collective-permute-done.11 = f32[1,128]{1,0:T(1,128)S(1)} collective-permute-done((f32[1,128]{1,0:T(1,128)S(1)}, f32[1,128]{1,0:T(1,128)S(1)}, u32[]{:S(2)}, u32[]{:S(2)}) %collective-permute-start.11) | collective-permute-done | bytes 544 | tf_op jit(solution)/shard_map/ppermute | solution.py:340
  33.9 0.9 %collective-permute-done.10 = f32[1,128]{1,0:T(1,128)S(1)} collective-permute-done((f32[1,128]{1,0:T(1,128)S(1)}, f32[1,128]{1,0:T(1,128)S(1)}, u32[]{:S(2)}, u32[]{:S(2)}) %collective-permute-start.10) | collective-permute-done | bytes 544 | tf_op jit(solution)/shard_map/ppermute | solution.py:340
  34.8 0.5 %add_add_fusion = f32[1,128]{1,0:T(1,128)} fusion(f32[1,128]{1,0:T(1,128)S(1)} %collective-permute-done.12, f32[1,128]{1,0:T(1,128)S(1)} %collective-permute-done.11, f32[1,128]{1,0:T(1,128)S(1)} %score_pair.1, f32[1,128]{1,0:T(1,128)S(1)} %collective-permute-done.10), kind=kLoop, calls=%fused_computation | loop fusion | flops 384 | bytes 2560 | tf_op jit(solution)/shard_map/add | solution.py:420
Async XLA Ops:
  0.0 23.4 %copy-start.3 = (s32[8,4]{0,1:T(4,128)S(1)}, s32[8,4]{0,1:T(4,128)}, u32[]{:S(2)}) copy-start(s32[8,4]{0,1:T(4,128)} %param.15) | copy-start | bytes 388
  0.0 22.6 %copy-start = (f32[3,3,64,128]{3,2,1,0:T(8,128)S(1)}, f32[3,3,64,128]{3,2,1,0:T(8,128)}, u32[]{:S(2)}) copy-start(f32[3,3,64,128]{3,2,1,0:T(8,128)} %param.22) | copy-start | bytes 884740
  0.0 22.6 %copy-start.1 = (f32[3,3,32,64]{3,2,1,0:T(8,128)S(1)}, f32[3,3,32,64]{3,2,1,0:T(8,128)}, u32[]{:S(2)}) copy-start(f32[3,3,32,64]{3,2,1,0:T(8,128)} %param.20) | copy-start | bytes 221188
  0.0 22.6 %copy-start.2 = (f32[3,3,1,32]{3,2,1,0:T(1,128)S(1)}, f32[3,3,1,32]{3,2,1,0:T(1,128)}, u32[]{:S(2)}) copy-start(f32[3,3,1,32]{3,2,1,0:T(1,128)} %param.18) | copy-start | bytes 3460
  0.0 23.4 %copy-start.8 = (f32[1,1,128,1]{2,3,1,0:T(1,128)S(1)}, f32[1,1,128,1]{2,3,1,0:T(1,128)}, u32[]{:S(2)}) copy-start(f32[1,1,128,1]{2,3,1,0:T(1,128)} %param.24) | copy-start | bytes 1540
  0.0 23.4 %copy-start.7 = (f32[128]{0:T(128)S(1)}, f32[128]{0:T(128)}, u32[]{:S(2)}) copy-start(f32[128]{0:T(128)} %param.23) | copy-start | bytes 1540
  0.0 23.4 %copy-start.6 = (f32[64]{0:T(128)S(1)}, f32[64]{0:T(128)}, u32[]{:S(2)}) copy-start(f32[64]{0:T(128)} %param.21) | copy-start | bytes 772
  0.0 23.4 %copy-start.5 = (f32[32]{0:T(128)S(1)}, f32[32]{0:T(128)}, u32[]{:S(2)}) copy-start(f32[32]{0:T(128)} %param.19) | copy-start | bytes 388
  0.0 23.4 %copy-start.4 = (s32[32]{0:T(128)S(1)}, s32[32]{0:T(128)}, u32[]{:S(2)}) copy-start(s32[32]{0:T(128)} %clen_ref.1) | copy-start | bytes 388
  2.1 14.0 %collective-permute-start = (bf16[2,9,16,256]{3,2,1,0:T(8,128)(2,1)S(1)}, bf16[2,9,16,256]{3,2,1,0:T(8,128)(2,1)S(1)}, u32[]{:S(2)}, u32[]{:S(2)}) collective-permute-start(bf16[2,9,16,256]{3,2,1,0:T(8,128)(2,1)S(1)} %get-tuple-element.15), channel_id=1, source_target_pairs={{0,28},{1,25},{2,30},{3,27},{4,24},{5,29},{6,26},{7,31},{8,20},{9,... | collective-permute-start | bytes 442376 | tf_op jit(solution)/shard_map/ppermute | solution.py:364
  8.2 12.5 %collective-permute-start.1 = (bf16[2,9,16,256]{3,2,1,0:T(8,128)(2,1)S(1)}, bf16[2,9,16,256]{3,2,1,0:T(8,128)(2,1)S(1)}, u32[]{:S(2)}, u32[]{:S(2)}) collective-permute-start(bf16[2,9,16,256]{3,2,1,0:T(8,128)(2,1)S(1)} %get-tuple-element.16), channel_id=1, source_target_pairs={{0,20},{1,17},{2,22},{3,19},{4,16},{5,21},{6,18},{7,23},{8,28},{9,... | collective-permute-start | bytes 442376 | tf_op jit(solution)/shard_map/ppermute | solution.py:364
  8.2 12.5 %collective-permute-start.2 = (bf16[2,9,16,256]{3,2,1,0:T(8,128)(2,1)S(1)}, bf16[2,9,16,256]{3,2,1,0:T(8,128)(2,1)S(1)}, u32[]{:S(2)}, u32[]{:S(2)}) collective-permute-start(bf16[2,9,16,256]{3,2,1,0:T(8,128)(2,1)S(1)} %get-tuple-element.17), channel_id=1, source_target_pairs={{0,12},{1,9},{2,14},{3,11},{4,8},{5,13},{6,10},{7,15},{8,4},{9,1},... | collective-permute-start | bytes 442376 | tf_op jit(solution)/shard_map/ppermute | solution.py:364
  9.9 11.3 %collective-permute-start.7 = (bf16[9,32,256]{2,1,0:T(8,128)(2,1)S(1)}, bf16[9,32,256]{2,1,0:T(8,128)(2,1)S(1)}, u32[]{:S(2)}, u32[]{:S(2)}) collective-permute-start(bf16[9,32,256]{2,1,0:T(8,128)(2,1)S(1)} %get-tuple-element.20.rest_8_), channel_id=1, source_target_pairs={{0,2},{1,3},{2,0},{3,1},{4,6},{5,7},{6,4},{7,5},{8,10},{9,11},{10,... | collective-permute-start | bytes 442376 | tf_op jit(solution)/shard_map/ppermute | solution.py:340
  11.4 4.7 %collective-permute-start.6 = (bf16[9,16,256]{2,1,0:T(8,128)(2,1)S(1)}, bf16[9,16,256]{2,1,0:T(8,128)(2,1)S(1)}, u32[]{:S(2)}, u32[]{:S(2)}) collective-permute-start(bf16[9,16,256]{2,1,0:T(8,128)(2,1)S(1)} %get-tuple-element.18), channel_id=1, source_target_pairs={{0,4},{4,0},{8,12},{12,8},{16,20},{20,16},{24,28},{28,24},{1,5},{5... | collective-permute-start | bytes 221192 | tf_op jit(solution)/shard_map/ppermute | solution.py:365
  16.1 7.2 %collective-permute-start.8 = (bf16[9,32,256]{2,1,0:T(8,128)(2,1)S(1)}, bf16[9,32,256]{2,1,0:T(8,128)(2,1)S(1)}, u32[]{:S(2)}, u32[]{:S(2)}) collective-permute-start(bf16[9,32,256]{2,1,0:T(8,128)(2,1)S(1)} %get-tuple-element.20.rest_8_), channel_id=1, source_target_pairs={{0,1},{1,0},{2,3},{3,2},{4,5},{5,4},{6,7},{7,6},{8,9},{9,8},{10,11... | collective-permute-start | bytes 442376 | tf_op jit(solution)/shard_map/ppermute | solution.py:340
  16.1 7.2 %collective-permute-start.3 = (bf16[2,9,16,256]{3,2,1,0:T(8,128)(2,1)S(1)}, bf16[2,9,16,256]{3,2,1,0:T(8,128)(2,1)S(1)}, u32[]{:S(2)}, u32[]{:S(2)}) collective-permute-start(bf16[2,9,16,256]{3,2,1,0:T(8,128)(2,1)S(1)} %collective-permute-done.rest_0_), channel_id=1, source_target_pairs={{0,1},{1,0},{2,3},{3,2},{4,5},{5,4},{6,7},{7,6},{8,9},{9,8},{10,11... | collective-permute-start | bytes 442376 | tf_op jit(solution)/shard_map/ppermute | solution.py:340
  20.7 2.7 %collective-permute-start.4 = (bf16[2,9,16,256]{3,2,1,0:T(8,128)(2,1)S(1)}, bf16[2,9,16,256]{3,2,1,0:T(8,128)(2,1)S(1)}, u32[]{:S(2)}, u32[]{:S(2)}) collective-permute-start(bf16[2,9,16,256]{3,2,1,0:T(8,128)(2,1)S(1)} %collective-permute-done.1.rest_1_), channel_id=1, source_target_pairs={{0,1},{1,0},{2,3},{3,2},{4,5},{5,4},{6,7},{7,6},{8,9},{9,8},{10,11... | collective-permute-start | bytes 442376 | tf_op jit(solution)/shard_map/ppermute | solution.py:340
  20.7 2.7 %collective-permute-start.5 = (bf16[2,9,16,256]{3,2,1,0:T(8,128)(2,1)S(1)}, bf16[2,9,16,256]{3,2,1,0:T(8,128)(2,1)S(1)}, u32[]{:S(2)}, u32[]{:S(2)}) collective-permute-start(bf16[2,9,16,256]{3,2,1,0:T(8,128)(2,1)S(1)} %collective-permute-done.2.rest_2_), channel_id=1, source_target_pairs={{0,1},{1,0},{2,3},{3,2},{4,5},{5,4},{6,7},{7,6},{8,9},{9,8},{10,11... | collective-permute-start | bytes 442376 | tf_op jit(solution)/shard_map/ppermute | solution.py:340
  21.2 2.2 %collective-permute-start.9 = (bf16[9,32,256]{2,1,0:T(8,128)(2,1)S(1)}, bf16[9,32,256]{2,1,0:T(8,128)(2,1)S(1)}, u32[]{:S(2)}, u32[]{:S(2)}) collective-permute-start(bf16[9,32,256]{2,1,0:T(8,128)(2,1)S(1)} %collective-permute-done.7.rest_9_), channel_id=1, source_target_pairs={{0,1},{1,0},{2,3},{3,2},{4,5},{5,4},{6,7},{7,6},{8,9},{9,8},{10,11... | collective-permute-start | bytes 442376 | tf_op jit(solution)/shard_map/ppermute | solution.py:340
  29.9 2.0 %collective-permute-start.12 = (f32[1,128]{1,0:T(1,128)S(1)}, f32[1,128]{1,0:T(1,128)S(1)}, u32[]{:S(2)}, u32[]{:S(2)}) collective-permute-start(f32[1,128]{1,0:T(1,128)S(1)} %score_pair.1), channel_id=1, source_target_pairs={{0,1},{1,0},{2,3},{3,2},{4,5},{5,4},{6,7},{7,6},{8,9},{9,8},{10,11... | collective-permute-start | bytes 1544 | tf_op jit(solution)/shard_map/ppermute | solution.py:340
  30.4 3.5 %collective-permute-start.11 = (f32[1,128]{1,0:T(1,128)S(1)}, f32[1,128]{1,0:T(1,128)S(1)}, u32[]{:S(2)}, u32[]{:S(2)}) collective-permute-start(f32[1,128]{1,0:T(1,128)S(1)} %score_pair.1), channel_id=1, source_target_pairs={{0,2},{1,3},{2,0},{3,1},{4,6},{5,7},{6,4},{7,5},{8,10},{9,11},{10,... | collective-permute-start | bytes 1544 | tf_op jit(solution)/shard_map/ppermute | solution.py:340
  31.9 3.0 %collective-permute-start.10 = (f32[1,128]{1,0:T(1,128)S(1)}, f32[1,128]{1,0:T(1,128)S(1)}, u32[]{:S(2)}, u32[]{:S(2)}) collective-permute-start(f32[1,128]{1,0:T(1,128)S(1)} %score_pair.1), channel_id=1, source_target_pairs={{0,3},{1,2},{2,1},{3,0},{4,7},{5,6},{6,5},{7,4},{8,11},{9,10},{10,... | collective-permute-start | bytes 1544 | tf_op jit(solution)/shard_map/ppermute | solution.py:340

commit v4 on v3

--- a/solution.py
+++ b/solution.py
@@ -54,7 +54,9 @@
         copy.wait()
 
 
-def weight_kernel(one_ref, two_ref, three_ref, w1_ref, w2_ref, w3a_ref, w3b_ref):
+def weight_kernel(one_ref, two_ref, three_ref, qlen_ref, b4_ref, w1_ref, w2_ref, w3a_ref, w3b_ref, qlen_out, b4_out):
+    qlen_out[...] = jnp.full(qlen_out.shape, qlen_ref[0], jnp.int32)
+    b4_out[...] = jnp.full(b4_out.shape, b4_ref[0], F32)
     row = lax.broadcasted_iota(jnp.int32, (LANES, 256), 0)
     lane = lax.broadcasted_iota(jnp.int32, (LANES, 256), 1)
 
@@ -76,10 +78,9 @@
             mask = (slot < 6) & (slot % 3 == d) & (row % 16 - column == t)
             total = jnp.where(mask, wide(one_ref[3 * d + t], 8), total)
     high, middle, low = split_three(total)
-    both = jnp.where(slot < 3, high.astype(F32), middle.astype(F32)).astype(BF16)
-    w1_ref[0:LANES, :] = both
-    w1_ref[LANES : 2 * LANES, :] = both
-    w1_ref[2 * LANES : 3 * LANES, :] = jnp.where(slot < 3, low.astype(F32), 0.0).astype(BF16)
+    for at, part in enumerate((middle, low)):
+        both = jnp.where(slot < 3, high.astype(F32), part.astype(F32)).astype(BF16)
+        w1_ref[at * LANES : (at + 1) * LANES, :] = both
 
     def place(ref, base, starts, value):
         for start, part in zip(starts, split_three(value)):
@@ -133,9 +134,12 @@
     clen_ref,
     *rest,
 ):
-    blocks = rest[:n_blocks]
     n_slabs = len(order)
-    slabs = rest[n_blocks : n_blocks + n_slabs]
+    slabs, rest = rest[:n_slabs], rest[n_slabs:]
+    blocks, rest = rest[:n_blocks], rest[n_blocks:]
+    late = ()
+    if n_blocks > 1:
+        late, rest = rest[9:11], rest[:9] + rest[11:]
     (
         w1_ref,
         w2_ref,
@@ -155,24 +159,23 @@
         x2,
         x3,
         pooled_two,
-    ) = rest[n_blocks + n_slabs :]
+    ) = rest
     query = lax.axis_index("pb")
     pair = lax.axis_index("slab")
     odd = lax.rem(pair, 2)
     feature_width = feats.shape[-1]
-    query_len = qlen_ref[0]
+    query_len = qlen_ref[...]
     clip_len = clen_ref[cand_ref[pair, query]]
 
     if n_blocks == 1:
         clip[...] = blocks[0][...]
     else:
-        steps = len(rounds[0])
-        band = blocks[-1].shape[1]
-        pieces = [(0, blocks[-1][...]), (1, blocks[-2][...])]
-        for at in range(steps):
-            first, second = rounds[0][at], rounds[1][at]
-            pieces.append((jnp.where(odd == 0, first, second), blocks[at][0]))
-            pieces.append((jnp.where(odd == 0, second, first), blocks[steps + at][1]))
+        first, third, first_passed, third_passed, one_away, own = blocks
+        band = own.shape[1]
+        pieces = [(0, own[...]), (1, one_away[...])]
+        for at, (direct, passed) in enumerate(((first, first_passed), late, (third, third_passed))):
+            for value, k, other in ((direct[0], 0, 1), (passed[1], 1, 0)):
+                pieces.append((jnp.where(odd == 0, rounds[k][at], rounds[other][at]), value))
         for k, value in pieces:
             clip[:, pl.ds(pl.multiple_of((query ^ k) * band, band), band), :] = value
     for k, slab in zip(order, slabs):
@@ -210,10 +213,11 @@
             field = jnp.where(lane % 16 == 0, 0.0, field)
         if n == windows - 1:
             field = jnp.where(lane % 16 == 9, 0.0, field)
-        high, low = split(field)
+        high = field.astype(BF16)
+        low = jnp.where(lane < 48, field - high.astype(F32), field).astype(BF16)
         x1[n * frames : (n + 1) * frames, 0:LANES] = high
         x1[n * frames : (n + 1) * frames, LANES : 2 * LANES] = low
-    made = dot(x1[...], w1_ref[0:256, :]) + dot(x1[:, 0:LANES], w1_ref[256:384, :])
+    made = dot(x1[...], w1_ref[...])
     made = jnp.maximum(made[:, :LANES], made[:, LANES:])
     bias_one = jnp.concatenate([b1_ref[...]] * 4, axis=1)
     bias_two = jnp.concatenate([b2_ref[...]] * 2, axis=1)
@@ -281,8 +285,8 @@
             high, low = split(value)
             x3[base : base + quarter, d * LANES : (d + 1) * LANES] = high
             x3[base : base + quarter, (3 + d) * LANES : (4 + d) * LANES] = low
-    bias_four = b4_ref[0]
-    row_best = jnp.full((quarter, 1), -2.0, F32)
+    bias_four = b4_ref[...]
+    row_best = jnp.full((quarter, LANES), -2.0, F32)
     group = 4
     for n in range(0, windows, group):
         made = jnp.zeros((group * quarter, 256), F32)
@@ -300,10 +304,9 @@
             for i in range(group):
                 keep = 4 * (2 * (n + i) + c) < clip_len
                 row_best = jnp.maximum(row_best, jnp.where(keep, final[i * quarter : (i + 1) * quarter], -2.0))
-    row = lax.broadcasted_iota(jnp.int32, (quarter, 1), 0)
+    row = lax.broadcasted_iota(jnp.int32, (quarter, LANES), 0)
     kept = jnp.where(4 * row < query_len, row_best, 0.0)
-    number = jnp.broadcast_to(((query_len + 3) // 4).astype(F32), (1, 1))
-    score = jnp.sum(kept, axis=0, keepdims=True) / number
+    score = jnp.sum(kept, axis=0, keepdims=True) / ((query_len + 3) // 4).astype(F32)
     lane = lax.broadcasted_iota(jnp.int32, out_ref.shape, 1)
     out_ref[...] = jnp.where(lane == pair, score, 0.0)
 
@@ -357,39 +360,54 @@
             compiler_params=pltpu.CompilerParams(vmem_limit_bytes=2 * 1024 * 1024),
             name="pick_bands",
         )(*[pltpu.with_memory_space_constraint(x, pltpu.HBM) for x in (candidates.T, store, own)])
+        def cross(at):
+            moves = [(q * n_slab + s, (q ^ rounds[s % 2][at]) * n_slab + s) for q in range(n_query) for s in range(n_slab)]
+            return lax.ppermute(sent[at], ("pb", "slab"), moves)
+
+        first, third = cross(0), cross(2)
         own = sent[steps + 2]
-        near = []
-        for at in range(steps):
-            moves = [(q * n_slab + s, (q ^ rounds[s % 2][at]) * n_slab + s) for q in range(n_query) for s in range(n_slab)]
-            near.append(lax.ppermute(sent[at], ("pb", "slab"), moves))
-        one_away = lax.ppermute(sent[steps], "pb", [(q, q ^ 1) for q in range(n_query)])
-        blocks = [*near, *[swap(x, 1) for x in near], one_away, sent[steps + 1]]
     else:
         ids = lax.dynamic_index_in_dim(candidates, lax.axis_index("slab"), 1, keepdims=False)
         got = lax.all_to_all(store[ids], "pb", 0, 0, tiled=True)
         blocks = [jnp.transpose(got, (1, 0, 2, 3)).reshape(regions, frames, feature_width)]
     slabs = [own]
-    steps = [1 << i for i in range(n_slab.bit_length() - 1)]
-    for k in reversed(steps):
+    hops = [1 << i for i in range(n_slab.bit_length() - 1)]
+    for k in reversed(hops):
         slabs = slabs + [swap(x, k) for x in slabs]
     order = [0]
-    for k in reversed(steps):
+    for k in reversed(hops):
         order = order + [o ^ k for o in order]
+    if rounds is not None:
+        one_away = lax.ppermute(sent[steps], "pb", [(q, q ^ 1) for q in range(n_query)])
+        blocks = [first, third, swap(first, 1), swap(third, 1), one_away, sent[steps + 1]]
 
     weights = pl.pallas_call(
         weight_kernel,
-        out_shape=[jax.ShapeDtypeStruct((rows, 256), BF16) for rows in (384, 2560, 1920, 1920)],
-        in_specs=[vmem] * 3,
-        out_specs=[vmem] * 4,
-        compiler_params=pltpu.CompilerParams(vmem_limit_bytes=4 * 1024 * 1024),
+        out_shape=[jax.ShapeDtypeStruct((rows, 256), BF16) for rows in (256, 2560, 1920, 1920)]
+        + [jax.ShapeDtypeStruct((1, LANES), t) for t in (jnp.int32, F32)],
+        in_specs=[vmem] * 3 + [smem] * 2,
+        out_specs=[vmem] * 6,
+        compiler_params=pltpu.CompilerParams(vmem_limit_bytes=10 * 1024 * 1024),
         cost_estimate=pl.CostEstimate(flops=2_000_000, bytes_accessed=6_000_000, transcendentals=0),
         name="lay_out_kernels",
-    )(kernel_one.reshape(9, 1, -1), kernel_two.reshape(9, 32, 64), kernel_three.reshape(9, 64, 128))
+    )(
+        kernel_one.reshape(9, 1, -1),
+        kernel_two.reshape(9, 32, 64),
+        kernel_three.reshape(9, 64, 128),
+        query_length,
+        bias_four,
+    )
+    *weights, query_len, last_bias = weights
+    late = []
+    if rounds is not None:
+        second = cross(1)
+        second, weights[0] = lax.optimization_barrier((second, weights[0]))
+        late = [second, swap(second, 1)]
 
     vector = pl.pallas_call(
         functools.partial(score_kernel, rounds, len(blocks), order, regions, frames),
         out_shape=jax.ShapeDtypeStruct((1, LANES), F32),
-        in_specs=[smem] * 3 + [vmem] * (len(blocks) + n_slab + 8) + [smem],
+        in_specs=[smem, vmem, smem] + [vmem] * (len(blocks) + len(late) + n_slab + 9),
         out_specs=vmem,
         scratch_shapes=[
             pltpu.VMEM((regions, frames, feature_width), BF16),
@@ -406,16 +424,17 @@
         name="score_pair",
     )(
         candidates.T,
-        query_length,
+        query_len,
         clip_length,
+        *slabs,
         *blocks,
-        *slabs,
         *weights,
         bias_one[None],
         bias_two[None],
         bias_three[None],
         kernel_four.reshape(1, -1),
-        bias_four,
+        last_bias,
+        *late,
     )
     vector = sum([swap(vector, k) for k in reversed(range(1, n_slab))], vector)
     return vector[:, :pair_count]

time: 35.5 us -> 32.7 us (0.921)
  the two profiles are of different devices: /device:TPU:0 before, /device:TPU:17 now
where the time goes in v4:
time: 32.7 us; the launch traced here: 32.5 us
  starting transfers between devices  13.9 us (43%)
  Pallas kernels  8.58 us (26%)
  waiting for transfers between devices  8.08 us (25%)
  between operations  1.45 us (4%)
  other arithmetic  0.52 us (2%)
    ppermute x9, starting transfers between devices, swap(): return lax.ppermute(x, 'slab', [(s, s ^ k) for s in range(n_slab)])  9.03 us
    pallas_call x1, Pallas kernels, per_device(): pl.pallas_call(functools.partial(score_kernel, rounds, len(blocks), order...  5.79 us
    ppermute x3, waiting for transfers between devices, cross(): return lax.ppermute(sent[at], ('pb', 'slab'), moves)  4.54 us
    ppermute x3, starting transfers between devices, cross(): return lax.ppermute(sent[at], ('pb', 'slab'), moves)  3.61 us
    ppermute x9, waiting for transfers between devices, swap(): return lax.ppermute(x, 'slab', [(s, s ^ k) for s in range(n_slab)])  3.54 us
    pallas_call x1, Pallas kernels, per_device(): pl.pallas_call(functools.partial(pick_kernel, rounds), out_shape=[jax.Sha...  2.06 us
    ppermute x1, starting transfers between devices, per_device(): lax.ppermute(sent[steps], 'pb', [(q, q ^ 1) for q in range(n_query)])  1.24 us
    pallas_call x1, Pallas kernels, per_device(): pl.pallas_call(weight_kernel, out_shape=[jax.ShapeDtypeStruct((rows, 256)...  0.73 us
  transfers between devices with their start and end apart: 13, of which 7 were waited for; matrix products, arithmetic and copies ran while one was open for 0% of the time, Pallas kernels for 2%

profile of v4, /device:TPU:17, one launch (start us, length us, event | category | flops | bytes accessed | tf_op | source)
XLA Modules:
  0.0 32.5 jit_solution(17914810006006527903)
XLA Ops:
  0.0 0.0 copy-start.3
  0.0 0.0 copy-start
  0.0 0.0 copy-start.1
  0.0 0.0 copy-start.2
  0.0 0.0 copy-start.8
  0.0 0.0 copy-start.7
  0.0 0.0 copy-start.6
  0.0 0.0 copy-start.5
  0.1 0.0 copy-start.4
  0.1 2.1 %pick_bands.1 = (bf16[2,9,16,256]{3,2,1,0:T(8,128)(2,1)S(1)}, bf16[2,9,16,256]{3,2,1,0:T(8,128)(2,1)S(1)}, bf16[2,9,16,256]{3,2,1,0:T(8,128)(2,1)S(1)}, bf16[9,1...) custom-call(s32[4,8]{1,0:T(4,128)} %bitcast.16, ...), custom_call_target="tpu_custom_call" | custom-call | tf_op jit(solution)/shard_map/pick_bands/pallas_call | solution.py:349
  2.1 0.1 collective-permute-start.8
  2.2 2.5 %collective-permute-start.3 = (bf16[2,9,16,256]{3,2,1,0:T(8,128)(2,1)S(1)}, bf16[2,9,16,256]{3,2,1,0:T(8,128)(2,1)S(1)}, u32[]{:S(2)}, u32[]{:S(2)}) collective-permute-start(bf16[2,9,16,256]{3,2,1,0:T(8,128)(2,1)S(1)} %get-tuple-element.21), channel_id=1, source_target_pairs={{0,28},{1,25},{2,30},{3,27},{4,24},{5,29},{6,26},{7,31},{8,20},{9,... | collective-permute-start | bytes 442376 | tf_op jit(solution)/shard_map/ppermute | solution.py:365
  4.7 1.1 %collective-permute-start.4 = (bf16[2,9,16,256]{3,2,1,0:T(8,128)(2,1)S(1)}, bf16[2,9,16,256]{3,2,1,0:T(8,128)(2,1)S(1)}, u32[]{:S(2)}, u32[]{:S(2)}) collective-permute-start(bf16[2,9,16,256]{3,2,1,0:T(8,128)(2,1)S(1)} %get-tuple-element.22), channel_id=1, source_target_pairs={{0,12},{1,9},{2,14},{3,11},{4,8},{5,13},{6,10},{7,15},{8,4},{9,1},... | collective-permute-start | bytes 442376 | tf_op jit(solution)/shard_map/ppermute | solution.py:365
  5.7 1.2 %collective-permute-start = (bf16[9,32,256]{2,1,0:T(8,128)(2,1)S(1)}, bf16[9,32,256]{2,1,0:T(8,128)(2,1)S(1)}, u32[]{:S(2)}, u32[]{:S(2)}) collective-permute-start(bf16[9,32,256]{2,1,0:T(8,128)(2,1)S(1)} %get-tuple-element.20.rest_0_), channel_id=1, source_target_pairs={{0,2},{1,3},{2,0},{3,1},{4,6},{5,7},{6,4},{7,5},{8,10},{9,11},{10,... | collective-permute-start | bytes 442376 | tf_op jit(solution)/shard_map/ppermute | solution.py:343
  7.0 1.2 %collective-permute-start.7 = (bf16[9,16,256]{2,1,0:T(8,128)(2,1)S(1)}, bf16[9,16,256]{2,1,0:T(8,128)(2,1)S(1)}, u32[]{:S(2)}, u32[]{:S(2)}) collective-permute-start(bf16[9,16,256]{2,1,0:T(8,128)(2,1)S(1)} %get-tuple-element.23), channel_id=1, source_target_pairs={{0,4},{4,0},{8,12},{12,8},{16,20},{20,16},{24,28},{28,24},{1,5},{5... | collective-permute-start | bytes 221192 | tf_op jit(solution)/shard_map/ppermute | solution.py:381
  9.5 0.0 copy-done
  9.5 0.0 copy-done.1
  9.5 0.0 copy-done.2
  9.5 0.7 %lay_out_kernels.1 = (bf16[256,256]{1,0:T(8,128)(2,1)S(1)}, bf16[2560,256]{1,0:T(8,128)(2,1)S(1)}, bf16[1920,256]{1,0:T(8,128)(2,1)S(1)}, bf16[1920,256]{1,0:T(8...) custom-call(f32[9,1,32]{2,1,0:T(1,128)S(1)} %bitcast.15, f32[9,32,64]{2,1,0:T(8,128)S(1)} %bitcast.14, ...), custom_call_target="tpu_custom_call" | custom-call | flops 2000000 | bytes 6000000 | tf_op jit(solution)/shard_map/lay_out_kernels/pallas_call | solution.py:384
  10.3 0.0 collective-permute-done.8.rest_19_
  10.3 3.5 %collective-permute-start.1 = (bf16[9,32,256]{2,1,0:T(8,128)(2,1)S(1)}, bf16[9,32,256]{2,1,0:T(8,128)(2,1)S(1)}, u32[]{:S(2)}, u32[]{:S(2)}) collective-permute-start(bf16[9,32,256]{2,1,0:T(8,128)(2,1)S(1)} %get-tuple-element.20.rest_0_), channel_id=1, source_target_pairs={{0,1},{1,0},{2,3},{3,2},{4,5},{5,4},{6,7},{7,6},{8,9},{9,8},{10,11... | collective-permute-start | bytes 442376 | tf_op jit(solution)/shard_map/ppermute | solution.py:343
  13.8 4.5 %collective-permute-done.3.rest_4_ = bf16[2,9,16,256]{3,2,1,0:T(8,128)(2,1)S(1)} collective-permute-done((bf16[2,9,16,256]{3,2,1,0:T(8,128)(2,1)S(1)}, bf16[2,9,16,256]{3,2,1,0:T(8,128)(2,1)S(1)}, u32[]{:S(2)}, u32[]{:S(2)}) %collective-permute-start.3) | collective-permute-done | bytes 147488 | tf_op jit(solution)/shard_map/ppermute | solution.py:365
  18.4 1.5 %collective-permute-start.5 = (bf16[2,9,16,256]{3,2,1,0:T(8,128)(2,1)S(1)}, bf16[2,9,16,256]{3,2,1,0:T(8,128)(2,1)S(1)}, u32[]{:S(2)}, u32[]{:S(2)}) collective-permute-start(bf16[2,9,16,256]{3,2,1,0:T(8,128)(2,1)S(1)} %collective-permute-done.3.rest_4_), channel_id=1, source_target_pairs={{0,1},{1,0},{2,3},{3,2},{4,5},{5,4},{6,7},{7,6},{8,9},{9,8},{10,11... | collective-permute-start | bytes 442376 | tf_op jit(solution)/shard_map/ppermute | solution.py:343
  19.8 0.0 collective-permute-done.4.rest_5_
  19.9 0.0 collective-permute-start.6
  19.9 0.0 collective-permute-done.rest_1_
  19.9 0.5 %collective-permute-start.2 = (bf16[9,32,256]{2,1,0:T(8,128)(2,1)S(1)}, bf16[9,32,256]{2,1,0:T(8,128)(2,1)S(1)}, u32[]{:S(2)}, u32[]{:S(2)}) collective-permute-start(bf16[9,32,256]{2,1,0:T(8,128)(2,1)S(1)} %collective-permute-done.rest_1_), channel_id=1, source_target_pairs={{0,1},{1,0},{2,3},{3,2},{4,5},{5,4},{6,7},{7,6},{8,9},{9,8},{10,11... | collective-permute-start | bytes 442376 | tf_op jit(solution)/shard_map/ppermute | solution.py:343
  20.4 0.0 collective-permute-done.7.rest_8_
  20.4 0.1 collective-permute-start.9
  20.4 0.0 collective-permute-done.1.rest_2_
  20.4 0.4 %collective-permute-done.5.rest_6_ = bf16[2,9,16,256]{3,2,1,0:T(8,128)(2,1)S(1)} collective-permute-done((bf16[2,9,16,256]{3,2,1,0:T(8,128)(2,1)S(1)}, bf16[2,9,16,256]{3,2,1,0:T(8,128)(2,1)S(1)}, u32[]{:S(2)}, u32[]{:S(2)}) %collective-permute-start.5) | collective-permute-done | bytes 147488 | tf_op jit(solution)/shard_map/ppermute | solution.py:343
  20.9 0.4 %collective-permute-done.6.rest_7_ = bf16[2,9,16,256]{3,2,1,0:T(8,128)(2,1)S(1)} collective-permute-done((bf16[2,9,16,256]{3,2,1,0:T(8,128)(2,1)S(1)}, bf16[2,9,16,256]{3,2,1,0:T(8,128)(2,1)S(1)}, u32[]{:S(2)}, u32[]{:S(2)}) %collective-permute-start.6) | collective-permute-done | bytes 147488 | tf_op jit(solution)/shard_map/ppermute | solution.py:343
  21.2 0.2 collective-permute-done.2.rest_3_
  21.4 0.3 collective-permute-done.9.rest_20_
  21.7 0.0 copy-done.3
  21.7 0.0 copy-done.8
  21.7 0.0 copy-done.7
  21.8 0.0 copy-done.6
  21.8 0.0 copy-done.5
  21.8 0.0 copy-done.4
  21.8 5.8 %score_pair.1 = f32[1,128]{1,0:T(1,128)S(1)} custom-call(s32[4,8]{1,0:T(4,128)S(1)} %bitcast.17, s32[1,128]{1,0:T(1,128)S(1)} %get-tuple-element.19.qlen_ref, s32[32]{0:T(128)S(1)} %copy-done.4, bf16[9,32,256]{2,1,0:T(8,128)(2,1)S(1)} %get-tuple-element.20.rest_0_, bf16[9,32,256]{2,1,0:T(8,128)(2,1)S(1)} %collective-permute-done.rest_1_, ...), custom_call_target="tpu_custom_call" | custom-call | flops 2000000000 | bytes 8000000 | tf_op jit(solution)/shard_map/score_pair/pallas_call | solution.py:407
  27.6 0.3 collective-permute-start.12
  27.8 1.2 %collective-permute-start.11 = (f32[1,128]{1,0:T(1,128)S(1)}, f32[1,128]{1,0:T(1,128)S(1)}, u32[]{:S(2)}, u32[]{:S(2)}) collective-permute-start(f32[1,128]{1,0:T(1,128)S(1)} %score_pair.1), channel_id=1, source_target_pairs={{0,2},{1,3},{2,0},{3,1},{4,6},{5,7},{6,4},{7,5},{8,10},{9,11},{10,... | collective-permute-start | bytes 1544 | tf_op jit(solution)/shard_map/ppermute | solution.py:343
  29.1 0.7 %collective-permute-start.10 = (f32[1,128]{1,0:T(1,128)S(1)}, f32[1,128]{1,0:T(1,128)S(1)}, u32[]{:S(2)}, u32[]{:S(2)}) collective-permute-start(f32[1,128]{1,0:T(1,128)S(1)} %score_pair.1), channel_id=1, source_target_pairs={{0,3},{1,2},{2,1},{3,0},{4,7},{5,6},{6,5},{7,4},{8,11},{9,10},{10,... | collective-permute-start | bytes 1544 | tf_op jit(solution)/shard_map/ppermute | solution.py:343
  29.8 0.0 collective-permute-done.12
  29.8 0.5 %collective-permute-done.11 = f32[1,128]{1,0:T(1,128)S(1)} collective-permute-done((f32[1,128]{1,0:T(1,128)S(1)}, f32[1,128]{1,0:T(1,128)S(1)}, u32[]{:S(2)}, u32[]{:S(2)}) %collective-permute-start.11) | collective-permute-done | bytes 544 | tf_op jit(solution)/shard_map/ppermute | solution.py:343
  30.2 1.8 %collective-permute-done.10 = f32[1,128]{1,0:T(1,128)S(1)} collective-permute-done((f32[1,128]{1,0:T(1,128)S(1)}, f32[1,128]{1,0:T(1,128)S(1)}, u32[]{:S(2)}, u32[]{:S(2)}) %collective-permute-start.10) | collective-permute-done | bytes 544 | tf_op jit(solution)/shard_map/ppermute | solution.py:343
  32.0 0.5 %add_add_fusion = f32[1,128]{1,0:T(1,128)} fusion(f32[1,128]{1,0:T(1,128)S(1)} %collective-permute-done.12, f32[1,128]{1,0:T(1,128)S(1)} %collective-permute-done.11, f32[1,128]{1,0:T(1,128)S(1)} %score_pair.1, f32[1,128]{1,0:T(1,128)S(1)} %collective-permute-done.10), kind=kLoop, calls=%fused_computation | loop fusion | flops 384 | bytes 2560 | tf_op jit(solution)/shard_map/add | solution.py:439
Async XLA Ops:
  0.0 21.7 %copy-start.3 = (s32[8,4]{0,1:T(4,128)S(1)}, s32[8,4]{0,1:T(4,128)}, u32[]{:S(2)}) copy-start(s32[8,4]{0,1:T(4,128)} %param.15) | copy-start | bytes 388
  0.0 9.5 %copy-start = (f32[3,3,64,128]{3,2,1,0:T(8,128)S(1)}, f32[3,3,64,128]{3,2,1,0:T(8,128)}, u32[]{:S(2)}) copy-start(f32[3,3,64,128]{3,2,1,0:T(8,128)} %param.22) | copy-start | bytes 884740
  0.0 9.5 %copy-start.1 = (f32[3,3,32,64]{3,2,1,0:T(8,128)S(1)}, f32[3,3,32,64]{3,2,1,0:T(8,128)}, u32[]{:S(2)}) copy-start(f32[3,3,32,64]{3,2,1,0:T(8,128)} %param.20) | copy-start | bytes 221188
  0.0 9.5 %copy-start.2 = (f32[3,3,1,32]{3,2,1,0:T(1,128)S(1)}, f32[3,3,1,32]{3,2,1,0:T(1,128)}, u32[]{:S(2)}) copy-start(f32[3,3,1,32]{3,2,1,0:T(1,128)} %param.18) | copy-start | bytes 3460
  0.0 21.7 %copy-start.8 = (f32[1,1,128,1]{2,3,1,0:T(1,128)S(1)}, f32[1,1,128,1]{2,3,1,0:T(1,128)}, u32[]{:S(2)}) copy-start(f32[1,1,128,1]{2,3,1,0:T(1,128)} %param.24) | copy-start | bytes 1540
  0.0 21.7 %copy-start.7 = (f32[128]{0:T(128)S(1)}, f32[128]{0:T(128)}, u32[]{:S(2)}) copy-start(f32[128]{0:T(128)} %param.23) | copy-start | bytes 1540
  0.0 21.7 %copy-start.6 = (f32[64]{0:T(128)S(1)}, f32[64]{0:T(128)}, u32[]{:S(2)}) copy-start(f32[64]{0:T(128)} %param.21) | copy-start | bytes 772
  0.0 21.7 %copy-start.5 = (f32[32]{0:T(128)S(1)}, f32[32]{0:T(128)}, u32[]{:S(2)}) copy-start(f32[32]{0:T(128)} %param.19) | copy-start | bytes 388
  0.1 21.7 %copy-start.4 = (s32[32]{0:T(128)S(1)}, s32[32]{0:T(128)}, u32[]{:S(2)}) copy-start(s32[32]{0:T(128)} %clen_ref.1) | copy-start | bytes 388
  2.1 8.1 %collective-permute-start.8 = (bf16[2,9,16,256]{3,2,1,0:T(8,128)(2,1)S(1)}, bf16[2,9,16,256]{3,2,1,0:T(8,128)(2,1)S(1)}, u32[]{:S(2)}, u32[]{:S(2)}) collective-permute-start(bf16[2,9,16,256]{3,2,1,0:T(8,128)(2,1)S(1)} %get-tuple-element.25), channel_id=1, source_target_pairs={{0,20},{1,17},{2,22},{3,19},{4,16},{5,21},{6,18},{7,23},{8,28},{9,... | collective-permute-start | bytes 442376 | tf_op jit(solution)/shard_map/ppermute | solution.py:365
  2.2 16.1 %collective-permute-start.3 = (bf16[2,9,16,256]{3,2,1,0:T(8,128)(2,1)S(1)}, bf16[2,9,16,256]{3,2,1,0:T(8,128)(2,1)S(1)}, u32[]{:S(2)}, u32[]{:S(2)}) collective-permute-start(bf16[2,9,16,256]{3,2,1,0:T(8,128)(2,1)S(1)} %get-tuple-element.21), channel_id=1, source_target_pairs={{0,28},{1,25},{2,30},{3,27},{4,24},{5,29},{6,26},{7,31},{8,20},{9,... | collective-permute-start | bytes 442376 | tf_op jit(solution)/shard_map/ppermute | solution.py:365
  4.7 15.2 %collective-permute-start.4 = (bf16[2,9,16,256]{3,2,1,0:T(8,128)(2,1)S(1)}, bf16[2,9,16,256]{3,2,1,0:T(8,128)(2,1)S(1)}, u32[]{:S(2)}, u32[]{:S(2)}) collective-permute-start(bf16[2,9,16,256]{3,2,1,0:T(8,128)(2,1)S(1)} %get-tuple-element.22), channel_id=1, source_target_pairs={{0,12},{1,9},{2,14},{3,11},{4,8},{5,13},{6,10},{7,15},{8,4},{9,1},... | collective-permute-start | bytes 442376 | tf_op jit(solution)/shard_map/ppermute | solution.py:365
  5.7 14.1 %collective-permute-start = (bf16[9,32,256]{2,1,0:T(8,128)(2,1)S(1)}, bf16[9,32,256]{2,1,0:T(8,128)(2,1)S(1)}, u32[]{:S(2)}, u32[]{:S(2)}) collective-permute-start(bf16[9,32,256]{2,1,0:T(8,128)(2,1)S(1)} %get-tuple-element.20.rest_0_), channel_id=1, source_target_pairs={{0,2},{1,3},{2,0},{3,1},{4,6},{5,7},{6,4},{7,5},{8,10},{9,11},{10,... | collective-permute-start | bytes 442376 | tf_op jit(solution)/shard_map/ppermute | solution.py:343
  7.0 13.4 %collective-permute-start.7 = (bf16[9,16,256]{2,1,0:T(8,128)(2,1)S(1)}, bf16[9,16,256]{2,1,0:T(8,128)(2,1)S(1)}, u32[]{:S(2)}, u32[]{:S(2)}) collective-permute-start(bf16[9,16,256]{2,1,0:T(8,128)(2,1)S(1)} %get-tuple-element.23), channel_id=1, source_target_pairs={{0,4},{4,0},{8,12},{12,8},{16,20},{20,16},{24,28},{28,24},{1,5},{5... | collective-permute-start | bytes 221192 | tf_op jit(solution)/shard_map/ppermute | solution.py:381
  10.3 10.2 %collective-permute-start.1 = (bf16[9,32,256]{2,1,0:T(8,128)(2,1)S(1)}, bf16[9,32,256]{2,1,0:T(8,128)(2,1)S(1)}, u32[]{:S(2)}, u32[]{:S(2)}) collective-permute-start(bf16[9,32,256]{2,1,0:T(8,128)(2,1)S(1)} %get-tuple-element.20.rest_0_), channel_id=1, source_target_pairs={{0,1},{1,0},{2,3},{3,2},{4,5},{5,4},{6,7},{7,6},{8,9},{9,8},{10,11... | collective-permute-start | bytes 442376 | tf_op jit(solution)/shard_map/ppermute | solution.py:343
  18.4 2.5 %collective-permute-start.5 = (bf16[2,9,16,256]{3,2,1,0:T(8,128)(2,1)S(1)}, bf16[2,9,16,256]{3,2,1,0:T(8,128)(2,1)S(1)}, u32[]{:S(2)}, u32[]{:S(2)}) collective-permute-start(bf16[2,9,16,256]{3,2,1,0:T(8,128)(2,1)S(1)} %collective-permute-done.3.rest_4_), channel_id=1, source_target_pairs={{0,1},{1,0},{2,3},{3,2},{4,5},{5,4},{6,7},{7,6},{8,9},{9,8},{10,11... | collective-permute-start | bytes 442376 | tf_op jit(solution)/shard_map/ppermute | solution.py:343
  19.9 1.4 %collective-permute-start.6 = (bf16[2,9,16,256]{3,2,1,0:T(8,128)(2,1)S(1)}, bf16[2,9,16,256]{3,2,1,0:T(8,128)(2,1)S(1)}, u32[]{:S(2)}, u32[]{:S(2)}) collective-permute-start(bf16[2,9,16,256]{3,2,1,0:T(8,128)(2,1)S(1)} %collective-permute-done.4.rest_5_), channel_id=1, source_target_pairs={{0,1},{1,0},{2,3},{3,2},{4,5},{5,4},{6,7},{7,6},{8,9},{9,8},{10,11... | collective-permute-start | bytes 442376 | tf_op jit(solution)/shard_map/ppermute | solution.py:343
  19.9 1.6 %collective-permute-start.2 = (bf16[9,32,256]{2,1,0:T(8,128)(2,1)S(1)}, bf16[9,32,256]{2,1,0:T(8,128)(2,1)S(1)}, u32[]{:S(2)}, u32[]{:S(2)}) collective-permute-start(bf16[9,32,256]{2,1,0:T(8,128)(2,1)S(1)} %collective-permute-done.rest_1_), channel_id=1, source_target_pairs={{0,1},{1,0},{2,3},{3,2},{4,5},{5,4},{6,7},{7,6},{8,9},{9,8},{10,11... | collective-permute-start | bytes 442376 | tf_op jit(solution)/shard_map/ppermute | solution.py:343
  20.4 1.4 %collective-permute-start.9 = (bf16[2,9,16,256]{3,2,1,0:T(8,128)(2,1)S(1)}, bf16[2,9,16,256]{3,2,1,0:T(8,128)(2,1)S(1)}, u32[]{:S(2)}, u32[]{:S(2)}) collective-permute-start(bf16[2,9,16,256]{3,2,1,0:T(8,128)(2,1)S(1)} %collective-permute-done.8.rest_19_), channel_id=1, source_target_pairs={{0,1},{1,0},{2,3},{3,2},{4,5},{5,4},{6,7},{7,6},{8,9},{9,8},{10,11... | collective-permute-start | bytes 442376 | tf_op jit(solution)/shard_map/ppermute | solution.py:343
  27.6 2.2 %collective-permute-start.12 = (f32[1,128]{1,0:T(1,128)S(1)}, f32[1,128]{1,0:T(1,128)S(1)}, u32[]{:S(2)}, u32[]{:S(2)}) collective-permute-start(f32[1,128]{1,0:T(1,128)S(1)} %score_pair.1), channel_id=1, source_target_pairs={{0,1},{1,0},{2,3},{3,2},{4,5},{5,4},{6,7},{7,6},{8,9},{9,8},{10,11... | collective-permute-start | bytes 1544 | tf_op jit(solution)/shard_map/ppermute | solution.py:343
  27.8 2.4 %collective-permute-start.11 = (f32[1,128]{1,0:T(1,128)S(1)}, f32[1,128]{1,0:T(1,128)S(1)}, u32[]{:S(2)}, u32[]{:S(2)}) collective-permute-start(f32[1,128]{1,0:T(1,128)S(1)} %score_pair.1), channel_id=1, source_target_pairs={{0,2},{1,3},{2,0},{3,1},{4,6},{5,7},{6,4},{7,5},{8,10},{9,11},{10,... | collective-permute-start | bytes 1544 | tf_op jit(solution)/shard_map/ppermute | solution.py:343
  29.1 3.0 %collective-permute-start.10 = (f32[1,128]{1,0:T(1,128)S(1)}, f32[1,128]{1,0:T(1,128)S(1)}, u32[]{:S(2)}, u32[]{:S(2)}) collective-permute-start(f32[1,128]{1,0:T(1,128)S(1)} %score_pair.1), channel_id=1, source_target_pairs={{0,3},{1,2},{2,1},{3,0},{4,7},{5,6},{6,5},{7,4},{8,11},{9,10},{10,... | collective-permute-start | bytes 1544 | tf_op jit(solution)/shard_map/ppermute | solution.py:343

commit v5 on v4

--- a/solution.py
+++ b/solution.py
@@ -13,7 +13,8 @@
 
 
 def exchange_rounds(count):
-    return list(range(count - 1, 1, -2)), list(range(count - 2, 1, -2))
+    odd, even = list(range(count - 1, 1, -2)), list(range(count - 2, 1, -2))
+    return odd, [even[1], even[0], *even[2:]]
 
 
 def split(x):
@@ -54,7 +55,7 @@
         copy.wait()
 
 
-def weight_kernel(one_ref, two_ref, three_ref, qlen_ref, b4_ref, w1_ref, w2_ref, w3a_ref, w3b_ref, qlen_out, b4_out):
+def weight_kernel(one_ref, two_ref, three_ref, qlen_ref, b4_ref, w1_ref, w2_ref, w3_ref, qlen_out, b4_out):
     qlen_out[...] = jnp.full(qlen_out.shape, qlen_ref[0], jnp.int32)
     b4_out[...] = jnp.full(b4_out.shape, b4_ref[0], F32)
     row = lax.broadcasted_iota(jnp.int32, (LANES, 256), 0)
@@ -101,14 +102,13 @@
         w2_ref[start + 576 : start + 640, :] = jnp.zeros((64, 256), BF16)
 
     column = lane // 128
-    starts = ((0, 384), (768, 1152), (1536,))
-    for ref, first in ((w3a_ref, 0), (w3b_ref, 2)):
+    for at, first in ((0, 0), (1, 2)):
         for d in range(3):
             total = jnp.zeros((LANES, 256), F32)
             for t in range(3):
                 tile = tall(wide(three_ref[3 * d + t], 2), 2)
                 total = jnp.where(row // 64 + first - column == t, tile, total)
-            place(ref, LANES * d, starts, total)
+            place(w3_ref, LANES * d, ((768 * at, 768 * at + 384), (1536 + 384 * at,)), total)
 
 
 def moved_rows(x, step):
@@ -139,12 +139,11 @@
     blocks, rest = rest[:n_blocks], rest[n_blocks:]
     late = ()
     if n_blocks > 1:
-        late, rest = rest[9:11], rest[:9] + rest[11:]
+        late, rest = rest[8:10], rest[:8] + rest[10:]
     (
         w1_ref,
         w2_ref,
-        w3a_ref,
-        w3b_ref,
+        w3_ref,
         b1_ref,
         b2_ref,
         b3_ref,
@@ -170,7 +169,7 @@
     if n_blocks == 1:
         clip[...] = blocks[0][...]
     else:
-        first, third, first_passed, third_passed, one_away, own = blocks
+        third, first, third_passed, first_passed, one_away, own = blocks
         band = own.shape[1]
         pieces = [(0, own[...]), (1, one_away[...])]
         for at, (direct, passed) in enumerate(((first, first_passed), late, (third, third_passed))):
@@ -266,12 +265,8 @@
                 x2[base : base + half, at : at + LANES] = high
                 x2[base : base + half, 640 + at : 640 + at + LANES] = low
     for n in range(0, windows, 2):
-        rows = pl.ds(n * half, 2 * half)
-        made = (
-            dot(x2[rows, :], w2_ref[0:1280, :])
-            + dot(x2[rows, 0:640], w2_ref[1280:1920, :])
-            + dot(x2[rows, 0:640], w2_ref[1920:2560, :])
-        )
+        left = x2[n * half : (n + 2) * half, :]
+        made = dot(jnp.concatenate([left, left[:, :640], left[:, :640]], axis=1), w2_ref[...])
         made = jnp.maximum(made[:, :LANES], made[:, LANES:])
         for i in range(2):
             here = jnp.maximum(made[i * half : i * half + quarter], made[i * half + quarter : (i + 1) * half])
@@ -289,14 +284,9 @@
     row_best = jnp.full((quarter, LANES), -2.0, F32)
     group = 4
     for n in range(0, windows, group):
-        made = jnp.zeros((group * quarter, 256), F32)
-        for at, ref in ((n, w3a_ref), (n + 1, w3b_ref)):
-            rows = pl.ds(at * quarter, group * quarter)
-            made = made + (
-                dot(x3[rows, :], ref[0:768, :])
-                + dot(x3[rows, :], ref[768:1536, :])
-                + dot(x3[rows, 0:384], ref[1536:1920, :])
-            )
+        left = x3[n * quarter : (n + group) * quarter, :]
+        right = x3[(n + 1) * quarter : (n + 1 + group) * quarter, :]
+        made = dot(jnp.concatenate([left, right, left[:, :384], right[:, :384]], axis=1), w3_ref[...])
         for c in range(2):
             third = jnp.maximum(made[:, c * LANES : (c + 1) * LANES] + b3_ref[...], 0.0)
             summed = jnp.sum(third * k4_ref[...], axis=1, keepdims=True)
@@ -364,7 +354,7 @@
             moves = [(q * n_slab + s, (q ^ rounds[s % 2][at]) * n_slab + s) for q in range(n_query) for s in range(n_slab)]
             return lax.ppermute(sent[at], ("pb", "slab"), moves)
 
-        first, third = cross(0), cross(2)
+        third, first = cross(2), cross(0)
         own = sent[steps + 2]
     else:
         ids = lax.dynamic_index_in_dim(candidates, lax.axis_index("slab"), 1, keepdims=False)
@@ -379,14 +369,14 @@
         order = order + [o ^ k for o in order]
     if rounds is not None:
         one_away = lax.ppermute(sent[steps], "pb", [(q, q ^ 1) for q in range(n_query)])
-        blocks = [first, third, swap(first, 1), swap(third, 1), one_away, sent[steps + 1]]
+        blocks = [third, first, swap(third, 1), swap(first, 1), one_away, sent[steps + 1]]
 
     weights = pl.pallas_call(
         weight_kernel,
-        out_shape=[jax.ShapeDtypeStruct((rows, 256), BF16) for rows in (256, 2560, 1920, 1920)]
+        out_shape=[jax.ShapeDtypeStruct((rows, 256), BF16) for rows in (256, 2560, 2304)]
         + [jax.ShapeDtypeStruct((1, LANES), t) for t in (jnp.int32, F32)],
         in_specs=[vmem] * 3 + [smem] * 2,
-        out_specs=[vmem] * 6,
+        out_specs=[vmem] * 5,
         compiler_params=pltpu.CompilerParams(vmem_limit_bytes=10 * 1024 * 1024),
         cost_estimate=pl.CostEstimate(flops=2_000_000, bytes_accessed=6_000_000, transcendentals=0),
         name="lay_out_kernels",
@@ -407,7 +397,7 @@
     vector = pl.pallas_call(
         functools.partial(score_kernel, rounds, len(blocks), order, regions, frames),
         out_shape=jax.ShapeDtypeStruct((1, LANES), F32),
-        in_specs=[smem, vmem, smem] + [vmem] * (len(blocks) + len(late) + n_slab + 9),
+        in_specs=[smem, vmem, smem] + [vmem] * (len(blocks) + len(late) + n_slab + 8),
         out_specs=vmem,
         scratch_shapes=[
             pltpu.VMEM((regions, frames, feature_width), BF16),

time: 32.7 us -> 31.3 us (0.957)
  the two profiles are of different devices: /device:TPU:17 before, /device:TPU:0 now
where the time goes in v5:
time: 31.3 us; the launch traced here: 30.9 us
  starting transfers between devices  12.7 us (41%)
  waiting for transfers between devices  8.33 us (27%)
  Pallas kernels  7.89 us (25%)
  between operations  1.42 us (5%)
  other arithmetic  0.52 us (2%)
    ppermute x3, starting transfers between devices, cross(): return lax.ppermute(sent[at], ('pb', 'slab'), moves)  7.77 us
    pallas_call x1, Pallas kernels, per_device(): pl.pallas_call(functools.partial(score_kernel, rounds, len(blocks), order...  5.18 us
    ppermute x9, starting transfers between devices, swap(): return lax.ppermute(x, 'slab', [(s, s ^ k) for s in range(n_slab)])  4.41 us
    ppermute x3, waiting for transfers between devices, cross(): return lax.ppermute(sent[at], ('pb', 'slab'), moves)  4.22 us
    ppermute x9, waiting for transfers between devices, swap(): return lax.ppermute(x, 'slab', [(s, s ^ k) for s in range(n_slab)])  4.1 us
    pallas_call x1, Pallas kernels, per_device(): pl.pallas_call(functools.partial(pick_kernel, rounds), out_shape=[jax.Sha...  2.06 us
    pallas_call x1, Pallas kernels, per_device(): pl.pallas_call(weight_kernel, out_shape=[jax.ShapeDtypeStruct((rows, 256)...  0.66 us
  transfers between devices with their start and end apart: 13, of which 8 were waited for; matrix products, arithmetic and copies ran while one was open for 0% of the time, Pallas kernels for 2%

profile of v5, /device:TPU:0, one launch (start us, length us, event | category | flops | bytes accessed | tf_op | source)
XLA Modules:
  0.0 30.9 jit_solution(5064697692052948273)
XLA Ops:
  0.0 0.0 copy-start
  0.0 0.0 copy-start.1
  0.0 0.0 copy-start.2
  0.0 0.0 copy-start.3
  0.0 0.0 copy-start.4
  0.0 0.0 copy-start.5
  0.0 0.0 copy-start.6
  0.0 0.0 copy-start.7
  0.0 0.0 copy-start.8
  0.1 2.1 %pick_bands.1 = (bf16[2,9,16,256]{3,2,1,0:T(8,128)(2,1)S(1)}, bf16[2,9,16,256]{3,2,1,0:T(8,128)(2,1)S(1)}, bf16[2,9,16,256]{3,2,1,0:T(8,128)(2,1)S(1)}, bf16[9,1...) custom-call(s32[4,8]{1,0:T(4,128)} %bitcast.16, ...), custom_call_target="tpu_custom_call" | custom-call | tf_op jit(solution)/shard_map/pick_bands/pallas_call | solution.py:339
  2.1 5.1 %collective-permute-start.8 = (bf16[2,9,16,256]{3,2,1,0:T(8,128)(2,1)S(1)}, bf16[2,9,16,256]{3,2,1,0:T(8,128)(2,1)S(1)}, u32[]{:S(2)}, u32[]{:S(2)}) collective-permute-start(bf16[2,9,16,256]{3,2,1,0:T(8,128)(2,1)S(1)} %get-tuple-element.24), channel_id=1, source_target_pairs={{0,20},{1,25},{2,22},{3,27},{4,16},{5,29},{6,18},{7,31},{8,28},{9,... | collective-permute-start | bytes 442376 | tf_op jit(solution)/shard_map/ppermute | solution.py:355
  7.2 1.5 %collective-permute-start.3 = (bf16[2,9,16,256]{3,2,1,0:T(8,128)(2,1)S(1)}, bf16[2,9,16,256]{3,2,1,0:T(8,128)(2,1)S(1)}, u32[]{:S(2)}, u32[]{:S(2)}) collective-permute-start(bf16[2,9,16,256]{3,2,1,0:T(8,128)(2,1)S(1)} %get-tuple-element.20), channel_id=1, source_target_pairs={{0,12},{1,9},{2,14},{3,11},{4,8},{5,13},{6,10},{7,15},{8,4},{9,1},... | collective-permute-start | bytes 442376 | tf_op jit(solution)/shard_map/ppermute | solution.py:355
  8.7 1.2 %collective-permute-start.4 = (bf16[2,9,16,256]{3,2,1,0:T(8,128)(2,1)S(1)}, bf16[2,9,16,256]{3,2,1,0:T(8,128)(2,1)S(1)}, u32[]{:S(2)}, u32[]{:S(2)}) collective-permute-start(bf16[2,9,16,256]{3,2,1,0:T(8,128)(2,1)S(1)} %get-tuple-element.21), channel_id=1, source_target_pairs={{0,28},{1,17},{2,30},{3,19},{4,24},{5,21},{6,26},{7,23},{8,20},{9,... | collective-permute-start | bytes 442376 | tf_op jit(solution)/shard_map/ppermute | solution.py:355
  9.9 1.5 %collective-permute-start = (bf16[9,32,256]{2,1,0:T(8,128)(2,1)S(1)}, bf16[9,32,256]{2,1,0:T(8,128)(2,1)S(1)}, u32[]{:S(2)}, u32[]{:S(2)}) collective-permute-start(bf16[9,32,256]{2,1,0:T(8,128)(2,1)S(1)} %get-tuple-element.19.rest_0_), channel_id=1, source_target_pairs={{0,2},{1,3},{2,0},{3,1},{4,6},{5,7},{6,4},{7,5},{8,10},{9,11},{10,... | collective-permute-start | bytes 442376 | tf_op jit(solution)/shard_map/ppermute | solution.py:333
  11.4 0.5 %collective-permute-start.7 = (bf16[9,16,256]{2,1,0:T(8,128)(2,1)S(1)}, bf16[9,16,256]{2,1,0:T(8,128)(2,1)S(1)}, u32[]{:S(2)}, u32[]{:S(2)}) collective-permute-start(bf16[9,16,256]{2,1,0:T(8,128)(2,1)S(1)} %get-tuple-element.22), channel_id=1, source_target_pairs={{0,4},{4,0},{8,12},{12,8},{16,20},{20,16},{24,28},{28,24},{1,5},{5... | collective-permute-start | bytes 221192 | tf_op jit(solution)/shard_map/ppermute | solution.py:371
  13.2 0.0 copy-done
  13.2 0.0 copy-done.1
  13.2 0.0 copy-done.2
  13.2 0.7 %lay_out_kernels.1 = (bf16[256,256]{1,0:T(8,128)(2,1)S(1)}, bf16[2560,256]{1,0:T(8,128)(2,1)S(1)}, bf16[2304,256]{1,0:T(8,128)(2,1)S(1)}, s32[1,128]{1,0:T(1,128)S(1)}, f32[1,128]{1,0:T(1,128)S(1)}) custom-call(f32[9,1,32]{2,1,0:T(1,128)S(1)} %bitcast.15, f32[9,32,64]{2,1,0:T(8,128)S(1)} %bitcast.14, f32[9,64,128]{2,1,0:T(8,128)S(1)} %bitcast.13, ...), custom_call_target="tpu_custom_call" | custom-call | flops 2000000 | bytes 6000000 | tf_op jit(solution)/shard_map/lay_out_kernels/pallas_call | solution.py:374
  13.9 2.0 %collective-permute-done.8.rest_18_ = bf16[2,9,16,256]{3,2,1,0:T(8,128)(2,1)S(1)} collective-permute-done((bf16[2,9,16,256]{3,2,1,0:T(8,128)(2,1)S(1)}, bf16[2,9,16,256]{3,2,1,0:T(8,128)(2,1)S(1)}, u32[]{:S(2)}, u32[]{:S(2)}) %collective-permute-start.8) | collective-permute-done | bytes 147488 | tf_op jit(solution)/shard_map/ppermute | solution.py:355
  15.9 0.0 collective-permute-start.1
  15.9 0.1 collective-permute-done.3.rest_4_
  16.0 0.4 %collective-permute-start.5 = (bf16[2,9,16,256]{3,2,1,0:T(8,128)(2,1)S(1)}, bf16[2,9,16,256]{3,2,1,0:T(8,128)(2,1)S(1)}, u32[]{:S(2)}, u32[]{:S(2)}) collective-permute-start(bf16[2,9,16,256]{3,2,1,0:T(8,128)(2,1)S(1)} %collective-permute-done.3.rest_4_), channel_id=1, source_target_pairs={{0,1},{1,0},{2,3},{3,2},{4,5},{5,4},{6,7},{7,6},{8,9},{9,8},{10,11... | collective-permute-start | bytes 442376 | tf_op jit(solution)/shard_map/ppermute | solution.py:333
  16.4 2.1 %collective-permute-done.4.rest_5_ = bf16[2,9,16,256]{3,2,1,0:T(8,128)(2,1)S(1)} collective-permute-done((bf16[2,9,16,256]{3,2,1,0:T(8,128)(2,1)S(1)}, bf16[2,9,16,256]{3,2,1,0:T(8,128)(2,1)S(1)}, u32[]{:S(2)}, u32[]{:S(2)}) %collective-permute-start.4) | collective-permute-done | bytes 147488 | tf_op jit(solution)/shard_map/ppermute | solution.py:355
  18.5 0.1 collective-permute-start.6
  18.6 0.0 collective-permute-done.rest_1_
  18.6 0.5 %collective-permute-start.2 = (bf16[9,32,256]{2,1,0:T(8,128)(2,1)S(1)}, bf16[9,32,256]{2,1,0:T(8,128)(2,1)S(1)}, u32[]{:S(2)}, u32[]{:S(2)}) collective-permute-start(bf16[9,32,256]{2,1,0:T(8,128)(2,1)S(1)} %collective-permute-done.rest_1_), channel_id=1, source_target_pairs={{0,1},{1,0},{2,3},{3,2},{4,5},{5,4},{6,7},{7,6},{8,9},{9,8},{10,11... | collective-permute-start | bytes 442376 | tf_op jit(solution)/shard_map/ppermute | solution.py:333
  19.0 0.0 collective-permute-done.7.rest_8_
  19.0 0.1 collective-permute-start.9
  19.1 0.0 collective-permute-done.1.rest_2_
  19.1 0.0 collective-permute-done.5.rest_6_
  19.1 0.8 %collective-permute-done.6.rest_7_ = bf16[2,9,16,256]{3,2,1,0:T(8,128)(2,1)S(1)} collective-permute-done((bf16[2,9,16,256]{3,2,1,0:T(8,128)(2,1)S(1)}, bf16[2,9,16,256]{3,2,1,0:T(8,128)(2,1)S(1)}, u32[]{:S(2)}, u32[]{:S(2)}) %collective-permute-start.6) | collective-permute-done | bytes 147488 | tf_op jit(solution)/shard_map/ppermute | solution.py:333
  19.9 0.2 collective-permute-done.2.rest_3_
  20.1 0.3 collective-permute-done.9.rest_19_
  20.4 0.0 copy-done.3
  20.4 0.0 copy-done.4
  20.4 0.0 copy-done.5
  20.4 0.0 copy-done.6
  20.4 0.0 copy-done.7
  20.4 0.0 copy-done.8
  20.4 5.2 %score_pair.1 = f32[1,128]{1,0:T(1,128)S(1)} custom-call(s32[4,8]{1,0:T(4,128)S(1)} %bitcast.17, s32[1,128]{1,0:T(1,128)S(1)} %get-tuple-element.18.qlen_ref, s32[32]{0:T(128)S(1)} %copy-done.4, bf16[9,32,256]{2,1,0:T(8,128)(2,1)S(1)} %get-tuple-element.19.rest_0_, bf16[9,32,256]{2,1,0:T(8,128)(2,1)S(1)} %collective-permute-done.rest_1_, ...), custom_call_target="tpu_custom_call" | custom-call | flops 2000000000 | bytes 8000000 | tf_op jit(solution)/shard_map/score_pair/pallas_call | solution.py:397
  25.6 0.3 collective-permute-start.12
  25.9 1.5 %collective-permute-start.11 = (f32[1,128]{1,0:T(1,128)S(1)}, f32[1,128]{1,0:T(1,128)S(1)}, u32[]{:S(2)}, u32[]{:S(2)}) collective-permute-start(f32[1,128]{1,0:T(1,128)S(1)} %score_pair.1), channel_id=1, source_target_pairs={{0,2},{1,3},{2,0},{3,1},{4,6},{5,7},{6,4},{7,5},{8,10},{9,11},{10,... | collective-permute-start | bytes 1544 | tf_op jit(solution)/shard_map/ppermute | solution.py:333
  27.4 0.2 collective-permute-start.10
  27.6 0.0 collective-permute-done.12
  27.6 1.9 %collective-permute-done.11 = f32[1,128]{1,0:T(1,128)S(1)} collective-permute-done((f32[1,128]{1,0:T(1,128)S(1)}, f32[1,128]{1,0:T(1,128)S(1)}, u32[]{:S(2)}, u32[]{:S(2)}) %collective-permute-start.11) | collective-permute-done | bytes 544 | tf_op jit(solution)/shard_map/ppermute | solution.py:333
  29.4 0.9 %collective-permute-done.10 = f32[1,128]{1,0:T(1,128)S(1)} collective-permute-done((f32[1,128]{1,0:T(1,128)S(1)}, f32[1,128]{1,0:T(1,128)S(1)}, u32[]{:S(2)}, u32[]{:S(2)}) %collective-permute-start.10) | collective-permute-done | bytes 544 | tf_op jit(solution)/shard_map/ppermute | solution.py:333
  30.4 0.5 %add_add_fusion = f32[1,128]{1,0:T(1,128)} fusion(f32[1,128]{1,0:T(1,128)S(1)} %collective-permute-done.12, f32[1,128]{1,0:T(1,128)S(1)} %collective-permute-done.11, f32[1,128]{1,0:T(1,128)S(1)} %score_pair.1, f32[1,128]{1,0:T(1,128)S(1)} %collective-permute-done.10), kind=kLoop, calls=%fused_computation | loop fusion | flops 384 | bytes 2560 | tf_op jit(solution)/shard_map/add | solution.py:429
Async XLA Ops:
  0.0 13.2 %copy-start = (f32[3,3,64,128]{3,2,1,0:T(8,128)S(1)}, f32[3,3,64,128]{3,2,1,0:T(8,128)}, u32[]{:S(2)}) copy-start(f32[3,3,64,128]{3,2,1,0:T(8,128)} %param.22) | copy-start | bytes 884740
  0.0 13.2 %copy-start.1 = (f32[3,3,32,64]{3,2,1,0:T(8,128)S(1)}, f32[3,3,32,64]{3,2,1,0:T(8,128)}, u32[]{:S(2)}) copy-start(f32[3,3,32,64]{3,2,1,0:T(8,128)} %param.20) | copy-start | bytes 221188
  0.0 13.2 %copy-start.2 = (f32[3,3,1,32]{3,2,1,0:T(1,128)S(1)}, f32[3,3,1,32]{3,2,1,0:T(1,128)}, u32[]{:S(2)}) copy-start(f32[3,3,1,32]{3,2,1,0:T(1,128)} %param.18) | copy-start | bytes 3460
  0.0 20.4 %copy-start.3 = (s32[8,4]{0,1:T(4,128)S(1)}, s32[8,4]{0,1:T(4,128)}, u32[]{:S(2)}) copy-start(s32[8,4]{0,1:T(4,128)} %param.15) | copy-start | bytes 388
  0.0 20.4 %copy-start.4 = (s32[32]{0:T(128)S(1)}, s32[32]{0:T(128)}, u32[]{:S(2)}) copy-start(s32[32]{0:T(128)} %clen_ref.1) | copy-start | bytes 388
  0.0 20.4 %copy-start.5 = (f32[32]{0:T(128)S(1)}, f32[32]{0:T(128)}, u32[]{:S(2)}) copy-start(f32[32]{0:T(128)} %param.19) | copy-start | bytes 388
  0.0 20.4 %copy-start.6 = (f32[64]{0:T(128)S(1)}, f32[64]{0:T(128)}, u32[]{:S(2)}) copy-start(f32[64]{0:T(128)} %param.21) | copy-start | bytes 772
  0.0 20.4 %copy-start.7 = (f32[128]{0:T(128)S(1)}, f32[128]{0:T(128)}, u32[]{:S(2)}) copy-start(f32[128]{0:T(128)} %param.23) | copy-start | bytes 1540
  0.0 20.4 %copy-start.8 = (f32[1,1,128,1]{2,3,1,0:T(1,128)S(1)}, f32[1,1,128,1]{2,3,1,0:T(1,128)}, u32[]{:S(2)}) copy-start(f32[1,1,128,1]{2,3,1,0:T(1,128)} %param.24) | copy-start | bytes 1540
  2.1 13.7 %collective-permute-start.8 = (bf16[2,9,16,256]{3,2,1,0:T(8,128)(2,1)S(1)}, bf16[2,9,16,256]{3,2,1,0:T(8,128)(2,1)S(1)}, u32[]{:S(2)}, u32[]{:S(2)}) collective-permute-start(bf16[2,9,16,256]{3,2,1,0:T(8,128)(2,1)S(1)} %get-tuple-element.24), channel_id=1, source_target_pairs={{0,20},{1,25},{2,22},{3,27},{4,16},{5,29},{6,18},{7,31},{8,28},{9,... | collective-permute-start | bytes 442376 | tf_op jit(solution)/shard_map/ppermute | solution.py:355
  7.2 8.8 %collective-permute-start.3 = (bf16[2,9,16,256]{3,2,1,0:T(8,128)(2,1)S(1)}, bf16[2,9,16,256]{3,2,1,0:T(8,128)(2,1)S(1)}, u32[]{:S(2)}, u32[]{:S(2)}) collective-permute-start(bf16[2,9,16,256]{3,2,1,0:T(8,128)(2,1)S(1)} %get-tuple-element.20), channel_id=1, source_target_pairs={{0,12},{1,9},{2,14},{3,11},{4,8},{5,13},{6,10},{7,15},{8,4},{9,1},... | collective-permute-start | bytes 442376 | tf_op jit(solution)/shard_map/ppermute | solution.py:355
  8.7 9.8 %collective-permute-start.4 = (bf16[2,9,16,256]{3,2,1,0:T(8,128)(2,1)S(1)}, bf16[2,9,16,256]{3,2,1,0:T(8,128)(2,1)S(1)}, u32[]{:S(2)}, u32[]{:S(2)}) collective-permute-start(bf16[2,9,16,256]{3,2,1,0:T(8,128)(2,1)S(1)} %get-tuple-element.21), channel_id=1, source_target_pairs={{0,28},{1,17},{2,30},{3,19},{4,24},{5,21},{6,26},{7,23},{8,20},{9,... | collective-permute-start | bytes 442376 | tf_op jit(solution)/shard_map/ppermute | solution.py:355
  9.9 8.7 %collective-permute-start = (bf16[9,32,256]{2,1,0:T(8,128)(2,1)S(1)}, bf16[9,32,256]{2,1,0:T(8,128)(2,1)S(1)}, u32[]{:S(2)}, u32[]{:S(2)}) collective-permute-start(bf16[9,32,256]{2,1,0:T(8,128)(2,1)S(1)} %get-tuple-element.19.rest_0_), channel_id=1, source_target_pairs={{0,2},{1,3},{2,0},{3,1},{4,6},{5,7},{6,4},{7,5},{8,10},{9,11},{10,... | collective-permute-start | bytes 442376 | tf_op jit(solution)/shard_map/ppermute | solution.py:333
  11.4 7.7 %collective-permute-start.7 = (bf16[9,16,256]{2,1,0:T(8,128)(2,1)S(1)}, bf16[9,16,256]{2,1,0:T(8,128)(2,1)S(1)}, u32[]{:S(2)}, u32[]{:S(2)}) collective-permute-start(bf16[9,16,256]{2,1,0:T(8,128)(2,1)S(1)} %get-tuple-element.22), channel_id=1, source_target_pairs={{0,4},{4,0},{8,12},{12,8},{16,20},{20,16},{24,28},{28,24},{1,5},{5... | collective-permute-start | bytes 221192 | tf_op jit(solution)/shard_map/ppermute | solution.py:371
  15.9 3.2 %collective-permute-start.1 = (bf16[9,32,256]{2,1,0:T(8,128)(2,1)S(1)}, bf16[9,32,256]{2,1,0:T(8,128)(2,1)S(1)}, u32[]{:S(2)}, u32[]{:S(2)}) collective-permute-start(bf16[9,32,256]{2,1,0:T(8,128)(2,1)S(1)} %get-tuple-element.19.rest_0_), channel_id=1, source_target_pairs={{0,1},{1,0},{2,3},{3,2},{4,5},{5,4},{6,7},{7,6},{8,9},{9,8},{10,11... | collective-permute-start | bytes 442376 | tf_op jit(solution)/shard_map/ppermute | solution.py:333
  16.0 3.1 %collective-permute-start.5 = (bf16[2,9,16,256]{3,2,1,0:T(8,128)(2,1)S(1)}, bf16[2,9,16,256]{3,2,1,0:T(8,128)(2,1)S(1)}, u32[]{:S(2)}, u32[]{:S(2)}) collective-permute-start(bf16[2,9,16,256]{3,2,1,0:T(8,128)(2,1)S(1)} %collective-permute-done.3.rest_4_), channel_id=1, source_target_pairs={{0,1},{1,0},{2,3},{3,2},{4,5},{5,4},{6,7},{7,6},{8,9},{9,8},{10,11... | collective-permute-start | bytes 442376 | tf_op jit(solution)/shard_map/ppermute | solution.py:333
  18.5 1.4 %collective-permute-start.6 = (bf16[2,9,16,256]{3,2,1,0:T(8,128)(2,1)S(1)}, bf16[2,9,16,256]{3,2,1,0:T(8,128)(2,1)S(1)}, u32[]{:S(2)}, u32[]{:S(2)}) collective-permute-start(bf16[2,9,16,256]{3,2,1,0:T(8,128)(2,1)S(1)} %collective-permute-done.4.rest_5_), channel_id=1, source_target_pairs={{0,1},{1,0},{2,3},{3,2},{4,5},{5,4},{6,7},{7,6},{8,9},{9,8},{10,11... | collective-permute-start | bytes 442376 | tf_op jit(solution)/shard_map/ppermute | solution.py:333
  18.6 1.5 %collective-permute-start.2 = (bf16[9,32,256]{2,1,0:T(8,128)(2,1)S(1)}, bf16[9,32,256]{2,1,0:T(8,128)(2,1)S(1)}, u32[]{:S(2)}, u32[]{:S(2)}) collective-permute-start(bf16[9,32,256]{2,1,0:T(8,128)(2,1)S(1)} %collective-permute-done.rest_1_), channel_id=1, source_target_pairs={{0,1},{1,0},{2,3},{3,2},{4,5},{5,4},{6,7},{7,6},{8,9},{9,8},{10,11... | collective-permute-start | bytes 442376 | tf_op jit(solution)/shard_map/ppermute | solution.py:333
  19.0 1.4 %collective-permute-start.9 = (bf16[2,9,16,256]{3,2,1,0:T(8,128)(2,1)S(1)}, bf16[2,9,16,256]{3,2,1,0:T(8,128)(2,1)S(1)}, u32[]{:S(2)}, u32[]{:S(2)}) collective-permute-start(bf16[2,9,16,256]{3,2,1,0:T(8,128)(2,1)S(1)} %collective-permute-done.8.rest_18_), channel_id=1, source_target_pairs={{0,1},{1,0},{2,3},{3,2},{4,5},{5,4},{6,7},{7,6},{8,9},{9,8},{10,11... | collective-permute-start | bytes 442376 | tf_op jit(solution)/shard_map/ppermute | solution.py:333
  25.6 1.9 %collective-permute-start.12 = (f32[1,128]{1,0:T(1,128)S(1)}, f32[1,128]{1,0:T(1,128)S(1)}, u32[]{:S(2)}, u32[]{:S(2)}) collective-permute-start(f32[1,128]{1,0:T(1,128)S(1)} %score_pair.1), channel_id=1, source_target_pairs={{0,1},{1,0},{2,3},{3,2},{4,5},{5,4},{6,7},{7,6},{8,9},{9,8},{10,11... | collective-permute-start | bytes 1544 | tf_op jit(solution)/shard_map/ppermute | solution.py:333
  25.9 3.5 %collective-permute-start.11 = (f32[1,128]{1,0:T(1,128)S(1)}, f32[1,128]{1,0:T(1,128)S(1)}, u32[]{:S(2)}, u32[]{:S(2)}) collective-permute-start(f32[1,128]{1,0:T(1,128)S(1)} %score_pair.1), channel_id=1, source_target_pairs={{0,2},{1,3},{2,0},{3,1},{4,6},{5,7},{6,4},{7,5},{8,10},{9,11},{10,... | collective-permute-start | bytes 1544 | tf_op jit(solution)/shard_map/ppermute | solution.py:333
  27.4 3.0 %collective-permute-start.10 = (f32[1,128]{1,0:T(1,128)S(1)}, f32[1,128]{1,0:T(1,128)S(1)}, u32[]{:S(2)}, u32[]{:S(2)}) collective-permute-start(f32[1,128]{1,0:T(1,128)S(1)} %score_pair.1), channel_id=1, source_target_pairs={{0,3},{1,2},{2,1},{3,0},{4,7},{5,6},{6,5},{7,4},{8,11},{9,10},{10,... | collective-permute-start | bytes 1544 | tf_op jit(solution)/shard_map/ppermute | solution.py:333

commit v6 on v5

--- a/solution.py
+++ b/solution.py
@@ -55,8 +55,24 @@
         copy.wait()
 
 
-def weight_kernel(one_ref, two_ref, three_ref, qlen_ref, b4_ref, w1_ref, w2_ref, w3_ref, qlen_out, b4_out):
+def weight_kernel(
+    one_ref,
+    two_ref,
+    three_ref,
+    cand_ref,
+    qlen_ref,
+    clen_ref,
+    b4_ref,
+    w1_ref,
+    w2_ref,
+    w3_ref,
+    qlen_out,
+    clen_out,
+    b4_out,
+):
     qlen_out[...] = jnp.full(qlen_out.shape, qlen_ref[0], jnp.int32)
+    clip_len = clen_ref[cand_ref[lax.axis_index("slab"), lax.axis_index("pb")]]
+    clen_out[...] = jnp.full(clen_out.shape, clip_len, jnp.int32)
     b4_out[...] = jnp.full(b4_out.shape, b4_ref[0], F32)
     row = lax.broadcasted_iota(jnp.int32, (LANES, 256), 0)
     lane = lax.broadcasted_iota(jnp.int32, (LANES, 256), 1)
@@ -129,7 +145,6 @@
     order,
     regions,
     frames,
-    cand_ref,
     qlen_ref,
     clen_ref,
     *rest,
@@ -164,7 +179,7 @@
     odd = lax.rem(pair, 2)
     feature_width = feats.shape[-1]
     query_len = qlen_ref[...]
-    clip_len = clen_ref[cand_ref[pair, query]]
+    clip_len = clen_ref[...]
 
     if n_blocks == 1:
         clip[...] = blocks[0][...]
@@ -374,9 +389,9 @@
     weights = pl.pallas_call(
         weight_kernel,
         out_shape=[jax.ShapeDtypeStruct((rows, 256), BF16) for rows in (256, 2560, 2304)]
-        + [jax.ShapeDtypeStruct((1, LANES), t) for t in (jnp.int32, F32)],
-        in_specs=[vmem] * 3 + [smem] * 2,
-        out_specs=[vmem] * 5,
+        + [jax.ShapeDtypeStruct((1, LANES), t) for t in (jnp.int32, jnp.int32, F32)],
+        in_specs=[vmem] * 3 + [smem] * 4,
+        out_specs=[vmem] * 6,
         compiler_params=pltpu.CompilerParams(vmem_limit_bytes=10 * 1024 * 1024),
         cost_estimate=pl.CostEstimate(flops=2_000_000, bytes_accessed=6_000_000, transcendentals=0),
         name="lay_out_kernels",
@@ -384,10 +399,12 @@
         kernel_one.reshape(9, 1, -1),
         kernel_two.reshape(9, 32, 64),
         kernel_three.reshape(9, 64, 128),
+        candidates.T,
         query_length,
+        clip_length,
         bias_four,
     )
-    *weights, query_len, last_bias = weights
+    *weights, query_len, clip_len, last_bias = weights
     late = []
     if rounds is not None:
         second = cross(1)
@@ -397,7 +414,7 @@
     vector = pl.pallas_call(
         functools.partial(score_kernel, rounds, len(blocks), order, regions, frames),
         out_shape=jax.ShapeDtypeStruct((1, LANES), F32),
-        in_specs=[smem, vmem, smem] + [vmem] * (len(blocks) + len(late) + n_slab + 8),
+        in_specs=[vmem] * (2 + len(blocks) + len(late) + n_slab + 8),
         out_specs=vmem,
         scratch_shapes=[
             pltpu.VMEM((regions, frames, feature_width), BF16),
@@ -413,9 +430,8 @@
         cost_estimate=pl.CostEstimate(flops=2_000_000_000, bytes_accessed=8_000_000, transcendentals=0),
         name="score_pair",
     )(
-        candidates.T,
         query_len,
-        clip_length,
+        clip_len,
         *slabs,
         *blocks,
         *weights,

time: 31.3 us -> 30.7 us (0.981)
  waiting for transfers between devices: 8.33 us -> 7.74 us
    ppermute x3, waiting for transfers between devices: 4.22 us -> 3.63 us  [cross(): return lax.ppermute(sent[at], ('pb', 'slab'), moves)]
    pallas_call x1, Pallas kernels: 5.18 us -> 4.6 us  [per_device(): pl.pallas_call(functools.partial(score_kernel, rounds, len(blocks), order...]
    pallas_call x1, Pallas kernels: 0.66 us -> 1.22 us  [per_device(): pl.pallas_call(weight_kernel, out_shape=[jax.ShapeDtypeStruct((rows, 256)...]
  transfers between devices with their start and end apart: 13 -> 13, of which waited for: 8 -> 8; matrix products, arithmetic and copies ran while one was open for 0% -> 0% of each run, Pallas kernels for 2% -> 4%
where the time goes in v6:
time: 30.7 us; the launch traced here: 30.3 us
  starting transfers between devices  12.7 us (41%)
  Pallas kernels  7.89 us (26%)
  waiting for transfers between devices  7.74 us (25%)
  between operations  1.42 us (5%)
  other arithmetic  0.52 us (2%)
    ppermute x3, starting transfers between devices, cross(): return lax.ppermute(sent[at], ('pb', 'slab'), moves)  7.77 us
    pallas_call x1, Pallas kernels, per_device(): pl.pallas_call(functools.partial(score_kernel, rounds, len(blocks), order...  4.6 us
    ppermute x9, starting transfers between devices, swap(): return lax.ppermute(x, 'slab', [(s, s ^ k) for s in range(n_slab)])  4.41 us
    ppermute x9, waiting for transfers between devices, swap(): return lax.ppermute(x, 'slab', [(s, s ^ k) for s in range(n_slab)])  4.1 us
    ppermute x3, waiting for transfers between devices, cross(): return lax.ppermute(sent[at], ('pb', 'slab'), moves)  3.63 us
    pallas_call x1, Pallas kernels, per_device(): pl.pallas_call(functools.partial(pick_kernel, rounds), out_shape=[jax.Sha...  2.06 us
    pallas_call x1, Pallas kernels, per_device(): pl.pallas_call(weight_kernel, out_shape=[jax.ShapeDtypeStruct((rows, 256)...  1.22 us
  transfers between devices with their start and end apart: 13, of which 8 were waited for; matrix products, arithmetic and copies ran while one was open for 0% of the time, Pallas kernels for 4%

profile of v6, /device:TPU:0, one launch (start us, length us, event | category | flops | bytes accessed | tf_op | source)
XLA Modules:
  0.0 30.3 jit_solution(9413652831971929959)
XLA Ops:
  0.0 0.0 copy-start.2
  0.0 0.0 copy-start
  0.0 0.0 copy-start.1
  0.0 0.0 copy-start.3
  0.0 0.0 copy-start.4
  0.0 0.0 copy-start.5
  0.0 0.0 copy-start.6
  0.0 0.0 copy-start.7
  0.0 0.0 copy-start.8
  0.1 2.1 %pick_bands.1 = (bf16[2,9,16,256]{3,2,1,0:T(8,128)(2,1)S(1)}, bf16[2,9,16,256]{3,2,1,0:T(8,128)(2,1)S(1)}, bf16[2,9,16,256]{3,2,1,0:T(8,128)(2,1)S(1)}, bf16[9,1...) custom-call(s32[4,8]{1,0:T(4,128)} %bitcast.15, ...), custom_call_target="tpu_custom_call" | custom-call | tf_op jit(solution)/shard_map/pick_bands/pallas_call | solution.py:354
  2.1 5.1 %collective-permute-start.8 = (bf16[2,9,16,256]{3,2,1,0:T(8,128)(2,1)S(1)}, bf16[2,9,16,256]{3,2,1,0:T(8,128)(2,1)S(1)}, u32[]{:S(2)}, u32[]{:S(2)}) collective-permute-start(bf16[2,9,16,256]{3,2,1,0:T(8,128)(2,1)S(1)} %get-tuple-element.26), channel_id=1, source_target_pairs={{0,20},{1,25},{2,22},{3,27},{4,16},{5,29},{6,18},{7,31},{8,28},{9,... | collective-permute-start | bytes 442376 | tf_op jit(solution)/shard_map/ppermute | solution.py:370
  7.2 1.5 %collective-permute-start.3 = (bf16[2,9,16,256]{3,2,1,0:T(8,128)(2,1)S(1)}, bf16[2,9,16,256]{3,2,1,0:T(8,128)(2,1)S(1)}, u32[]{:S(2)}, u32[]{:S(2)}) collective-permute-start(bf16[2,9,16,256]{3,2,1,0:T(8,128)(2,1)S(1)} %get-tuple-element.22), channel_id=1, source_target_pairs={{0,12},{1,9},{2,14},{3,11},{4,8},{5,13},{6,10},{7,15},{8,4},{9,1},... | collective-permute-start | bytes 442376 | tf_op jit(solution)/shard_map/ppermute | solution.py:370
  8.7 1.2 %collective-permute-start.4 = (bf16[2,9,16,256]{3,2,1,0:T(8,128)(2,1)S(1)}, bf16[2,9,16,256]{3,2,1,0:T(8,128)(2,1)S(1)}, u32[]{:S(2)}, u32[]{:S(2)}) collective-permute-start(bf16[2,9,16,256]{3,2,1,0:T(8,128)(2,1)S(1)} %get-tuple-element.23), channel_id=1, source_target_pairs={{0,28},{1,17},{2,30},{3,19},{4,24},{5,21},{6,26},{7,23},{8,20},{9,... | collective-permute-start | bytes 442376 | tf_op jit(solution)/shard_map/ppermute | solution.py:370
  9.9 1.5 %collective-permute-start = (bf16[9,32,256]{2,1,0:T(8,128)(2,1)S(1)}, bf16[9,32,256]{2,1,0:T(8,128)(2,1)S(1)}, u32[]{:S(2)}, u32[]{:S(2)}) collective-permute-start(bf16[9,32,256]{2,1,0:T(8,128)(2,1)S(1)} %get-tuple-element.21.rest_0_), channel_id=1, source_target_pairs={{0,2},{1,3},{2,0},{3,1},{4,6},{5,7},{6,4},{7,5},{8,10},{9,11},{10,... | collective-permute-start | bytes 442376 | tf_op jit(solution)/shard_map/ppermute | solution.py:348
  11.4 0.5 %collective-permute-start.7 = (bf16[9,16,256]{2,1,0:T(8,128)(2,1)S(1)}, bf16[9,16,256]{2,1,0:T(8,128)(2,1)S(1)}, u32[]{:S(2)}, u32[]{:S(2)}) collective-permute-start(bf16[9,16,256]{2,1,0:T(8,128)(2,1)S(1)} %get-tuple-element.24), channel_id=1, source_target_pairs={{0,4},{4,0},{8,12},{12,8},{16,20},{20,16},{24,28},{28,24},{1,5},{5... | collective-permute-start | bytes 221192 | tf_op jit(solution)/shard_map/ppermute | solution.py:386
  13.2 0.0 copy-done.2
  13.2 0.0 copy-done
  13.2 0.0 copy-done.1
  13.2 0.0 copy-done.3
  13.2 0.0 copy-done.4
  13.2 1.2 %lay_out_kernels.1 = (bf16[256,256]{1,0:T(8,128)(2,1)S(1)}, bf16[2560,256]{1,0:T(8,128)(2,1)S(1)}, bf16[2304,256]{1,0:T(8,128)(2,1)S(1)}, s32[1,128]{1,0:T(1,128...) custom-call(f32[9,1,32]{2,1,0:T(1,128)S(1)} %bitcast.17, f32[9,32,64]{2,1,0:T(8,128)S(1)} %bitcast.14, ...), custom_call_target="tpu_custom_call" | custom-call | flops 2000000 | bytes 6000000 | tf_op jit(solution)/shard_map/lay_out_kernels/pallas_call | solution.py:389
  14.5 1.4 %collective-permute-done.8.rest_18_ = bf16[2,9,16,256]{3,2,1,0:T(8,128)(2,1)S(1)} collective-permute-done((bf16[2,9,16,256]{3,2,1,0:T(8,128)(2,1)S(1)}, bf16[2,9,16,256]{3,2,1,0:T(8,128)(2,1)S(1)}, u32[]{:S(2)}, u32[]{:S(2)}) %collective-permute-start.8) | collective-permute-done | bytes 147488 | tf_op jit(solution)/shard_map/ppermute | solution.py:370
  15.9 0.0 collective-permute-start.1
  15.9 0.1 collective-permute-done.3.rest_4_
  16.0 0.4 %collective-permute-start.5 = (bf16[2,9,16,256]{3,2,1,0:T(8,128)(2,1)S(1)}, bf16[2,9,16,256]{3,2,1,0:T(8,128)(2,1)S(1)}, u32[]{:S(2)}, u32[]{:S(2)}) collective-permute-start(bf16[2,9,16,256]{3,2,1,0:T(8,128)(2,1)S(1)} %collective-permute-done.3.rest_4_), channel_id=1, source_target_pairs={{0,1},{1,0},{2,3},{3,2},{4,5},{5,4},{6,7},{7,6},{8,9},{9,8},{10,11... | collective-permute-start | bytes 442376 | tf_op jit(solution)/shard_map/ppermute | solution.py:348
  16.4 2.1 %collective-permute-done.4.rest_5_ = bf16[2,9,16,256]{3,2,1,0:T(8,128)(2,1)S(1)} collective-permute-done((bf16[2,9,16,256]{3,2,1,0:T(8,128)(2,1)S(1)}, bf16[2,9,16,256]{3,2,1,0:T(8,128)(2,1)S(1)}, u32[]{:S(2)}, u32[]{:S(2)}) %collective-permute-start.4) | collective-permute-done | bytes 147488 | tf_op jit(solution)/shard_map/ppermute | solution.py:370
  18.5 0.1 collective-permute-start.6
  18.6 0.0 collective-permute-done.rest_1_
  18.6 0.5 %collective-permute-start.2 = (bf16[9,32,256]{2,1,0:T(8,128)(2,1)S(1)}, bf16[9,32,256]{2,1,0:T(8,128)(2,1)S(1)}, u32[]{:S(2)}, u32[]{:S(2)}) collective-permute-start(bf16[9,32,256]{2,1,0:T(8,128)(2,1)S(1)} %collective-permute-done.rest_1_), channel_id=1, source_target_pairs={{0,1},{1,0},{2,3},{3,2},{4,5},{5,4},{6,7},{7,6},{8,9},{9,8},{10,11... | collective-permute-start | bytes 442376 | tf_op jit(solution)/shard_map/ppermute | solution.py:348
  19.0 0.0 collective-permute-done.7.rest_8_
  19.0 0.1 collective-permute-start.9
  19.1 0.0 collective-permute-done.1.rest_2_
  19.1 0.0 collective-permute-done.5.rest_6_
  19.1 0.8 %collective-permute-done.6.rest_7_ = bf16[2,9,16,256]{3,2,1,0:T(8,128)(2,1)S(1)} collective-permute-done((bf16[2,9,16,256]{3,2,1,0:T(8,128)(2,1)S(1)}, bf16[2,9,16,256]{3,2,1,0:T(8,128)(2,1)S(1)}, u32[]{:S(2)}, u32[]{:S(2)}) %collective-permute-start.6) | collective-permute-done | bytes 147488 | tf_op jit(solution)/shard_map/ppermute | solution.py:348
  19.9 0.2 collective-permute-done.2.rest_3_
  20.1 0.3 %collective-permute-done.9.rest_19_ = bf16[2,9,16,256]{3,2,1,0:T(8,128)(2,1)S(1)} collective-permute-done((bf16[2,9,16,256]{3,2,1,0:T(8,128)(2,1)S(1)}, bf16[2,9,16,256]{3,2,1,0:T(8,128)(2,1)S(1)}, u32[]{:S(2)}, u32[]{:S(2)}) %collective-permute-start.9) | collective-permute-done | bytes 147488 | tf_op jit(solution)/shard_map/ppermute | solution.py:348
  20.4 0.0 copy-done.5
  20.4 0.0 copy-done.6
  20.4 0.0 copy-done.7
  20.4 0.0 copy-done.8
  20.4 4.6 %score_pair.1 = f32[1,128]{1,0:T(1,128)S(1)} custom-call(s32[1,128]{1,0:T(1,128)S(1)} %get-tuple-element.19.qlen_ref, s32[1,128]{1,0:T(1,128)S(1)} %get-tuple-element.20.clen_ref, bf16[9,32,256]{2,1,0:T(8,128)(2,1)S(1)} %get-tuple-element.21.rest_0_, bf16[9,32,256]{2,1,0:T(8,128)(2,1)S(1)} %collective-permute-done.rest_1_, ...), custom_call_target="tpu_custom_call" | custom-call | flops 2000000000 | bytes 8000000 | tf_op jit(solution)/shard_map/score_pair/pallas_call | solution.py:414
  25.0 0.3 collective-permute-start.12
  25.3 1.5 %collective-permute-start.11 = (f32[1,128]{1,0:T(1,128)S(1)}, f32[1,128]{1,0:T(1,128)S(1)}, u32[]{:S(2)}, u32[]{:S(2)}) collective-permute-start(f32[1,128]{1,0:T(1,128)S(1)} %score_pair.1), channel_id=1, source_target_pairs={{0,2},{1,3},{2,0},{3,1},{4,6},{5,7},{6,4},{7,5},{8,10},{9,11},{10,... | collective-permute-start | bytes 1544 | tf_op jit(solution)/shard_map/ppermute | solution.py:348
  26.8 0.2 collective-permute-start.10
  27.0 0.0 collective-permute-done.12
  27.0 1.9 %collective-permute-done.11 = f32[1,128]{1,0:T(1,128)S(1)} collective-permute-done((f32[1,128]{1,0:T(1,128)S(1)}, f32[1,128]{1,0:T(1,128)S(1)}, u32[]{:S(2)}, u32[]{:S(2)}) %collective-permute-start.11) | collective-permute-done | bytes 544 | tf_op jit(solution)/shard_map/ppermute | solution.py:348
  28.8 0.9 %collective-permute-done.10 = f32[1,128]{1,0:T(1,128)S(1)} collective-permute-done((f32[1,128]{1,0:T(1,128)S(1)}, f32[1,128]{1,0:T(1,128)S(1)}, u32[]{:S(2)}, u32[]{:S(2)}) %collective-permute-start.10) | collective-permute-done | bytes 544 | tf_op jit(solution)/shard_map/ppermute | solution.py:348
  29.8 0.5 %add_add_fusion = f32[1,128]{1,0:T(1,128)} fusion(f32[1,128]{1,0:T(1,128)S(1)} %collective-permute-done.12, f32[1,128]{1,0:T(1,128)S(1)} %collective-permute-done.11, f32[1,128]{1,0:T(1,128)S(1)} %score_pair.1, f32[1,128]{1,0:T(1,128)S(1)} %collective-permute-done.10), kind=kLoop, calls=%fused_computation | loop fusion | flops 384 | bytes 2560 | tf_op jit(solution)/shard_map/add | solution.py:445
Async XLA Ops:
  0.0 13.2 %copy-start.2 = (s32[8,4]{0,1:T(4,128)S(1)}, s32[8,4]{0,1:T(4,128)}, u32[]{:S(2)}) copy-start(s32[8,4]{0,1:T(4,128)} %param.15) | copy-start | bytes 388
  0.0 13.2 %copy-start = (f32[3,3,64,128]{3,2,1,0:T(8,128)S(1)}, f32[3,3,64,128]{3,2,1,0:T(8,128)}, u32[]{:S(2)}) copy-start(f32[3,3,64,128]{3,2,1,0:T(8,128)} %param.22) | copy-start | bytes 884740
  0.0 13.2 %copy-start.1 = (f32[3,3,32,64]{3,2,1,0:T(8,128)S(1)}, f32[3,3,32,64]{3,2,1,0:T(8,128)}, u32[]{:S(2)}) copy-start(f32[3,3,32,64]{3,2,1,0:T(8,128)} %param.20) | copy-start | bytes 221188
  0.0 13.2 %copy-start.3 = (f32[3,3,1,32]{3,2,1,0:T(1,128)S(1)}, f32[3,3,1,32]{3,2,1,0:T(1,128)}, u32[]{:S(2)}) copy-start(f32[3,3,1,32]{3,2,1,0:T(1,128)} %param.18) | copy-start | bytes 3460
  0.0 13.2 %copy-start.4 = (s32[32]{0:T(128)S(1)}, s32[32]{0:T(128)}, u32[]{:S(2)}) copy-start(s32[32]{0:T(128)} %clen_ref.1) | copy-start | bytes 388
  0.0 20.4 %copy-start.5 = (f32[32]{0:T(128)S(1)}, f32[32]{0:T(128)}, u32[]{:S(2)}) copy-start(f32[32]{0:T(128)} %param.19) | copy-start | bytes 388
  0.0 20.4 %copy-start.6 = (f32[64]{0:T(128)S(1)}, f32[64]{0:T(128)}, u32[]{:S(2)}) copy-start(f32[64]{0:T(128)} %param.21) | copy-start | bytes 772
  0.0 20.4 %copy-start.7 = (f32[128]{0:T(128)S(1)}, f32[128]{0:T(128)}, u32[]{:S(2)}) copy-start(f32[128]{0:T(128)} %param.23) | copy-start | bytes 1540
  0.0 20.4 %copy-start.8 = (f32[1,1,128,1]{2,3,1,0:T(1,128)S(1)}, f32[1,1,128,1]{2,3,1,0:T(1,128)}, u32[]{:S(2)}) copy-start(f32[1,1,128,1]{2,3,1,0:T(1,128)} %param.24) | copy-start | bytes 1540
  2.1 13.7 %collective-permute-start.8 = (bf16[2,9,16,256]{3,2,1,0:T(8,128)(2,1)S(1)}, bf16[2,9,16,256]{3,2,1,0:T(8,128)(2,1)S(1)}, u32[]{:S(2)}, u32[]{:S(2)}) collective-permute-start(bf16[2,9,16,256]{3,2,1,0:T(8,128)(2,1)S(1)} %get-tuple-element.26), channel_id=1, source_target_pairs={{0,20},{1,25},{2,22},{3,27},{4,16},{5,29},{6,18},{7,31},{8,28},{9,... | collective-permute-start | bytes 442376 | tf_op jit(solution)/shard_map/ppermute | solution.py:370
  7.2 8.8 %collective-permute-start.3 = (bf16[2,9,16,256]{3,2,1,0:T(8,128)(2,1)S(1)}, bf16[2,9,16,256]{3,2,1,0:T(8,128)(2,1)S(1)}, u32[]{:S(2)}, u32[]{:S(2)}) collective-permute-start(bf16[2,9,16,256]{3,2,1,0:T(8,128)(2,1)S(1)} %get-tuple-element.22), channel_id=1, source_target_pairs={{0,12},{1,9},{2,14},{3,11},{4,8},{5,13},{6,10},{7,15},{8,4},{9,1},... | collective-permute-start | bytes 442376 | tf_op jit(solution)/shard_map/ppermute | solution.py:370
  8.7 9.8 %collective-permute-start.4 = (bf16[2,9,16,256]{3,2,1,0:T(8,128)(2,1)S(1)}, bf16[2,9,16,256]{3,2,1,0:T(8,128)(2,1)S(1)}, u32[]{:S(2)}, u32[]{:S(2)}) collective-permute-start(bf16[2,9,16,256]{3,2,1,0:T(8,128)(2,1)S(1)} %get-tuple-element.23), channel_id=1, source_target_pairs={{0,28},{1,17},{2,30},{3,19},{4,24},{5,21},{6,26},{7,23},{8,20},{9,... | collective-permute-start | bytes 442376 | tf_op jit(solution)/shard_map/ppermute | solution.py:370
  9.9 8.7 %collective-permute-start = (bf16[9,32,256]{2,1,0:T(8,128)(2,1)S(1)}, bf16[9,32,256]{2,1,0:T(8,128)(2,1)S(1)}, u32[]{:S(2)}, u32[]{:S(2)}) collective-permute-start(bf16[9,32,256]{2,1,0:T(8,128)(2,1)S(1)} %get-tuple-element.21.rest_0_), channel_id=1, source_target_pairs={{0,2},{1,3},{2,0},{3,1},{4,6},{5,7},{6,4},{7,5},{8,10},{9,11},{10,... | collective-permute-start | bytes 442376 | tf_op jit(solution)/shard_map/ppermute | solution.py:348
  11.4 7.7 %collective-permute-start.7 = (bf16[9,16,256]{2,1,0:T(8,128)(2,1)S(1)}, bf16[9,16,256]{2,1,0:T(8,128)(2,1)S(1)}, u32[]{:S(2)}, u32[]{:S(2)}) collective-permute-start(bf16[9,16,256]{2,1,0:T(8,128)(2,1)S(1)} %get-tuple-element.24), channel_id=1, source_target_pairs={{0,4},{4,0},{8,12},{12,8},{16,20},{20,16},{24,28},{28,24},{1,5},{5... | collective-permute-start | bytes 221192 | tf_op jit(solution)/shard_map/ppermute | solution.py:386
  15.9 3.2 %collective-permute-start.1 = (bf16[9,32,256]{2,1,0:T(8,128)(2,1)S(1)}, bf16[9,32,256]{2,1,0:T(8,128)(2,1)S(1)}, u32[]{:S(2)}, u32[]{:S(2)}) collective-permute-start(bf16[9,32,256]{2,1,0:T(8,128)(2,1)S(1)} %get-tuple-element.21.rest_0_), channel_id=1, source_target_pairs={{0,1},{1,0},{2,3},{3,2},{4,5},{5,4},{6,7},{7,6},{8,9},{9,8},{10,11... | collective-permute-start | bytes 442376 | tf_op jit(solution)/shard_map/ppermute | solution.py:348
  16.0 3.1 %collective-permute-start.5 = (bf16[2,9,16,256]{3,2,1,0:T(8,128)(2,1)S(1)}, bf16[2,9,16,256]{3,2,1,0:T(8,128)(2,1)S(1)}, u32[]{:S(2)}, u32[]{:S(2)}) collective-permute-start(bf16[2,9,16,256]{3,2,1,0:T(8,128)(2,1)S(1)} %collective-permute-done.3.rest_4_), channel_id=1, source_target_pairs={{0,1},{1,0},{2,3},{3,2},{4,5},{5,4},{6,7},{7,6},{8,9},{9,8},{10,11... | collective-permute-start | bytes 442376 | tf_op jit(solution)/shard_map/ppermute | solution.py:348
  18.5 1.4 %collective-permute-start.6 = (bf16[2,9,16,256]{3,2,1,0:T(8,128)(2,1)S(1)}, bf16[2,9,16,256]{3,2,1,0:T(8,128)(2,1)S(1)}, u32[]{:S(2)}, u32[]{:S(2)}) collective-permute-start(bf16[2,9,16,256]{3,2,1,0:T(8,128)(2,1)S(1)} %collective-permute-done.4.rest_5_), channel_id=1, source_target_pairs={{0,1},{1,0},{2,3},{3,2},{4,5},{5,4},{6,7},{7,6},{8,9},{9,8},{10,11... | collective-permute-start | bytes 442376 | tf_op jit(solution)/shard_map/ppermute | solution.py:348
  18.6 1.5 %collective-permute-start.2 = (bf16[9,32,256]{2,1,0:T(8,128)(2,1)S(1)}, bf16[9,32,256]{2,1,0:T(8,128)(2,1)S(1)}, u32[]{:S(2)}, u32[]{:S(2)}) collective-permute-start(bf16[9,32,256]{2,1,0:T(8,128)(2,1)S(1)} %collective-permute-done.rest_1_), channel_id=1, source_target_pairs={{0,1},{1,0},{2,3},{3,2},{4,5},{5,4},{6,7},{7,6},{8,9},{9,8},{10,11... | collective-permute-start | bytes 442376 | tf_op jit(solution)/shard_map/ppermute | solution.py:348
  19.0 1.4 %collective-permute-start.9 = (bf16[2,9,16,256]{3,2,1,0:T(8,128)(2,1)S(1)}, bf16[2,9,16,256]{3,2,1,0:T(8,128)(2,1)S(1)}, u32[]{:S(2)}, u32[]{:S(2)}) collective-permute-start(bf16[2,9,16,256]{3,2,1,0:T(8,128)(2,1)S(1)} %collective-permute-done.8.rest_18_), channel_id=1, source_target_pairs={{0,1},{1,0},{2,3},{3,2},{4,5},{5,4},{6,7},{7,6},{8,9},{9,8},{10,11... | collective-permute-start | bytes 442376 | tf_op jit(solution)/shard_map/ppermute | solution.py:348
  25.0 1.9 %collective-permute-start.12 = (f32[1,128]{1,0:T(1,128)S(1)}, f32[1,128]{1,0:T(1,128)S(1)}, u32[]{:S(2)}, u32[]{:S(2)}) collective-permute-start(f32[1,128]{1,0:T(1,128)S(1)} %score_pair.1), channel_id=1, source_target_pairs={{0,1},{1,0},{2,3},{3,2},{4,5},{5,4},{6,7},{7,6},{8,9},{9,8},{10,11... | collective-permute-start | bytes 1544 | tf_op jit(solution)/shard_map/ppermute | solution.py:348
  25.3 3.5 %collective-permute-start.11 = (f32[1,128]{1,0:T(1,128)S(1)}, f32[1,128]{1,0:T(1,128)S(1)}, u32[]{:S(2)}, u32[]{:S(2)}) collective-permute-start(f32[1,128]{1,0:T(1,128)S(1)} %score_pair.1), channel_id=1, source_target_pairs={{0,2},{1,3},{2,0},{3,1},{4,6},{5,7},{6,4},{7,5},{8,10},{9,11},{10,... | collective-permute-start | bytes 1544 | tf_op jit(solution)/shard_map/ppermute | solution.py:348
  26.8 3.0 %collective-permute-start.10 = (f32[1,128]{1,0:T(1,128)S(1)}, f32[1,128]{1,0:T(1,128)S(1)}, u32[]{:S(2)}, u32[]{:S(2)}) collective-permute-start(f32[1,128]{1,0:T(1,128)S(1)} %score_pair.1), channel_id=1, source_target_pairs={{0,3},{1,2},{2,1},{3,0},{4,7},{5,6},{6,5},{7,4},{8,11},{9,10},{10,... | collective-permute-start | bytes 1544 | tf_op jit(solution)/shard_map/ppermute | solution.py:348

commit v7 on v6

--- a/solution.py
+++ b/solution.py
@@ -217,6 +217,7 @@
     windows = frames // 8
     rolled = [pltpu.roll(ordered, 8 * m + 1, 1) for m in range(16)]
     lane = lax.broadcasted_iota(jnp.int32, (frames, LANES), 1)
+    chunks = []
     for n in range(windows):
         field = None
         for slot in range(5, -1, -1):
@@ -231,13 +232,14 @@
         low = jnp.where(lane < 48, field - high.astype(F32), field).astype(BF16)
         x1[n * frames : (n + 1) * frames, 0:LANES] = high
         x1[n * frames : (n + 1) * frames, LANES : 2 * LANES] = low
-    made = dot(x1[...], w1_ref[...])
-    made = jnp.maximum(made[:, :LANES], made[:, LANES:])
+        if n % 4 == 3:
+            made = dot(x1[(n - 3) * frames : (n + 1) * frames, :], w1_ref[...])
+            chunks.append(jnp.maximum(made[:, :LANES], made[:, LANES:]))
     bias_one = jnp.concatenate([b1_ref[...]] * 4, axis=1)
     bias_two = jnp.concatenate([b2_ref[...]] * 2, axis=1)
     first = []
     for n in range(windows):
-        here = made[n * frames : (n + 1) * frames]
+        here = chunks[n // 4][n % 4 * frames : (n % 4 + 1) * frames]
         halves = []
         for e in range(2):
             pooled = jnp.maximum(

time: 30.7 us -> 30.6 us (level)
  no operation moved by 1% of the time
where the time goes in v7:
time: 30.6 us; the launch traced here: 30.1 us
  starting transfers between devices  12.7 us (42%)
  Pallas kernels  7.75 us (25%)
  waiting for transfers between devices  7.74 us (25%)
  between operations  1.42 us (5%)
  other arithmetic  0.52 us (2%)
    ppermute x3, starting transfers between devices, cross(): return lax.ppermute(sent[at], ('pb', 'slab'), moves)  7.77 us
    pallas_call x1, Pallas kernels, per_device(): pl.pallas_call(functools.partial(score_kernel, rounds, len(blocks), order...  4.46 us
    ppermute x9, starting transfers between devices, swap(): return lax.ppermute(x, 'slab', [(s, s ^ k) for s in range(n_slab)])  4.41 us
    ppermute x9, waiting for transfers between devices, swap(): return lax.ppermute(x, 'slab', [(s, s ^ k) for s in range(n_slab)])  4.1 us
    ppermute x3, waiting for transfers between devices, cross(): return lax.ppermute(sent[at], ('pb', 'slab'), moves)  3.63 us
    pallas_call x1, Pallas kernels, per_device(): pl.pallas_call(functools.partial(pick_kernel, rounds), out_shape=[jax.Sha...  2.06 us
    pallas_call x1, Pallas kernels, per_device(): pl.pallas_call(weight_kernel, out_shape=[jax.ShapeDtypeStruct((rows, 256)...  1.22 us
  transfers between devices with their start and end apart: 13, of which 8 were waited for; matrix products, arithmetic and copies ran while one was open for 0% of the time, Pallas kernels for 4%

profile of v7, /device:TPU:0, one launch (start us, length us, event | category | flops | bytes accessed | tf_op | source)
XLA Modules:
  0.0 30.1 jit_solution(13389046587432137677)
XLA Ops:
  0.0 0.0 copy-start.2
  0.0 0.0 copy-start
  0.0 0.0 copy-start.1
  0.0 0.0 copy-start.3
  0.0 0.0 copy-start.4
  0.0 0.0 copy-start.5
  0.0 0.0 copy-start.6
  0.0 0.0 copy-start.7
  0.0 0.0 copy-start.8
  0.1 2.1 %pick_bands.1 = (bf16[2,9,16,256]{3,2,1,0:T(8,128)(2,1)S(1)}, bf16[2,9,16,256]{3,2,1,0:T(8,128)(2,1)S(1)}, bf16[2,9,16,256]{3,2,1,0:T(8,128)(2,1)S(1)}, bf16[9,1...) custom-call(s32[4,8]{1,0:T(4,128)} %bitcast.15, ...), custom_call_target="tpu_custom_call" | custom-call | tf_op jit(solution)/shard_map/pick_bands/pallas_call | solution.py:356
  2.1 5.1 %collective-permute-start.8 = (bf16[2,9,16,256]{3,2,1,0:T(8,128)(2,1)S(1)}, bf16[2,9,16,256]{3,2,1,0:T(8,128)(2,1)S(1)}, u32[]{:S(2)}, u32[]{:S(2)}) collective-permute-start(bf16[2,9,16,256]{3,2,1,0:T(8,128)(2,1)S(1)} %get-tuple-element.26), channel_id=1, source_target_pairs={{0,20},{1,25},{2,22},{3,27},{4,16},{5,29},{6,18},{7,31},{8,28},{9,... | collective-permute-start | bytes 442376 | tf_op jit(solution)/shard_map/ppermute | solution.py:372
  7.2 1.5 %collective-permute-start.3 = (bf16[2,9,16,256]{3,2,1,0:T(8,128)(2,1)S(1)}, bf16[2,9,16,256]{3,2,1,0:T(8,128)(2,1)S(1)}, u32[]{:S(2)}, u32[]{:S(2)}) collective-permute-start(bf16[2,9,16,256]{3,2,1,0:T(8,128)(2,1)S(1)} %get-tuple-element.22), channel_id=1, source_target_pairs={{0,12},{1,9},{2,14},{3,11},{4,8},{5,13},{6,10},{7,15},{8,4},{9,1},... | collective-permute-start | bytes 442376 | tf_op jit(solution)/shard_map/ppermute | solution.py:372
  8.7 1.2 %collective-permute-start.4 = (bf16[2,9,16,256]{3,2,1,0:T(8,128)(2,1)S(1)}, bf16[2,9,16,256]{3,2,1,0:T(8,128)(2,1)S(1)}, u32[]{:S(2)}, u32[]{:S(2)}) collective-permute-start(bf16[2,9,16,256]{3,2,1,0:T(8,128)(2,1)S(1)} %get-tuple-element.23), channel_id=1, source_target_pairs={{0,28},{1,17},{2,30},{3,19},{4,24},{5,21},{6,26},{7,23},{8,20},{9,... | collective-permute-start | bytes 442376 | tf_op jit(solution)/shard_map/ppermute | solution.py:372
  9.9 1.5 %collective-permute-start = (bf16[9,32,256]{2,1,0:T(8,128)(2,1)S(1)}, bf16[9,32,256]{2,1,0:T(8,128)(2,1)S(1)}, u32[]{:S(2)}, u32[]{:S(2)}) collective-permute-start(bf16[9,32,256]{2,1,0:T(8,128)(2,1)S(1)} %get-tuple-element.21.rest_0_), channel_id=1, source_target_pairs={{0,2},{1,3},{2,0},{3,1},{4,6},{5,7},{6,4},{7,5},{8,10},{9,11},{10,... | collective-permute-start | bytes 442376 | tf_op jit(solution)/shard_map/ppermute | solution.py:350
  11.4 0.5 %collective-permute-start.7 = (bf16[9,16,256]{2,1,0:T(8,128)(2,1)S(1)}, bf16[9,16,256]{2,1,0:T(8,128)(2,1)S(1)}, u32[]{:S(2)}, u32[]{:S(2)}) collective-permute-start(bf16[9,16,256]{2,1,0:T(8,128)(2,1)S(1)} %get-tuple-element.24), channel_id=1, source_target_pairs={{0,4},{4,0},{8,12},{12,8},{16,20},{20,16},{24,28},{28,24},{1,5},{5... | collective-permute-start | bytes 221192 | tf_op jit(solution)/shard_map/ppermute | solution.py:388
  13.2 0.0 copy-done.2
  13.2 0.0 copy-done
  13.2 0.0 copy-done.1
  13.2 0.0 copy-done.3
  13.2 0.0 copy-done.4
  13.2 1.2 %lay_out_kernels.1 = (bf16[256,256]{1,0:T(8,128)(2,1)S(1)}, bf16[2560,256]{1,0:T(8,128)(2,1)S(1)}, bf16[2304,256]{1,0:T(8,128)(2,1)S(1)}, s32[1,128]{1,0:T(1,128...) custom-call(f32[9,1,32]{2,1,0:T(1,128)S(1)} %bitcast.17, f32[9,32,64]{2,1,0:T(8,128)S(1)} %bitcast.14, ...), custom_call_target="tpu_custom_call" | custom-call | flops 2000000 | bytes 6000000 | tf_op jit(solution)/shard_map/lay_out_kernels/pallas_call | solution.py:391
  14.5 1.4 %collective-permute-done.8.rest_18_ = bf16[2,9,16,256]{3,2,1,0:T(8,128)(2,1)S(1)} collective-permute-done((bf16[2,9,16,256]{3,2,1,0:T(8,128)(2,1)S(1)}, bf16[2,9,16,256]{3,2,1,0:T(8,128)(2,1)S(1)}, u32[]{:S(2)}, u32[]{:S(2)}) %collective-permute-start.8) | collective-permute-done | bytes 147488 | tf_op jit(solution)/shard_map/ppermute | solution.py:372
  15.9 0.0 collective-permute-start.1
  15.9 0.1 collective-permute-done.3.rest_4_
  16.0 0.4 %collective-permute-start.5 = (bf16[2,9,16,256]{3,2,1,0:T(8,128)(2,1)S(1)}, bf16[2,9,16,256]{3,2,1,0:T(8,128)(2,1)S(1)}, u32[]{:S(2)}, u32[]{:S(2)}) collective-permute-start(bf16[2,9,16,256]{3,2,1,0:T(8,128)(2,1)S(1)} %collective-permute-done.3.rest_4_), channel_id=1, source_target_pairs={{0,1},{1,0},{2,3},{3,2},{4,5},{5,4},{6,7},{7,6},{8,9},{9,8},{10,11... | collective-permute-start | bytes 442376 | tf_op jit(solution)/shard_map/ppermute | solution.py:350
  16.4 2.1 %collective-permute-done.4.rest_5_ = bf16[2,9,16,256]{3,2,1,0:T(8,128)(2,1)S(1)} collective-permute-done((bf16[2,9,16,256]{3,2,1,0:T(8,128)(2,1)S(1)}, bf16[2,9,16,256]{3,2,1,0:T(8,128)(2,1)S(1)}, u32[]{:S(2)}, u32[]{:S(2)}) %collective-permute-start.4) | collective-permute-done | bytes 147488 | tf_op jit(solution)/shard_map/ppermute | solution.py:372
  18.5 0.1 collective-permute-start.6
  18.6 0.0 collective-permute-done.rest_1_
  18.6 0.5 %collective-permute-start.2 = (bf16[9,32,256]{2,1,0:T(8,128)(2,1)S(1)}, bf16[9,32,256]{2,1,0:T(8,128)(2,1)S(1)}, u32[]{:S(2)}, u32[]{:S(2)}) collective-permute-start(bf16[9,32,256]{2,1,0:T(8,128)(2,1)S(1)} %collective-permute-done.rest_1_), channel_id=1, source_target_pairs={{0,1},{1,0},{2,3},{3,2},{4,5},{5,4},{6,7},{7,6},{8,9},{9,8},{10,11... | collective-permute-start | bytes 442376 | tf_op jit(solution)/shard_map/ppermute | solution.py:350
  19.0 0.0 collective-permute-done.7.rest_8_
  19.0 0.1 collective-permute-start.9
  19.1 0.0 collective-permute-done.1.rest_2_
  19.1 0.0 collective-permute-done.5.rest_6_
  19.1 0.8 %collective-permute-done.6.rest_7_ = bf16[2,9,16,256]{3,2,1,0:T(8,128)(2,1)S(1)} collective-permute-done((bf16[2,9,16,256]{3,2,1,0:T(8,128)(2,1)S(1)}, bf16[2,9,16,256]{3,2,1,0:T(8,128)(2,1)S(1)}, u32[]{:S(2)}, u32[]{:S(2)}) %collective-permute-start.6) | collective-permute-done | bytes 147488 | tf_op jit(solution)/shard_map/ppermute | solution.py:350
  19.9 0.2 collective-permute-done.2.rest_3_
  20.1 0.3 %collective-permute-done.9.rest_19_ = bf16[2,9,16,256]{3,2,1,0:T(8,128)(2,1)S(1)} collective-permute-done((bf16[2,9,16,256]{3,2,1,0:T(8,128)(2,1)S(1)}, bf16[2,9,16,256]{3,2,1,0:T(8,128)(2,1)S(1)}, u32[]{:S(2)}, u32[]{:S(2)}) %collective-permute-start.9) | collective-permute-done | bytes 147488 | tf_op jit(solution)/shard_map/ppermute | solution.py:350
  20.4 0.0 copy-done.5
  20.4 0.0 copy-done.6
  20.4 0.0 copy-done.7
  20.4 0.0 copy-done.8
  20.4 4.5 %score_pair.1 = f32[1,128]{1,0:T(1,128)S(1)} custom-call(s32[1,128]{1,0:T(1,128)S(1)} %get-tuple-element.19.qlen_ref, s32[1,128]{1,0:T(1,128)S(1)} %get-tuple-element.20.clen_ref, bf16[9,32,256]{2,1,0:T(8,128)(2,1)S(1)} %get-tuple-element.21.rest_0_, bf16[9,32,256]{2,1,0:T(8,128)(2,1)S(1)} %collective-permute-done.rest_1_, ...), custom_call_target="tpu_custom_call" | custom-call | flops 2000000000 | bytes 8000000 | tf_op jit(solution)/shard_map/score_pair/pallas_call | solution.py:416
  24.9 0.3 collective-permute-start.12
  25.2 1.5 %collective-permute-start.11 = (f32[1,128]{1,0:T(1,128)S(1)}, f32[1,128]{1,0:T(1,128)S(1)}, u32[]{:S(2)}, u32[]{:S(2)}) collective-permute-start(f32[1,128]{1,0:T(1,128)S(1)} %score_pair.1), channel_id=1, source_target_pairs={{0,2},{1,3},{2,0},{3,1},{4,6},{5,7},{6,4},{7,5},{8,10},{9,11},{10,... | collective-permute-start | bytes 1544 | tf_op jit(solution)/shard_map/ppermute | solution.py:350
  26.7 0.2 collective-permute-start.10
  26.8 0.0 collective-permute-done.12
  26.8 1.9 %collective-permute-done.11 = f32[1,128]{1,0:T(1,128)S(1)} collective-permute-done((f32[1,128]{1,0:T(1,128)S(1)}, f32[1,128]{1,0:T(1,128)S(1)}, u32[]{:S(2)}, u32[]{:S(2)}) %collective-permute-start.11) | collective-permute-done | bytes 544 | tf_op jit(solution)/shard_map/ppermute | solution.py:350
  28.7 0.9 %collective-permute-done.10 = f32[1,128]{1,0:T(1,128)S(1)} collective-permute-done((f32[1,128]{1,0:T(1,128)S(1)}, f32[1,128]{1,0:T(1,128)S(1)}, u32[]{:S(2)}, u32[]{:S(2)}) %collective-permute-start.10) | collective-permute-done | bytes 544 | tf_op jit(solution)/shard_map/ppermute | solution.py:350
  29.6 0.5 %add_add_fusion = f32[1,128]{1,0:T(1,128)} fusion(f32[1,128]{1,0:T(1,128)S(1)} %collective-permute-done.12, f32[1,128]{1,0:T(1,128)S(1)} %collective-permute-done.11, f32[1,128]{1,0:T(1,128)S(1)} %score_pair.1, f32[1,128]{1,0:T(1,128)S(1)} %collective-permute-done.10), kind=kLoop, calls=%fused_computation | loop fusion | flops 384 | bytes 2560 | tf_op jit(solution)/shard_map/add | solution.py:447
Async XLA Ops:
  0.0 13.2 %copy-start.2 = (s32[8,4]{0,1:T(4,128)S(1)}, s32[8,4]{0,1:T(4,128)}, u32[]{:S(2)}) copy-start(s32[8,4]{0,1:T(4,128)} %param.15) | copy-start | bytes 388
  0.0 13.2 %copy-start = (f32[3,3,64,128]{3,2,1,0:T(8,128)S(1)}, f32[3,3,64,128]{3,2,1,0:T(8,128)}, u32[]{:S(2)}) copy-start(f32[3,3,64,128]{3,2,1,0:T(8,128)} %param.22) | copy-start | bytes 884740
  0.0 13.2 %copy-start.1 = (f32[3,3,32,64]{3,2,1,0:T(8,128)S(1)}, f32[3,3,32,64]{3,2,1,0:T(8,128)}, u32[]{:S(2)}) copy-start(f32[3,3,32,64]{3,2,1,0:T(8,128)} %param.20) | copy-start | bytes 221188
  0.0 13.2 %copy-start.3 = (f32[3,3,1,32]{3,2,1,0:T(1,128)S(1)}, f32[3,3,1,32]{3,2,1,0:T(1,128)}, u32[]{:S(2)}) copy-start(f32[3,3,1,32]{3,2,1,0:T(1,128)} %param.18) | copy-start | bytes 3460
  0.0 13.2 %copy-start.4 = (s32[32]{0:T(128)S(1)}, s32[32]{0:T(128)}, u32[]{:S(2)}) copy-start(s32[32]{0:T(128)} %clen_ref.1) | copy-start | bytes 388
  0.0 20.4 %copy-start.5 = (f32[32]{0:T(128)S(1)}, f32[32]{0:T(128)}, u32[]{:S(2)}) copy-start(f32[32]{0:T(128)} %param.19) | copy-start | bytes 388
  0.0 20.4 %copy-start.6 = (f32[64]{0:T(128)S(1)}, f32[64]{0:T(128)}, u32[]{:S(2)}) copy-start(f32[64]{0:T(128)} %param.21) | copy-start | bytes 772
  0.0 20.4 %copy-start.7 = (f32[128]{0:T(128)S(1)}, f32[128]{0:T(128)}, u32[]{:S(2)}) copy-start(f32[128]{0:T(128)} %param.23) | copy-start | bytes 1540
  0.0 20.4 %copy-start.8 = (f32[1,1,128,1]{2,3,1,0:T(1,128)S(1)}, f32[1,1,128,1]{2,3,1,0:T(1,128)}, u32[]{:S(2)}) copy-start(f32[1,1,128,1]{2,3,1,0:T(1,128)} %param.24) | copy-start | bytes 1540
  2.1 13.7 %collective-permute-start.8 = (bf16[2,9,16,256]{3,2,1,0:T(8,128)(2,1)S(1)}, bf16[2,9,16,256]{3,2,1,0:T(8,128)(2,1)S(1)}, u32[]{:S(2)}, u32[]{:S(2)}) collective-permute-start(bf16[2,9,16,256]{3,2,1,0:T(8,128)(2,1)S(1)} %get-tuple-element.26), channel_id=1, source_target_pairs={{0,20},{1,25},{2,22},{3,27},{4,16},{5,29},{6,18},{7,31},{8,28},{9,... | collective-permute-start | bytes 442376 | tf_op jit(solution)/shard_map/ppermute | solution.py:372
  7.2 8.8 %collective-permute-start.3 = (bf16[2,9,16,256]{3,2,1,0:T(8,128)(2,1)S(1)}, bf16[2,9,16,256]{3,2,1,0:T(8,128)(2,1)S(1)}, u32[]{:S(2)}, u32[]{:S(2)}) collective-permute-start(bf16[2,9,16,256]{3,2,1,0:T(8,128)(2,1)S(1)} %get-tuple-element.22), channel_id=1, source_target_pairs={{0,12},{1,9},{2,14},{3,11},{4,8},{5,13},{6,10},{7,15},{8,4},{9,1},... | collective-permute-start | bytes 442376 | tf_op jit(solution)/shard_map/ppermute | solution.py:372
  8.7 9.8 %collective-permute-start.4 = (bf16[2,9,16,256]{3,2,1,0:T(8,128)(2,1)S(1)}, bf16[2,9,16,256]{3,2,1,0:T(8,128)(2,1)S(1)}, u32[]{:S(2)}, u32[]{:S(2)}) collective-permute-start(bf16[2,9,16,256]{3,2,1,0:T(8,128)(2,1)S(1)} %get-tuple-element.23), channel_id=1, source_target_pairs={{0,28},{1,17},{2,30},{3,19},{4,24},{5,21},{6,26},{7,23},{8,20},{9,... | collective-permute-start | bytes 442376 | tf_op jit(solution)/shard_map/ppermute | solution.py:372
  9.9 8.7 %collective-permute-start = (bf16[9,32,256]{2,1,0:T(8,128)(2,1)S(1)}, bf16[9,32,256]{2,1,0:T(8,128)(2,1)S(1)}, u32[]{:S(2)}, u32[]{:S(2)}) collective-permute-start(bf16[9,32,256]{2,1,0:T(8,128)(2,1)S(1)} %get-tuple-element.21.rest_0_), channel_id=1, source_target_pairs={{0,2},{1,3},{2,0},{3,1},{4,6},{5,7},{6,4},{7,5},{8,10},{9,11},{10,... | collective-permute-start | bytes 442376 | tf_op jit(solution)/shard_map/ppermute | solution.py:350
  11.4 7.7 %collective-permute-start.7 = (bf16[9,16,256]{2,1,0:T(8,128)(2,1)S(1)}, bf16[9,16,256]{2,1,0:T(8,128)(2,1)S(1)}, u32[]{:S(2)}, u32[]{:S(2)}) collective-permute-start(bf16[9,16,256]{2,1,0:T(8,128)(2,1)S(1)} %get-tuple-element.24), channel_id=1, source_target_pairs={{0,4},{4,0},{8,12},{12,8},{16,20},{20,16},{24,28},{28,24},{1,5},{5... | collective-permute-start | bytes 221192 | tf_op jit(solution)/shard_map/ppermute | solution.py:388
  15.9 3.2 %collective-permute-start.1 = (bf16[9,32,256]{2,1,0:T(8,128)(2,1)S(1)}, bf16[9,32,256]{2,1,0:T(8,128)(2,1)S(1)}, u32[]{:S(2)}, u32[]{:S(2)}) collective-permute-start(bf16[9,32,256]{2,1,0:T(8,128)(2,1)S(1)} %get-tuple-element.21.rest_0_), channel_id=1, source_target_pairs={{0,1},{1,0},{2,3},{3,2},{4,5},{5,4},{6,7},{7,6},{8,9},{9,8},{10,11... | collective-permute-start | bytes 442376 | tf_op jit(solution)/shard_map/ppermute | solution.py:350
  16.0 3.1 %collective-permute-start.5 = (bf16[2,9,16,256]{3,2,1,0:T(8,128)(2,1)S(1)}, bf16[2,9,16,256]{3,2,1,0:T(8,128)(2,1)S(1)}, u32[]{:S(2)}, u32[]{:S(2)}) collective-permute-start(bf16[2,9,16,256]{3,2,1,0:T(8,128)(2,1)S(1)} %collective-permute-done.3.rest_4_), channel_id=1, source_target_pairs={{0,1},{1,0},{2,3},{3,2},{4,5},{5,4},{6,7},{7,6},{8,9},{9,8},{10,11... | collective-permute-start | bytes 442376 | tf_op jit(solution)/shard_map/ppermute | solution.py:350
  18.5 1.4 %collective-permute-start.6 = (bf16[2,9,16,256]{3,2,1,0:T(8,128)(2,1)S(1)}, bf16[2,9,16,256]{3,2,1,0:T(8,128)(2,1)S(1)}, u32[]{:S(2)}, u32[]{:S(2)}) collective-permute-start(bf16[2,9,16,256]{3,2,1,0:T(8,128)(2,1)S(1)} %collective-permute-done.4.rest_5_), channel_id=1, source_target_pairs={{0,1},{1,0},{2,3},{3,2},{4,5},{5,4},{6,7},{7,6},{8,9},{9,8},{10,11... | collective-permute-start | bytes 442376 | tf_op jit(solution)/shard_map/ppermute | solution.py:350
  18.6 1.5 %collective-permute-start.2 = (bf16[9,32,256]{2,1,0:T(8,128)(2,1)S(1)}, bf16[9,32,256]{2,1,0:T(8,128)(2,1)S(1)}, u32[]{:S(2)}, u32[]{:S(2)}) collective-permute-start(bf16[9,32,256]{2,1,0:T(8,128)(2,1)S(1)} %collective-permute-done.rest_1_), channel_id=1, source_target_pairs={{0,1},{1,0},{2,3},{3,2},{4,5},{5,4},{6,7},{7,6},{8,9},{9,8},{10,11... | collective-permute-start | bytes 442376 | tf_op jit(solution)/shard_map/ppermute | solution.py:350
  19.0 1.4 %collective-permute-start.9 = (bf16[2,9,16,256]{3,2,1,0:T(8,128)(2,1)S(1)}, bf16[2,9,16,256]{3,2,1,0:T(8,128)(2,1)S(1)}, u32[]{:S(2)}, u32[]{:S(2)}) collective-permute-start(bf16[2,9,16,256]{3,2,1,0:T(8,128)(2,1)S(1)} %collective-permute-done.8.rest_18_), channel_id=1, source_target_pairs={{0,1},{1,0},{2,3},{3,2},{4,5},{5,4},{6,7},{7,6},{8,9},{9,8},{10,11... | collective-permute-start | bytes 442376 | tf_op jit(solution)/shard_map/ppermute | solution.py:350
  24.9 1.9 %collective-permute-start.12 = (f32[1,128]{1,0:T(1,128)S(1)}, f32[1,128]{1,0:T(1,128)S(1)}, u32[]{:S(2)}, u32[]{:S(2)}) collective-permute-start(f32[1,128]{1,0:T(1,128)S(1)} %score_pair.1), channel_id=1, source_target_pairs={{0,1},{1,0},{2,3},{3,2},{4,5},{5,4},{6,7},{7,6},{8,9},{9,8},{10,11... | collective-permute-start | bytes 1544 | tf_op jit(solution)/shard_map/ppermute | solution.py:350
  25.2 3.5 %collective-permute-start.11 = (f32[1,128]{1,0:T(1,128)S(1)}, f32[1,128]{1,0:T(1,128)S(1)}, u32[]{:S(2)}, u32[]{:S(2)}) collective-permute-start(f32[1,128]{1,0:T(1,128)S(1)} %score_pair.1), channel_id=1, source_target_pairs={{0,2},{1,3},{2,0},{3,1},{4,6},{5,7},{6,4},{7,5},{8,10},{9,11},{10,... | collective-permute-start | bytes 1544 | tf_op jit(solution)/shard_map/ppermute | solution.py:350
  26.7 3.0 %collective-permute-start.10 = (f32[1,128]{1,0:T(1,128)S(1)}, f32[1,128]{1,0:T(1,128)S(1)}, u32[]{:S(2)}, u32[]{:S(2)}) collective-permute-start(f32[1,128]{1,0:T(1,128)S(1)} %score_pair.1), channel_id=1, source_target_pairs={{0,3},{1,2},{2,1},{3,0},{4,7},{5,6},{6,5},{7,4},{8,11},{9,10},{10,... | collective-permute-start | bytes 1544 | tf_op jit(solution)/shard_map/ppermute | solution.py:350

commit v8 on v7

--- a/solution.py
+++ b/solution.py
@@ -281,13 +281,13 @@
                 at = (3 + i) * LANES
                 x2[base : base + half, at : at + LANES] = high
                 x2[base : base + half, 640 + at : 640 + at + LANES] = low
-    for n in range(0, windows, 2):
-        left = x2[n * half : (n + 2) * half, :]
-        made = dot(jnp.concatenate([left, left[:, :640], left[:, :640]], axis=1), w2_ref[...])
-        made = jnp.maximum(made[:, :LANES], made[:, LANES:])
-        for i in range(2):
-            here = jnp.maximum(made[i * half : i * half + quarter], made[i * half + quarter : (i + 1) * half])
-            pooled_two[n + i] = jnp.maximum(here + bias_two, 0.0)
+        if n > 0 and n % 2 == 0:
+            left = x2[(n - 2) * half : n * half, :]
+            made = dot(jnp.concatenate([left, left[:, :640], left[:, :640]], axis=1), w2_ref[...])
+            made = jnp.maximum(made[:, :LANES], made[:, LANES:])
+            for i in range(2):
+                here = jnp.maximum(made[i * half : i * half + quarter], made[i * half + quarter : (i + 1) * half])
+                pooled_two[n - 2 + i] = jnp.maximum(here + bias_two, 0.0)
     second = [pooled_two[n] for n in range(windows)]
 
     moved = shifted(second, 64)

time: 30.6 us -> 30.6 us (level)
  no operation moved by 1% of the time
where the time goes in v8:
time: 30.6 us; the launch traced here: 30.1 us
  starting transfers between devices  12.7 us (42%)
  Pallas kernels  7.75 us (25%)
  waiting for transfers between devices  7.74 us (25%)
  between operations  1.42 us (5%)
  other arithmetic  0.52 us (2%)
    ppermute x3, starting transfers between devices, cross(): return lax.ppermute(sent[at], ('pb', 'slab'), moves)  7.77 us
    pallas_call x1, Pallas kernels, per_device(): pl.pallas_call(functools.partial(score_kernel, rounds, len(blocks), order...  4.46 us
    ppermute x9, starting transfers between devices, swap(): return lax.ppermute(x, 'slab', [(s, s ^ k) for s in range(n_slab)])  4.41 us
    ppermute x9, waiting for transfers between devices, swap(): return lax.ppermute(x, 'slab', [(s, s ^ k) for s in range(n_slab)])  4.1 us
    ppermute x3, waiting for transfers between devices, cross(): return lax.ppermute(sent[at], ('pb', 'slab'), moves)  3.63 us
    pallas_call x1, Pallas kernels, per_device(): pl.pallas_call(functools.partial(pick_kernel, rounds), out_shape=[jax.Sha...  2.06 us
    pallas_call x1, Pallas kernels, per_device(): pl.pallas_call(weight_kernel, out_shape=[jax.ShapeDtypeStruct((rows, 256)...  1.22 us
  transfers between devices with their start and end apart: 13, of which 8 were waited for; matrix products, arithmetic and copies ran while one was open for 0% of the time, Pallas kernels for 4%

profile of v8, /device:TPU:0, one launch (start us, length us, event | category | flops | bytes accessed | tf_op | source)
XLA Modules:
  0.0 30.1 jit_solution(13389046587432137677)
XLA Ops:
  0.0 0.0 copy-start.2
  0.0 0.0 copy-start
  0.0 0.0 copy-start.1
  0.0 0.0 copy-start.3
  0.0 0.0 copy-start.4
  0.0 0.0 copy-start.5
  0.0 0.0 copy-start.6
  0.0 0.0 copy-start.7
  0.0 0.0 copy-start.8
  0.1 2.1 %pick_bands.1 = (bf16[2,9,16,256]{3,2,1,0:T(8,128)(2,1)S(1)}, bf16[2,9,16,256]{3,2,1,0:T(8,128)(2,1)S(1)}, bf16[2,9,16,256]{3,2,1,0:T(8,128)(2,1)S(1)}, bf16[9,1...) custom-call(s32[4,8]{1,0:T(4,128)} %bitcast.15, ...), custom_call_target="tpu_custom_call" | custom-call | tf_op jit(solution)/shard_map/pick_bands/pallas_call | solution.py:356
  2.1 5.1 %collective-permute-start.8 = (bf16[2,9,16,256]{3,2,1,0:T(8,128)(2,1)S(1)}, bf16[2,9,16,256]{3,2,1,0:T(8,128)(2,1)S(1)}, u32[]{:S(2)}, u32[]{:S(2)}) collective-permute-start(bf16[2,9,16,256]{3,2,1,0:T(8,128)(2,1)S(1)} %get-tuple-element.26), channel_id=1, source_target_pairs={{0,20},{1,25},{2,22},{3,27},{4,16},{5,29},{6,18},{7,31},{8,28},{9,... | collective-permute-start | bytes 442376 | tf_op jit(solution)/shard_map/ppermute | solution.py:372
  7.2 1.5 %collective-permute-start.3 = (bf16[2,9,16,256]{3,2,1,0:T(8,128)(2,1)S(1)}, bf16[2,9,16,256]{3,2,1,0:T(8,128)(2,1)S(1)}, u32[]{:S(2)}, u32[]{:S(2)}) collective-permute-start(bf16[2,9,16,256]{3,2,1,0:T(8,128)(2,1)S(1)} %get-tuple-element.22), channel_id=1, source_target_pairs={{0,12},{1,9},{2,14},{3,11},{4,8},{5,13},{6,10},{7,15},{8,4},{9,1},... | collective-permute-start | bytes 442376 | tf_op jit(solution)/shard_map/ppermute | solution.py:372
  8.7 1.2 %collective-permute-start.4 = (bf16[2,9,16,256]{3,2,1,0:T(8,128)(2,1)S(1)}, bf16[2,9,16,256]{3,2,1,0:T(8,128)(2,1)S(1)}, u32[]{:S(2)}, u32[]{:S(2)}) collective-permute-start(bf16[2,9,16,256]{3,2,1,0:T(8,128)(2,1)S(1)} %get-tuple-element.23), channel_id=1, source_target_pairs={{0,28},{1,17},{2,30},{3,19},{4,24},{5,21},{6,26},{7,23},{8,20},{9,... | collective-permute-start | bytes 442376 | tf_op jit(solution)/shard_map/ppermute | solution.py:372
  9.9 1.5 %collective-permute-start = (bf16[9,32,256]{2,1,0:T(8,128)(2,1)S(1)}, bf16[9,32,256]{2,1,0:T(8,128)(2,1)S(1)}, u32[]{:S(2)}, u32[]{:S(2)}) collective-permute-start(bf16[9,32,256]{2,1,0:T(8,128)(2,1)S(1)} %get-tuple-element.21.rest_0_), channel_id=1, source_target_pairs={{0,2},{1,3},{2,0},{3,1},{4,6},{5,7},{6,4},{7,5},{8,10},{9,11},{10,... | collective-permute-start | bytes 442376 | tf_op jit(solution)/shard_map/ppermute | solution.py:350
  11.4 0.5 %collective-permute-start.7 = (bf16[9,16,256]{2,1,0:T(8,128)(2,1)S(1)}, bf16[9,16,256]{2,1,0:T(8,128)(2,1)S(1)}, u32[]{:S(2)}, u32[]{:S(2)}) collective-permute-start(bf16[9,16,256]{2,1,0:T(8,128)(2,1)S(1)} %get-tuple-element.24), channel_id=1, source_target_pairs={{0,4},{4,0},{8,12},{12,8},{16,20},{20,16},{24,28},{28,24},{1,5},{5... | collective-permute-start | bytes 221192 | tf_op jit(solution)/shard_map/ppermute | solution.py:388
  13.2 0.0 copy-done.2
  13.2 0.0 copy-done
  13.2 0.0 copy-done.1
  13.2 0.0 copy-done.3
  13.2 0.0 copy-done.4
  13.2 1.2 %lay_out_kernels.1 = (bf16[256,256]{1,0:T(8,128)(2,1)S(1)}, bf16[2560,256]{1,0:T(8,128)(2,1)S(1)}, bf16[2304,256]{1,0:T(8,128)(2,1)S(1)}, s32[1,128]{1,0:T(1,128...) custom-call(f32[9,1,32]{2,1,0:T(1,128)S(1)} %bitcast.17, f32[9,32,64]{2,1,0:T(8,128)S(1)} %bitcast.14, ...), custom_call_target="tpu_custom_call" | custom-call | flops 2000000 | bytes 6000000 | tf_op jit(solution)/shard_map/lay_out_kernels/pallas_call | solution.py:391
  14.5 1.4 %collective-permute-done.8.rest_18_ = bf16[2,9,16,256]{3,2,1,0:T(8,128)(2,1)S(1)} collective-permute-done((bf16[2,9,16,256]{3,2,1,0:T(8,128)(2,1)S(1)}, bf16[2,9,16,256]{3,2,1,0:T(8,128)(2,1)S(1)}, u32[]{:S(2)}, u32[]{:S(2)}) %collective-permute-start.8) | collective-permute-done | bytes 147488 | tf_op jit(solution)/shard_map/ppermute | solution.py:372
  15.9 0.0 collective-permute-start.1
  15.9 0.1 collective-permute-done.3.rest_4_
  16.0 0.4 %collective-permute-start.5 = (bf16[2,9,16,256]{3,2,1,0:T(8,128)(2,1)S(1)}, bf16[2,9,16,256]{3,2,1,0:T(8,128)(2,1)S(1)}, u32[]{:S(2)}, u32[]{:S(2)}) collective-permute-start(bf16[2,9,16,256]{3,2,1,0:T(8,128)(2,1)S(1)} %collective-permute-done.3.rest_4_), channel_id=1, source_target_pairs={{0,1},{1,0},{2,3},{3,2},{4,5},{5,4},{6,7},{7,6},{8,9},{9,8},{10,11... | collective-permute-start | bytes 442376 | tf_op jit(solution)/shard_map/ppermute | solution.py:350
  16.4 2.1 %collective-permute-done.4.rest_5_ = bf16[2,9,16,256]{3,2,1,0:T(8,128)(2,1)S(1)} collective-permute-done((bf16[2,9,16,256]{3,2,1,0:T(8,128)(2,1)S(1)}, bf16[2,9,16,256]{3,2,1,0:T(8,128)(2,1)S(1)}, u32[]{:S(2)}, u32[]{:S(2)}) %collective-permute-start.4) | collective-permute-done | bytes 147488 | tf_op jit(solution)/shard_map/ppermute | solution.py:372
  18.5 0.1 collective-permute-start.6
  18.6 0.0 collective-permute-done.rest_1_
  18.6 0.5 %collective-permute-start.2 = (bf16[9,32,256]{2,1,0:T(8,128)(2,1)S(1)}, bf16[9,32,256]{2,1,0:T(8,128)(2,1)S(1)}, u32[]{:S(2)}, u32[]{:S(2)}) collective-permute-start(bf16[9,32,256]{2,1,0:T(8,128)(2,1)S(1)} %collective-permute-done.rest_1_), channel_id=1, source_target_pairs={{0,1},{1,0},{2,3},{3,2},{4,5},{5,4},{6,7},{7,6},{8,9},{9,8},{10,11... | collective-permute-start | bytes 442376 | tf_op jit(solution)/shard_map/ppermute | solution.py:350
  19.0 0.0 collective-permute-done.7.rest_8_
  19.0 0.1 collective-permute-start.9
  19.1 0.0 collective-permute-done.1.rest_2_
  19.1 0.0 collective-permute-done.5.rest_6_
  19.1 0.8 %collective-permute-done.6.rest_7_ = bf16[2,9,16,256]{3,2,1,0:T(8,128)(2,1)S(1)} collective-permute-done((bf16[2,9,16,256]{3,2,1,0:T(8,128)(2,1)S(1)}, bf16[2,9,16,256]{3,2,1,0:T(8,128)(2,1)S(1)}, u32[]{:S(2)}, u32[]{:S(2)}) %collective-permute-start.6) | collective-permute-done | bytes 147488 | tf_op jit(solution)/shard_map/ppermute | solution.py:350
  19.9 0.2 collective-permute-done.2.rest_3_
  20.1 0.3 %collective-permute-done.9.rest_19_ = bf16[2,9,16,256]{3,2,1,0:T(8,128)(2,1)S(1)} collective-permute-done((bf16[2,9,16,256]{3,2,1,0:T(8,128)(2,1)S(1)}, bf16[2,9,16,256]{3,2,1,0:T(8,128)(2,1)S(1)}, u32[]{:S(2)}, u32[]{:S(2)}) %collective-permute-start.9) | collective-permute-done | bytes 147488 | tf_op jit(solution)/shard_map/ppermute | solution.py:350
  20.4 0.0 copy-done.5
  20.4 0.0 copy-done.6
  20.4 0.0 copy-done.7
  20.4 0.0 copy-done.8
  20.4 4.5 %score_pair.1 = f32[1,128]{1,0:T(1,128)S(1)} custom-call(s32[1,128]{1,0:T(1,128)S(1)} %get-tuple-element.19.qlen_ref, s32[1,128]{1,0:T(1,128)S(1)} %get-tuple-element.20.clen_ref, bf16[9,32,256]{2,1,0:T(8,128)(2,1)S(1)} %get-tuple-element.21.rest_0_, bf16[9,32,256]{2,1,0:T(8,128)(2,1)S(1)} %collective-permute-done.rest_1_, ...), custom_call_target="tpu_custom_call" | custom-call | flops 2000000000 | bytes 8000000 | tf_op jit(solution)/shard_map/score_pair/pallas_call | solution.py:416
  24.9 0.3 collective-permute-start.12
  25.2 1.5 %collective-permute-start.11 = (f32[1,128]{1,0:T(1,128)S(1)}, f32[1,128]{1,0:T(1,128)S(1)}, u32[]{:S(2)}, u32[]{:S(2)}) collective-permute-start(f32[1,128]{1,0:T(1,128)S(1)} %score_pair.1), channel_id=1, source_target_pairs={{0,2},{1,3},{2,0},{3,1},{4,6},{5,7},{6,4},{7,5},{8,10},{9,11},{10,... | collective-permute-start | bytes 1544 | tf_op jit(solution)/shard_map/ppermute | solution.py:350
  26.7 0.2 collective-permute-start.10
  26.8 0.0 collective-permute-done.12
  26.8 1.9 %collective-permute-done.11 = f32[1,128]{1,0:T(1,128)S(1)} collective-permute-done((f32[1,128]{1,0:T(1,128)S(1)}, f32[1,128]{1,0:T(1,128)S(1)}, u32[]{:S(2)}, u32[]{:S(2)}) %collective-permute-start.11) | collective-permute-done | bytes 544 | tf_op jit(solution)/shard_map/ppermute | solution.py:350
  28.7 0.9 %collective-permute-done.10 = f32[1,128]{1,0:T(1,128)S(1)} collective-permute-done((f32[1,128]{1,0:T(1,128)S(1)}, f32[1,128]{1,0:T(1,128)S(1)}, u32[]{:S(2)}, u32[]{:S(2)}) %collective-permute-start.10) | collective-permute-done | bytes 544 | tf_op jit(solution)/shard_map/ppermute | solution.py:350
  29.6 0.5 %add_add_fusion = f32[1,128]{1,0:T(1,128)} fusion(f32[1,128]{1,0:T(1,128)S(1)} %collective-permute-done.12, f32[1,128]{1,0:T(1,128)S(1)} %collective-permute-done.11, f32[1,128]{1,0:T(1,128)S(1)} %score_pair.1, f32[1,128]{1,0:T(1,128)S(1)} %collective-permute-done.10), kind=kLoop, calls=%fused_computation | loop fusion | flops 384 | bytes 2560 | tf_op jit(solution)/shard_map/add | solution.py:447
Async XLA Ops:
  0.0 13.2 %copy-start.2 = (s32[8,4]{0,1:T(4,128)S(1)}, s32[8,4]{0,1:T(4,128)}, u32[]{:S(2)}) copy-start(s32[8,4]{0,1:T(4,128)} %param.15) | copy-start | bytes 388
  0.0 13.2 %copy-start = (f32[3,3,64,128]{3,2,1,0:T(8,128)S(1)}, f32[3,3,64,128]{3,2,1,0:T(8,128)}, u32[]{:S(2)}) copy-start(f32[3,3,64,128]{3,2,1,0:T(8,128)} %param.22) | copy-start | bytes 884740
  0.0 13.2 %copy-start.1 = (f32[3,3,32,64]{3,2,1,0:T(8,128)S(1)}, f32[3,3,32,64]{3,2,1,0:T(8,128)}, u32[]{:S(2)}) copy-start(f32[3,3,32,64]{3,2,1,0:T(8,128)} %param.20) | copy-start | bytes 221188
  0.0 13.2 %copy-start.3 = (f32[3,3,1,32]{3,2,1,0:T(1,128)S(1)}, f32[3,3,1,32]{3,2,1,0:T(1,128)}, u32[]{:S(2)}) copy-start(f32[3,3,1,32]{3,2,1,0:T(1,128)} %param.18) | copy-start | bytes 3460
  0.0 13.2 %copy-start.4 = (s32[32]{0:T(128)S(1)}, s32[32]{0:T(128)}, u32[]{:S(2)}) copy-start(s32[32]{0:T(128)} %clen_ref.1) | copy-start | bytes 388
  0.0 20.4 %copy-start.5 = (f32[32]{0:T(128)S(1)}, f32[32]{0:T(128)}, u32[]{:S(2)}) copy-start(f32[32]{0:T(128)} %param.19) | copy-start | bytes 388
  0.0 20.4 %copy-start.6 = (f32[64]{0:T(128)S(1)}, f32[64]{0:T(128)}, u32[]{:S(2)}) copy-start(f32[64]{0:T(128)} %param.21) | copy-start | bytes 772
  0.0 20.4 %copy-start.7 = (f32[128]{0:T(128)S(1)}, f32[128]{0:T(128)}, u32[]{:S(2)}) copy-start(f32[128]{0:T(128)} %param.23) | copy-start | bytes 1540
  0.0 20.4 %copy-start.8 = (f32[1,1,128,1]{2,3,1,0:T(1,128)S(1)}, f32[1,1,128,1]{2,3,1,0:T(1,128)}, u32[]{:S(2)}) copy-start(f32[1,1,128,1]{2,3,1,0:T(1,128)} %param.24) | copy-start | bytes 1540
  2.1 13.7 %collective-permute-start.8 = (bf16[2,9,16,256]{3,2,1,0:T(8,128)(2,1)S(1)}, bf16[2,9,16,256]{3,2,1,0:T(8,128)(2,1)S(1)}, u32[]{:S(2)}, u32[]{:S(2)}) collective-permute-start(bf16[2,9,16,256]{3,2,1,0:T(8,128)(2,1)S(1)} %get-tuple-element.26), channel_id=1, source_target_pairs={{0,20},{1,25},{2,22},{3,27},{4,16},{5,29},{6,18},{7,31},{8,28},{9,... | collective-permute-start | bytes 442376 | tf_op jit(solution)/shard_map/ppermute | solution.py:372
  7.2 8.8 %collective-permute-start.3 = (bf16[2,9,16,256]{3,2,1,0:T(8,128)(2,1)S(1)}, bf16[2,9,16,256]{3,2,1,0:T(8,128)(2,1)S(1)}, u32[]{:S(2)}, u32[]{:S(2)}) collective-permute-start(bf16[2,9,16,256]{3,2,1,0:T(8,128)(2,1)S(1)} %get-tuple-element.22), channel_id=1, source_target_pairs={{0,12},{1,9},{2,14},{3,11},{4,8},{5,13},{6,10},{7,15},{8,4},{9,1},... | collective-permute-start | bytes 442376 | tf_op jit(solution)/shard_map/ppermute | solution.py:372
  8.7 9.8 %collective-permute-start.4 = (bf16[2,9,16,256]{3,2,1,0:T(8,128)(2,1)S(1)}, bf16[2,9,16,256]{3,2,1,0:T(8,128)(2,1)S(1)}, u32[]{:S(2)}, u32[]{:S(2)}) collective-permute-start(bf16[2,9,16,256]{3,2,1,0:T(8,128)(2,1)S(1)} %get-tuple-element.23), channel_id=1, source_target_pairs={{0,28},{1,17},{2,30},{3,19},{4,24},{5,21},{6,26},{7,23},{8,20},{9,... | collective-permute-start | bytes 442376 | tf_op jit(solution)/shard_map/ppermute | solution.py:372
  9.9 8.7 %collective-permute-start = (bf16[9,32,256]{2,1,0:T(8,128)(2,1)S(1)}, bf16[9,32,256]{2,1,0:T(8,128)(2,1)S(1)}, u32[]{:S(2)}, u32[]{:S(2)}) collective-permute-start(bf16[9,32,256]{2,1,0:T(8,128)(2,1)S(1)} %get-tuple-element.21.rest_0_), channel_id=1, source_target_pairs={{0,2},{1,3},{2,0},{3,1},{4,6},{5,7},{6,4},{7,5},{8,10},{9,11},{10,... | collective-permute-start | bytes 442376 | tf_op jit(solution)/shard_map/ppermute | solution.py:350
  11.4 7.7 %collective-permute-start.7 = (bf16[9,16,256]{2,1,0:T(8,128)(2,1)S(1)}, bf16[9,16,256]{2,1,0:T(8,128)(2,1)S(1)}, u32[]{:S(2)}, u32[]{:S(2)}) collective-permute-start(bf16[9,16,256]{2,1,0:T(8,128)(2,1)S(1)} %get-tuple-element.24), channel_id=1, source_target_pairs={{0,4},{4,0},{8,12},{12,8},{16,20},{20,16},{24,28},{28,24},{1,5},{5... | collective-permute-start | bytes 221192 | tf_op jit(solution)/shard_map/ppermute | solution.py:388
  15.9 3.2 %collective-permute-start.1 = (bf16[9,32,256]{2,1,0:T(8,128)(2,1)S(1)}, bf16[9,32,256]{2,1,0:T(8,128)(2,1)S(1)}, u32[]{:S(2)}, u32[]{:S(2)}) collective-permute-start(bf16[9,32,256]{2,1,0:T(8,128)(2,1)S(1)} %get-tuple-element.21.rest_0_), channel_id=1, source_target_pairs={{0,1},{1,0},{2,3},{3,2},{4,5},{5,4},{6,7},{7,6},{8,9},{9,8},{10,11... | collective-permute-start | bytes 442376 | tf_op jit(solution)/shard_map/ppermute | solution.py:350
  16.0 3.1 %collective-permute-start.5 = (bf16[2,9,16,256]{3,2,1,0:T(8,128)(2,1)S(1)}, bf16[2,9,16,256]{3,2,1,0:T(8,128)(2,1)S(1)}, u32[]{:S(2)}, u32[]{:S(2)}) collective-permute-start(bf16[2,9,16,256]{3,2,1,0:T(8,128)(2,1)S(1)} %collective-permute-done.3.rest_4_), channel_id=1, source_target_pairs={{0,1},{1,0},{2,3},{3,2},{4,5},{5,4},{6,7},{7,6},{8,9},{9,8},{10,11... | collective-permute-start | bytes 442376 | tf_op jit(solution)/shard_map/ppermute | solution.py:350
  18.5 1.4 %collective-permute-start.6 = (bf16[2,9,16,256]{3,2,1,0:T(8,128)(2,1)S(1)}, bf16[2,9,16,256]{3,2,1,0:T(8,128)(2,1)S(1)}, u32[]{:S(2)}, u32[]{:S(2)}) collective-permute-start(bf16[2,9,16,256]{3,2,1,0:T(8,128)(2,1)S(1)} %collective-permute-done.4.rest_5_), channel_id=1, source_target_pairs={{0,1},{1,0},{2,3},{3,2},{4,5},{5,4},{6,7},{7,6},{8,9},{9,8},{10,11... | collective-permute-start | bytes 442376 | tf_op jit(solution)/shard_map/ppermute | solution.py:350
  18.6 1.5 %collective-permute-start.2 = (bf16[9,32,256]{2,1,0:T(8,128)(2,1)S(1)}, bf16[9,32,256]{2,1,0:T(8,128)(2,1)S(1)}, u32[]{:S(2)}, u32[]{:S(2)}) collective-permute-start(bf16[9,32,256]{2,1,0:T(8,128)(2,1)S(1)} %collective-permute-done.rest_1_), channel_id=1, source_target_pairs={{0,1},{1,0},{2,3},{3,2},{4,5},{5,4},{6,7},{7,6},{8,9},{9,8},{10,11... | collective-permute-start | bytes 442376 | tf_op jit(solution)/shard_map/ppermute | solution.py:350
  19.0 1.4 %collective-permute-start.9 = (bf16[2,9,16,256]{3,2,1,0:T(8,128)(2,1)S(1)}, bf16[2,9,16,256]{3,2,1,0:T(8,128)(2,1)S(1)}, u32[]{:S(2)}, u32[]{:S(2)}) collective-permute-start(bf16[2,9,16,256]{3,2,1,0:T(8,128)(2,1)S(1)} %collective-permute-done.8.rest_18_), channel_id=1, source_target_pairs={{0,1},{1,0},{2,3},{3,2},{4,5},{5,4},{6,7},{7,6},{8,9},{9,8},{10,11... | collective-permute-start | bytes 442376 | tf_op jit(solution)/shard_map/ppermute | solution.py:350
  24.9 1.9 %collective-permute-start.12 = (f32[1,128]{1,0:T(1,128)S(1)}, f32[1,128]{1,0:T(1,128)S(1)}, u32[]{:S(2)}, u32[]{:S(2)}) collective-permute-start(f32[1,128]{1,0:T(1,128)S(1)} %score_pair.1), channel_id=1, source_target_pairs={{0,1},{1,0},{2,3},{3,2},{4,5},{5,4},{6,7},{7,6},{8,9},{9,8},{10,11... | collective-permute-start | bytes 1544 | tf_op jit(solution)/shard_map/ppermute | solution.py:350
  25.2 3.5 %collective-permute-start.11 = (f32[1,128]{1,0:T(1,128)S(1)}, f32[1,128]{1,0:T(1,128)S(1)}, u32[]{:S(2)}, u32[]{:S(2)}) collective-permute-start(f32[1,128]{1,0:T(1,128)S(1)} %score_pair.1), channel_id=1, source_target_pairs={{0,2},{1,3},{2,0},{3,1},{4,6},{5,7},{6,4},{7,5},{8,10},{9,11},{10,... | collective-permute-start | bytes 1544 | tf_op jit(solution)/shard_map/ppermute | solution.py:350
  26.7 3.0 %collective-permute-start.10 = (f32[1,128]{1,0:T(1,128)S(1)}, f32[1,128]{1,0:T(1,128)S(1)}, u32[]{:S(2)}, u32[]{:S(2)}) collective-permute-start(f32[1,128]{1,0:T(1,128)S(1)} %score_pair.1), channel_id=1, source_target_pairs={{0,3},{1,2},{2,1},{3,0},{4,7},{5,6},{6,5},{7,4},{8,11},{9,10},{10,... | collective-permute-start | bytes 1544 | tf_op jit(solution)/shard_map/ppermute | solution.py:350
